TPU v7x, 128 devices: a whole 4x4x4 slice. The times are simulated.
128 devices in a mesh: row: 8 (over x, y_hi), col: 16 (over z, y_lo, core).
Axes of the slice: x: 4, y: 4 (y_hi: 2, y_lo: 2; y = y_hi * 2 + y_lo), z: 4, core: 2. Of those that a mesh axis runs over, the one named last changes fastest.
Arguments:
- vectors: bfloat16 [131072, 128], P(('row', 'col')), may hold values from -6 to 6
- tiles: bfloat16 [20480, 256, 256], P(('row', 'col')), may hold values from -0.03125 to 0.03125
- tile_rows: int32 [20480], P(('row', 'col')), may hold values from 0 to 63
- tile_cols: int32 [20480], P(('row', 'col')), may hold values from 0 to 31
- tile_count: int32 [128], P(('row', 'col')), may hold values from 40 to 160, as said below
Outputs:
- filtered: float32 [131072, 128], P(('row', 'col'))
Inputs may be any that keep to these rules, and one draw needn't show every extreme that they name: `tile_count`: slots of a device at and beyond its count are empty: their tiles and indices carry no meaning; exactly one device has 160 live slots.
All inputs are finite; a program needn't handle non-finite values.
Results may differ from a plain program's by a relative error of at most 0.015.
Values may be sent and summed in bfloat16 or wider, within the bound.
No kernel may reach another device: no remote copies, remote signals or barrier semaphores. Data moves between devices by JAX's collectives and lax.ppermute only.
A program may use at most 192 MiB of HBM per device.

v0:
```python
import jax
import jax.numpy as jnp
from jax import lax
from jax.sharding import PartitionSpec as P

center_value = 0.5
radius_value = 1.5


def row_gather(field_in):
    return lax.all_gather(field_in, "col", axis=0, tiled=True)


def col_gather(field_in):
    return lax.all_gather(field_in, "row", axis=0, tiled=True)


def direct_reduce(partial_sums):
    return lax.psum_scatter(
        partial_sums.astype(jnp.bfloat16), "col", scatter_dimension=0, tiled=True
    ).astype(jnp.float32)


def mirror_reduce(partial_sums):
    return lax.psum_scatter(
        partial_sums.astype(jnp.bfloat16), "row", scatter_dimension=0, tiled=True
    ).astype(jnp.float32)


def block_sums(onehot, products):
    flat = products.reshape(products.shape[0], -1)
    upper = flat.astype(jnp.bfloat16)
    lower = (flat - upper.astype(jnp.float32)).astype(jnp.bfloat16)
    total = jnp.dot(onehot, upper, preferred_element_type=jnp.float32)
    return total + jnp.dot(onehot, lower, preferred_element_type=jnp.float32)


def slot_products(tiles, row_flat, col_flat, tile_rows, tile_cols, row_onehot, col_onehot):
    block_width = tiles.shape[1]
    vector_count = row_flat.shape[1]
    row_blocks = row_flat.reshape(-1, block_width, vector_count)
    col_blocks = col_flat.reshape(-1, block_width, vector_count)
    picked_cols = jnp.take(col_blocks, tile_cols, axis=0)
    direct = jnp.einsum("tab,tbk->tak", tiles, picked_cols, preferred_element_type=jnp.float32)
    direct_part = block_sums(row_onehot, direct)
    picked_rows = jnp.take(row_blocks, tile_rows, axis=0)
    mirror = jnp.einsum("tba,tbk->tak", tiles, picked_rows, preferred_element_type=jnp.float32)
    mirror_part = block_sums(col_onehot, mirror)
    return (direct_part.reshape(-1, vector_count), mirror_part.reshape(-1, vector_count))


def local(vectors, tiles, tile_rows, tile_cols, tile_count):
    row_devices = lax.axis_size("row")
    col_devices = lax.axis_size("col")
    slot_count = tiles.shape[0]
    block_width = tiles.shape[1]
    owned_blocks = vectors.shape[0] // block_width
    live_slots = jnp.arange(slot_count) < tile_count[0]
    row_onehot = (
        tile_rows[None, :] == jnp.arange(col_devices * owned_blocks)[:, None]
    ) & live_slots[None, :]
    row_onehot = row_onehot.astype(jnp.bfloat16)
    col_onehot = (
        tile_cols[None, :] == jnp.arange(row_devices * owned_blocks)[:, None]
    ) & live_slots[None, :]
    col_onehot = col_onehot.astype(jnp.bfloat16)
    x_float = vectors.astype(jnp.float32)
    row_flat = row_gather(vectors)
    col_flat = col_gather(vectors)
    direct_part, mirror_part = slot_products(
        tiles, row_flat, col_flat, tile_rows, tile_cols, row_onehot, col_onehot
    )
    applied = direct_reduce(direct_part) + mirror_reduce(mirror_part)
    first_term = ((applied - center_value * x_float) / radius_value).astype(jnp.bfloat16)
    first_rows = row_gather(first_term)
    first_cols = col_gather(first_term)
    direct_next, mirror_next = slot_products(
        tiles, first_rows, first_cols, tile_rows, tile_cols, row_onehot, col_onehot
    )
    second = direct_reduce(direct_next) + mirror_reduce(mirror_next)
    return 2.0 * (second - center_value * first_term.astype(jnp.float32)) / radius_value - x_float


def solution(mesh):
    return jax.shard_map(
        local,
        mesh=mesh,
        in_specs=(
            P(("row", "col"), None),
            P(("row", "col"), None, None),
            P(("row", "col")),
            P(("row", "col")),
            P(("row", "col")),
        ),
        out_specs=P(("row", "col"), None),
        check_vma=False,
    )
```

profile of v0, /device:TPU:14, one launch (start us, length us, event | category | flops | bytes accessed | tf_op | source)
XLA Modules:
  0.0 678.8 jit_solution(17597338681864549095)
XLA Ops:
  6.5 0.7 all-gather.5.cloned.1.call-update
  7.3 0.7 all-gather.7.cloned.1.call-update
  10.1 55.6 %all-gather.5.cloned.1.call-done = bf16[8192,128]{1,0:T(8,128)(2,1)} async-done(((bf16[1024,128]{1,0:T(8,128)(2,1)}), bf16[8192,128]{1,0:T(8,128)(2,1)}) %all-gather.5.cloned.1.call-update) | async-done | bytes 2097168 | tf_op jit(solution)/shard_map/all_gather | solution.py:15
  65.7 9.2 %gather_fusion = bf16[160,256,128]{2,1,0:T(8,128)(2,1)} fusion(bf16[32,256,128]{2,1,0:T(8,128)(2,1)} %bitcast.66, s32[1024]{0:T(1024)S(1)} %pad_clamp_fusion.1), kind=kCustom, calls=%fused_computation.clone | custom fusion | bytes 20972160 | tf_op jit(solution)/shard_map/jit(_take)/gather | solution.py:43
  74.9 24.1 %fusion.28 = f32[160,256,128]{1,2,0:T(8,128)} fusion(bf16[160,256,256]{2,1,0:T(8,128)(2,1)} %param.10, bf16[160,256,128]{2,1,0:T(8,128)(2,1)} %gather_fusion, pred[160]{0:T(512)(128)(4,1)S(1)} %compare_and_fusion), kind=kOutput, calls=%fused_computation.40 | convolution fusion | flops 2689597440 | bytes 52428960 | tf_op jit(solution)/shard_map/tab,tbk->tak/dot_general | solution.py:44
  99.0 21.4 %copy.7 = f32[160,256,128]{2,1,0:T(8,128)} copy(f32[160,256,128]{1,2,0:T(8,128)} %fusion.28) | data formatting | bytes 41943040 | tf_op jit(solution)/shard_map/tab,tbk->tak/dot_general | solution.py:44
  120.4 22.3 %fusion.8 = f32[64,32768]{1,0:T(8,128)} fusion(f32[20,8,256,128]{3,2,1,0:T(8,128)} %bitcast.62, s32[160]{0:T(256)S(1)} %copy-done.2, pred[160]{0:T(512)(128)(4,1)S(1)} %iota_compare_fusion.2), kind=kOutput, calls=%fused_computation.24 | convolution fusion | flops 671109120 | bytes 29360928 | tf_op jit(solution)/shard_map/dot_general | solution.py:34
  142.6 24.1 %fusion = bf16[64,32768]{1,0:T(8,128)(2,1)} fusion(f32[64,32768]{1,0:T(8,128)} %fusion.8, f32[20,8,256,128]{3,2,1,0:T(8,128)} %bitcast.63, s32[160]{0:T(256)S(1)} %copy-done.2, pred[160]{0:T(512)(128)(4,1)S(1)} %iota_compare_fusion.2), kind=kOutput, calls=%fused_computation.6 | convolution fusion | flops 696274944 | bytes 33555232 | tf_op jit(solution)/shard_map/dot_general | solution.py:35
  166.9 7.4 %convert_element_type.87 = bf16[16384,128]{1,0:T(8,128)(2,1)} reshape(bf16[64,32768]{1,0:T(8,128)(2,1)} %fusion) | data formatting | bytes 8388608 | tf_op jit(solution)/shard_map/convert_element_type | solution.py:20
  174.4 9.8 %gather_fusion.1 = bf16[160,256,128]{2,1,0:T(8,128)(2,1)} fusion(bf16[64,256,128]{2,1,0:T(8,128)(2,1)} %bitcast.68, s32[1024]{0:T(1024)S(1)} %pad_clamp_fusion), kind=kCustom, calls=%fused_computation.1.clone | custom fusion | bytes 20972160 | tf_op jit(solution)/shard_map/jit(_take)/gather | solution.py:46
  184.2 19.9 %fusion.31 = f32[160,256,128]{1,2,0:T(8,128)} fusion(bf16[160,256,256]{2,1,0:T(8,128)(2,1)} %param.10, bf16[160,256,128]{2,1,0:T(8,128)(2,1)} %gather_fusion.1, pred[160]{0:T(512)(128)(4,1)S(1)} %compare_and_fusion.1), kind=kOutput, calls=%fused_computation.41 | convolution fusion | flops 2689597440 | bytes 52428960 | tf_op jit(solution)/shard_map/tba,tbk->tak/dot_general | solution.py:47
  204.1 21.3 %copy.9 = f32[160,256,128]{2,1,0:T(8,128)} copy(f32[160,256,128]{1,2,0:T(8,128)} %fusion.31) | data formatting | bytes 41943040 | tf_op jit(solution)/shard_map/tba,tbk->tak/dot_general | solution.py:47
  225.4 18.6 %fusion.9 = f32[32,32768]{1,0:T(8,128)S(1)} fusion(f32[20,8,256,128]{3,2,1,0:T(8,128)} %bitcast.60, s32[160]{0:T(256)S(1)} %copy-done.3, pred[160]{0:T(512)(128)(4,1)S(1)} %iota_compare_fusion.2), kind=kOutput, calls=%fused_computation.25 | convolution fusion | flops 335554560 | bytes 25166624 | tf_op jit(solution)/shard_map/dot_general | solution.py:34
  244.1 19.0 %fusion.2 = bf16[32,32768]{1,0:T(8,128)(2,1)S(1)} fusion(f32[32,32768]{1,0:T(8,128)S(1)} %fusion.9, f32[20,8,256,128]{3,2,1,0:T(8,128)} %bitcast.61, s32[160]{0:T(256)S(1)} %copy-done.3, pred[160]{0:T(512)(128)(4,1)S(1)} %iota_compare_fusion.2), kind=kOutput, calls=%fused_computation.10 | convolution fusion | flops 358623232 | bytes 27263776 | tf_op jit(solution)/shard_map/dot_general | solution.py:35
  263.1 2.4 convert_element_type.93
  265.6 74.2 %reduce-scatter.7.cloned.1.call-done = bf16[1024,128]{1,0:T(8,128)(2,1)} async-done(((bf16[8192,128]{1,0:T(8,128)(2,1)}), bf16[1024,128]{1,0:T(8,128)(2,1)}) %reduce-scatter.7.cloned.1.call-update) | async-done | bytes 262160 | tf_op jit(solution)/shard_map/reduce_scatter | solution.py:25
  339.8 1.9 fusion.46
  342.3 53.7 %all-gather.9.cloned.1.call-done = bf16[8192,128]{1,0:T(8,128)(2,1)} async-done(((bf16[1024,128]{1,0:T(8,128)(2,1)}), bf16[8192,128]{1,0:T(8,128)(2,1)}) %all-gather.9.cloned.1.call-update) | async-done | bytes 2097168 | tf_op jit(solution)/shard_map/all_gather | solution.py:15
  396.0 9.2 %gather_fusion.2 = bf16[160,256,128]{2,1,0:T(8,128)(2,1)} fusion(bf16[32,256,128]{2,1,0:T(8,128)(2,1)} %bitcast.67, s32[1024]{0:T(1024)S(1)} %pad_clamp_fusion.1), kind=kCustom, calls=%fused_computation.2.clone | custom fusion | bytes 20972160 | tf_op jit(solution)/shard_map/jit(_take)/gather | solution.py:43
  405.2 24.2 %fusion.34 = f32[160,256,128]{1,2,0:T(8,128)} fusion(bf16[160,256,256]{2,1,0:T(8,128)(2,1)} %param.10, bf16[160,256,128]{2,1,0:T(8,128)(2,1)} %gather_fusion.2, pred[160]{0:T(512)(128)(4,1)S(1)} %compare_and_fusion), kind=kOutput, calls=%fused_computation.42 | convolution fusion | flops 2689597440 | bytes 52428960 | tf_op jit(solution)/shard_map/tab,tbk->tak/dot_general | solution.py:44
  429.3 21.3 %copy.11 = f32[160,256,128]{2,1,0:T(8,128)} copy(f32[160,256,128]{1,2,0:T(8,128)} %fusion.34) | data formatting | bytes 41943040 | tf_op jit(solution)/shard_map/tab,tbk->tak/dot_general | solution.py:44
  450.7 22.3 %fusion.10 = f32[64,32768]{1,0:T(8,128)} fusion(f32[20,8,256,128]{3,2,1,0:T(8,128)} %bitcast.64, s32[160]{0:T(256)S(1)} %copy-done.2, pred[160]{0:T(512)(128)(4,1)S(1)} %iota_compare_fusion.2), kind=kOutput, calls=%fused_computation.26 | convolution fusion | flops 671109120 | bytes 29360928 | tf_op jit(solution)/shard_map/dot_general | solution.py:34
  472.9 24.1 %fusion.1 = bf16[64,32768]{1,0:T(8,128)(2,1)} fusion(f32[64,32768]{1,0:T(8,128)} %fusion.10, f32[20,8,256,128]{3,2,1,0:T(8,128)} %bitcast.65, s32[160]{0:T(256)S(1)} %copy-done.2, pred[160]{0:T(512)(128)(4,1)S(1)} %iota_compare_fusion.2), kind=kOutput, calls=%fused_computation.7 | convolution fusion | flops 696274944 | bytes 33555232 | tf_op jit(solution)/shard_map/dot_general | solution.py:35
  497.0 7.5 %convert_element_type.101 = bf16[16384,128]{1,0:T(8,128)(2,1)} reshape(bf16[64,32768]{1,0:T(8,128)(2,1)} %fusion.1) | data formatting | bytes 8388608 | tf_op jit(solution)/shard_map/convert_element_type | solution.py:20
  504.6 9.8 %gather_fusion.3 = bf16[160,256,128]{2,1,0:T(8,128)(2,1)} fusion(bf16[64,256,128]{2,1,0:T(8,128)(2,1)} %bitcast.69, s32[1024]{0:T(1024)S(1)} %pad_clamp_fusion), kind=kCustom, calls=%fused_computation.3.clone | custom fusion | bytes 20972160 | tf_op jit(solution)/shard_map/jit(_take)/gather | solution.py:46
  514.5 19.9 %fusion.37 = f32[160,256,128]{1,2,0:T(8,128)} fusion(bf16[160,256,256]{2,1,0:T(8,128)(2,1)} %param.10, bf16[160,256,128]{2,1,0:T(8,128)(2,1)} %gather_fusion.3, pred[160]{0:T(512)(128)(4,1)S(1)} %compare_and_fusion.1), kind=kOutput, calls=%fused_computation.43 | convolution fusion | flops 2689597440 | bytes 52428960 | tf_op jit(solution)/shard_map/tba,tbk->tak/dot_general | solution.py:47
  534.4 21.3 %copy.13 = f32[160,256,128]{2,1,0:T(8,128)} copy(f32[160,256,128]{1,2,0:T(8,128)} %fusion.37) | data formatting | bytes 41943040 | tf_op jit(solution)/shard_map/tba,tbk->tak/dot_general | solution.py:47
  555.6 18.6 %fusion.11 = f32[32,32768]{1,0:T(8,128)S(1)} fusion(f32[20,8,256,128]{3,2,1,0:T(8,128)} %bitcast.58, s32[160]{0:T(256)S(1)} %copy-done.3, pred[160]{0:T(512)(128)(4,1)S(1)} %iota_compare_fusion.2), kind=kOutput, calls=%fused_computation.27 | convolution fusion | flops 335554560 | bytes 25166624 | tf_op jit(solution)/shard_map/dot_general | solution.py:34
  574.3 18.8 %fusion.3 = bf16[32,32768]{1,0:T(8,128)(2,1)S(1)} fusion(f32[32,32768]{1,0:T(8,128)S(1)} %fusion.11, f32[20,8,256,128]{3,2,1,0:T(8,128)} %bitcast.59, s32[160]{0:T(256)S(1)} %copy-done.3, pred[160]{0:T(512)(128)(4,1)S(1)} %iota_compare_fusion.2), kind=kOutput, calls=%fused_computation.11 | convolution fusion | flops 358623232 | bytes 27263776 | tf_op jit(solution)/shard_map/dot_general | solution.py:35
  593.1 2.4 convert_element_type.107
  595.6 74.2 %reduce-scatter.11.cloned.1.call-done = bf16[1024,128]{1,0:T(8,128)(2,1)} async-done(((bf16[8192,128]{1,0:T(8,128)(2,1)}), bf16[1024,128]{1,0:T(8,128)(2,1)}) %reduce-scatter.11.cloned.1.call-update) | async-done | bytes 262160 | tf_op jit(solution)/shard_map/reduce_scatter | solution.py:25
  669.8 2.0 convert_subtract_fusion
  (33 shorter events, 2.4 us)
Async XLA Ops:
  6.5 59.2 %all-gather.5.cloned.1.call-start = ((), (), s32[]{:S(2)}) async-start(), calls=%async_computation.4 | async-start | bytes 2359296 | tf_op jit(solution)/shard_map/all_gather | solution.py:15
  7.3 167.1 %all-gather.7.cloned.1.call-start = ((), (), s32[]{:S(2)}) async-start(), calls=%async_computation.6 | async-start | bytes 4456448 | tf_op jit(solution)/shard_map/all_gather | solution.py:11
  8.0 257.6 %reduce-scatter.5.cloned.1.call-start = ((), (), s32[]{:S(2)}) async-start(), calls=%async_computation.5 | async-start | bytes 4456448 | tf_op jit(solution)/shard_map/reduce_scatter | solution.py:19
  99.0 21.4 %copy-start.2 = (s32[160]{0:T(256)S(1)}, s32[160]{0:T(256)}, u32[]{:S(2)}) copy-start(s32[160]{0:T(256)} %param.11) | copy-start | bytes 1924
  174.3 165.5 %reduce-scatter.7.cloned.1.call-start = ((), (), s32[]{:S(2)}) async-start(), calls=%async_computation.7 | async-start | bytes 2359296 | tf_op jit(solution)/shard_map/reduce_scatter | solution.py:25
  204.1 21.3 %copy-start.3 = (s32[160]{0:T(256)S(1)}, s32[160]{0:T(256)}, u32[]{:S(2)}) copy-start(s32[160]{0:T(256)} %param.12) | copy-start | bytes 1924
  244.1 95.7 %copy-start = (bf16[1024,128]{1,0:T(8,128)(2,1)S(1)}, bf16[1024,128]{1,0:T(8,128)(2,1)}, u32[]{:S(2)}) copy-start(bf16[1024,128]{1,0:T(8,128)(2,1)} %param.9) | copy-start | bytes 786436
  265.5 130.5 %all-gather.9.cloned.1.call-start = ((), (), s32[]{:S(2)}) async-start(), calls=%async_computation.8 | async-start | bytes 2359296 | tf_op jit(solution)/shard_map/all_gather | solution.py:15
  341.7 163.0 %all-gather.11.cloned.1.call-start = ((), (), s32[]{:S(2)}) async-start(), calls=%async_computation.10 | async-start | bytes 4456448 | tf_op jit(solution)/shard_map/all_gather | solution.py:11
  342.2 253.3 %reduce-scatter.9.cloned.1.call-start = ((), (), s32[]{:S(2)}) async-start(), calls=%async_computation.9 | async-start | bytes 4456448 | tf_op jit(solution)/shard_map/reduce_scatter | solution.py:19
  504.6 165.2 %reduce-scatter.11.cloned.1.call-start = ((), (), s32[]{:S(2)}) async-start(), calls=%async_computation.11 | async-start | bytes 2359296 | tf_op jit(solution)/shard_map/reduce_scatter | solution.py:25
  574.3 95.5 %copy-start.1 = (bf16[1024,128]{1,0:T(8,128)(2,1)S(1)}, bf16[1024,128]{1,0:T(8,128)(2,1)}, u32[]{:S(2)}) copy-start(bf16[1024,128]{1,0:T(8,128)(2,1)} %fusion.46) | copy-start | bytes 786436
Sparse Core Ops, SparseCore 0:
  9.7 55.9 all-gather.4
  67.4 37.3 all-gather.6
  174.4 65.8 reduce-scatter.4
  265.6 74.0 reduce-scatter.6
  342.2 53.7 all-gather.8
  397.7 37.4 all-gather.10
  504.7 66.0 reduce-scatter.8
  595.7 74.0 reduce-scatter.10
where the time goes:
time: 687 us; the launch traced here: 679 us
  waiting for transfers between devices  260 us (38%)
  matrix products  256 us (37%)
  local copies, waits for them, and re-layouts  143 us (21%)
  between operations  14.7 us (2%)
    reduce_scatter x2, waiting for transfers between devices, mirror_reduce(): lax.psum_scatter(partial_sums.astype(jnp.bfloat16), 'row', scatter_dimens...  148 us
    all_gather x2, waiting for transfers between devices, col_gather(): return lax.all_gather(field_in, 'row', axis=0, tiled=True)  109 us
    dot_general x4, matrix products, block_sums(): return total + jnp.dot(onehot, lower, preferred_element_type=jnp.float32)  86 us
    dot_general x4, matrix products, block_sums(): total = jnp.dot(onehot, upper, preferred_element_type=jnp.float32)  81.8 us
    dot_general x2, matrix products, slot_products(): jnp.einsum('tab,tbk->tak', tiles, picked_cols, preferred_element_type=jnp...  48.3 us
    dot_general x2, local copies, waits for them, and re-layouts, slot_products(): jnp.einsum('tab,tbk->tak', tiles, picked_cols, preferred_element_type=jnp...  42.7 us
    dot_general x2, local copies, waits for them, and re-layouts, slot_products(): jnp.einsum('tba,tbk->tak', tiles, picked_rows, preferred_element_type=jnp...  42.5 us
    dot_general x2, matrix products, slot_products(): jnp.einsum('tba,tbk->tak', tiles, picked_rows, preferred_element_type=jnp...  39.8 us
  transfers between devices with their start and end apart: 8, of which 4 were waited for; matrix products, arithmetic and copies ran while one was open for 59% of the time, Pallas kernels for 0%

commit v1 on v0

v1 whole, which is shorter than its diff:
```python
import functools

import jax
import jax.numpy as jnp
from jax import lax
from jax.experimental import pallas as pl
from jax.experimental.pallas import tpu as pltpu
from jax.sharding import PartitionSpec as P

center_value = 0.5
radius_value = 1.5

BS = 256
NV = 128
OWN = 4
CHUNK = 16

ROW_STEPS = [(dx, dy) for dx in range(4) for dy in range(2)]
COL_STEPS = [(dz, dy) for dz in range(4) for dy in range(2)]


def send_row(value, step):
    dx, dy = step
    pairs = [(x * 2 + y, (x + dx) % 4 * 2 + (y ^ dy)) for x in range(4) for y in range(2)]
    return lax.ppermute(value, "row", pairs)


def send_col(value, step, dk=0):
    dz, dy = step
    pairs = [
        (z * 4 + y * 2 + k, (z + dz) % 4 * 4 + (y ^ dy) * 2 + (k ^ dk))
        for z in range(4)
        for y in range(2)
        for k in range(2)
    ]
    return lax.ppermute(value, "col", pairs)


def spmv_kernel(mirror, n_in, n_out, out_slot, in_slot, count, tiles, *rest):
    v_in = rest[:n_in]
    outs = rest[n_in : n_in + n_out]
    acc, held, sems = rest[n_in + n_out :]
    step = pl.program_id(0)

    @pl.when(step == 0)
    def _():
        part = held.shape[0] // n_in
        copies = [
            pltpu.make_async_copy(v_in[j], held.at[pl.ds(j * part, part)], sems.at[j])
            for j in range(n_in)
        ]
        for copy in copies:
            copy.start()
        acc[...] = jnp.zeros_like(acc)
        for copy in copies:
            copy.wait()

    @pl.when(step * CHUNK < count[0])
    def _():
        for j in range(CHUNK):
            slot = step * CHUNK + j
            base = pl.multiple_of(in_slot[slot] * BS, BS)
            vec = held[pl.ds(base, BS), :]
            dims = (((0,), (0,)), ((), ())) if mirror else (((1,), (0,)), ((), ()))
            acc[out_slot[slot]] += lax.dot_general(
                tiles[j], vec, dims, preferred_element_type=jnp.float32
            )

    @pl.when(step == pl.num_programs(0) - 1)
    def _():
        at = 0
        for out in outs:
            blocks = out.shape[0] // BS

            @pl.loop(0, blocks)
            def _(b):
                out[pl.ds(pl.multiple_of(b * BS, BS), BS), :] = acc[at + b].astype(out.dtype)

            at += blocks


def spmv(mirror, tiles, out_slot, in_slot, count, v_in, out_rows):
    slots = tiles.shape[0]
    n_in, n_out = len(v_in), len(out_rows)
    blocks_out = sum(out_rows) // BS

    def tile_index(i, out_slot, in_slot, count):
        last = jnp.maximum((count[0] + CHUNK - 1) // CHUNK - 1, 0)
        return jnp.minimum(i, last), 0, 0

    return pl.pallas_call(
        functools.partial(spmv_kernel, mirror, n_in, n_out),
        grid_spec=pltpu.PrefetchScalarGridSpec(
            num_scalar_prefetch=3,
            grid=(slots // CHUNK,),
            in_specs=[pl.BlockSpec((CHUNK, BS, BS), tile_index)]
            + [pl.BlockSpec(memory_space=pl.ANY)] * n_in,
            out_specs=[pl.BlockSpec((n, NV), lambda i, *_: (0, 0)) for n in out_rows],
            scratch_shapes=[
                pltpu.VMEM((blocks_out + 1, BS, NV), jnp.float32),
                pltpu.VMEM((sum(v.shape[0] for v in v_in), NV), jnp.bfloat16),
                pltpu.SemaphoreType.DMA((n_in,)),
            ],
        ),
        out_shape=[jax.ShapeDtypeStruct((n, NV), jnp.bfloat16) for n in out_rows],
        compiler_params=pltpu.CompilerParams(vmem_limit_bytes=56 * 2**20),
        cost_estimate=pl.CostEstimate(
            flops=2 * slots * BS * BS * NV, bytes_accessed=slots * BS * BS * 2, transcendentals=0
        ),
        name="mirror_sums" if mirror else "direct_sums",
    )(out_slot, in_slot, count, tiles, *v_in)


def gather_row(field):
    parts = {(0, 0): field, (0, 1): send_row(field, (0, 1))}
    for dx in (2, 1, 3):
        parts[dx, 0] = send_row(field, (dx, 0))
    for dx in (2, 1, 3):
        parts[dx, 1] = send_row(parts[0, 1], (dx, 0))
    return [parts[step] for step in ROW_STEPS]


def gather_col(field):
    return [lax.all_gather(field, "col", axis=0, tiled=True)]


def scatter_col(chunks):
    groups = [[at * 2 + k for at in range(8)] for k in range(2)]
    return lax.all_to_all(chunks, "col", 0, 0, axis_index_groups=groups, tiled=True)


def apply(field, tiles, slots, count):
    direct_out, direct_in, mirror_out, mirror_in = slots
    rows = OWN * BS
    row_parts = gather_row(field)
    col_parts = gather_col(field)
    mine, other = spmv(False, tiles, direct_out, direct_in, count, row_parts, [8 * rows, 8 * rows])
    theirs = send_col(other, (0, 0), 1)
    mirrored = spmv(True, tiles, mirror_out, mirror_in, count, col_parts, [rows] * 8)
    chunks = (mine.astype(jnp.float32) + theirs.astype(jnp.float32)).astype(jnp.bfloat16)
    parts = list(scatter_col(chunks).reshape(8, rows, NV))
    parts += [c if step == (0, 0) else send_row(c, step) for step, c in zip(ROW_STEPS, mirrored)]
    return sum(part.astype(jnp.float32) for part in parts)


def local(vectors, tiles, tile_rows, tile_cols, tile_count):
    row_at = lax.axis_index("row")
    col_at = lax.axis_index("col")
    x, yh = row_at // 2, row_at % 2
    k = col_at % 2
    live = jnp.arange(tiles.shape[0], dtype=jnp.int32) < tile_count[0]
    own_r = tile_rows // OWN
    oz, oy, ok = own_r // 4, own_r // 2 % 2, own_r % 2
    to_col = (oz * 2 + oy + (ok ^ k) * 8) * OWN + tile_rows % OWN
    from_col = tile_rows
    own_c = tile_cols // OWN
    ox, oh = own_c // 2, own_c % 2
    to_row = ((ox - x) % 4 * 2 + (oh ^ yh)) * OWN + tile_cols % OWN
    from_row = ((x - ox) % 4 * 2 + (oh ^ yh)) * OWN + tile_cols % OWN
    slots = (
        jnp.where(live, to_col, 16 * OWN),
        jnp.where(live, from_row, 0),
        jnp.where(live, to_row, 8 * OWN),
        jnp.where(live, from_col, 0),
    )
    x_float = vectors.astype(jnp.float32)
    applied = apply(vectors, tiles, slots, tile_count)
    first_term = ((applied - center_value * x_float) / radius_value).astype(jnp.bfloat16)
    second = apply(first_term, tiles, slots, tile_count)
    return 2.0 * (second - center_value * first_term.astype(jnp.float32)) / radius_value - x_float


def solution(mesh):
    return jax.shard_map(
        local,
        mesh=mesh,
        in_specs=(
            P(("row", "col"), None),
            P(("row", "col"), None, None),
            P(("row", "col")),
            P(("row", "col")),
            P(("row", "col")),
        ),
        out_specs=P(("row", "col"), None),
        check_vma=False,
    )
```

time: 687 us -> 248 us (0.36); the launches traced: 679 us -> 248 us
  matrix products: 256 us -> 0 us
  waiting for transfers between devices: 260 us -> 94.8 us
  local copies, waits for them, and re-layouts: 143 us -> 1.43 us
  starting transfers between devices: 0.28 us -> 71 us
  Pallas kernels: 0 us -> 53.5 us
  other arithmetic: 5.25 us -> 13.5 us
    dot_general x12 -> x0, matrix products: 256 us -> none  [the longest x4 86 us: block_sums(): return total + jnp.dot(onehot, lower, preferred_element_type=jnp.float32)]
    reduce_scatter x4 -> x0, waiting for transfers between devices: 148 us -> none  [the longest x2 148 us: mirror_reduce(): lax.psum_scatter(partial_sums.astype(jnp.bfloat16), 'row', scatter_dimens...]
    all_gather x4 -> x2, waiting for transfers between devices: 109 us -> 0.01 us  [gather_col(): return [lax.all_gather(field, 'col', axis=0, tiled=True)]]
    ppermute x0 -> x30, waiting for transfers between devices: none -> 90.6 us  [the longest x28 82.6 us: send_row(): return lax.ppermute(value, 'row', pairs)]
    dot_general x4 -> x0, local copies, waits for them, and re-layouts: 85.2 us -> none  [the longest x2 42.7 us: slot_products(): jnp.einsum('tab,tbk->tak', tiles, picked_cols, preferred_element_type=jnp...]
    pallas_call x0 -> x4, Pallas kernels: none -> 53.5 us  [spmv(): pl.pallas_call(functools.partial(spmv_kernel, mirror, n_in, n_out), grid_...]
    ppermute x0 -> x30, starting transfers between devices: none -> 52.7 us  [the longest x28 50.3 us: send_row(): return lax.ppermute(value, 'row', pairs)]
    gather x4 -> x0, local copies, waits for them, and re-layouts: 38 us -> none  [the longest x2 19.7 us: slot_products(): picked_rows = jnp.take(row_blocks, tile_rows, axis=0)]
  transfers between devices with their start and end apart: 8 -> 34, of which waited for: 4 -> 17; matrix products, arithmetic and copies ran while one was open for 59% -> 3% of each run, Pallas kernels for 0% -> 22%
where the time goes in v1:
time: 248 us
  waiting for transfers between devices  94.8 us (38%)
  starting transfers between devices  71 us (29%)
  Pallas kernels  53.5 us (22%)
  between operations  14.2 us (6%)
  other arithmetic  13.5 us (5%)
    ppermute x28, waiting for transfers between devices, send_row(): return lax.ppermute(value, 'row', pairs)  82.6 us
    pallas_call x4, Pallas kernels, spmv(): pl.pallas_call(functools.partial(spmv_kernel, mirror, n_in, n_out), grid_...  53.5 us
    ppermute x28, starting transfers between devices, send_row(): return lax.ppermute(value, 'row', pairs)  50.3 us
    all_to_all x2, starting transfers between devices, scatter_col(): lax.all_to_all(chunks, 'col', 0, 0, axis_index_groups=groups, tiled=True)  18.3 us
    ppermute x2, waiting for transfers between devices, send_col(): return lax.ppermute(value, 'col', pairs)  7.99 us
    convert_element_type x2, other arithmetic, apply(): (mine.astype(jnp.float32) + theirs.astype(jnp.float32)).astype(jnp.bfloat16)  6.99 us
  transfers between devices with their start and end apart: 34, of which 17 were waited for; matrix products, arithmetic and copies ran while one was open for 3% of the time, Pallas kernels for 22%

profile of v1, /device:TPU:14, one launch (start us, length us, event | category | flops | bytes accessed | tf_op | source)
XLA Modules:
  0.0 248.5 jit_solution(17302212843167168660)
XLA Ops:
  12.5 4.6 %collective-permute-done.rest_1_ = bf16[1024,128]{1,0:T(8,128)(2,1)S(1)} collective-permute-done((bf16[1024,128]{1,0:T(8,128)(2,1)}, bf16[1024,128]{1,0:T(8,128)(2,1)S(1)}, u32[]{:S(2)}, u32[]{:S(2)}) %collective-permute-start) | collective-permute-done | bytes 262176 | tf_op jit(solution)/shard_map/ppermute | solution.py:25
  20.0 2.9 %collective-permute-start.6 = (bf16[1024,128]{1,0:T(8,128)(2,1)S(1)}, bf16[1024,128]{1,0:T(8,128)(2,1)S(1)}, u32[]{:S(2)}, u32[]{:S(2)}) collective-permute-start(bf16[1024,128]{1,0:T(8,128)(2,1)S(1)} %collective-permute-done.rest_1_), channel_id=1, source_target_pairs={{0,96},{16,112},{32,0},{48,16},{64,32},{80,48},{96,64},{112,80},{1... | collective-permute-start | bytes 786440 | tf_op jit(solution)/shard_map/ppermute | solution.py:25
  26.8 3.6 %collective-permute-done.2.rest_3_ = bf16[1024,128]{1,0:T(8,128)(2,1)S(1)} collective-permute-done((bf16[1024,128]{1,0:T(8,128)(2,1)S(1)}, bf16[1024,128]{1,0:T(8,128)(2,1)S(1)}, u32[]{:S(2)}, u32[]{:S(2)}) %collective-permute-start.2) | collective-permute-done | bytes 262176 | tf_op jit(solution)/shard_map/ppermute | solution.py:25
  32.4 3.8 %collective-permute-done.6.rest_7_ = bf16[1024,128]{1,0:T(8,128)(2,1)S(1)} collective-permute-done((bf16[1024,128]{1,0:T(8,128)(2,1)S(1)}, bf16[1024,128]{1,0:T(8,128)(2,1)S(1)}, u32[]{:S(2)}, u32[]{:S(2)}) %collective-permute-start.6) | collective-permute-done | bytes 262176 | tf_op jit(solution)/shard_map/ppermute | solution.py:25
  36.9 13.4 %direct_sums.2 = (bf16[8192,128]{1,0:T(8,128)(2,1)}, bf16[8192,128]{1,0:T(8,128)(2,1)}) custom-call(s32[160]{0:T(256)} %get-tuple-element.47.out_slot, s32[160]{0:T(256)} %get-tuple-element.50.in_slot, s32[1]{0:T(128)} %copy.6.count, bf16[160,256,256]{2,1,0:T(8,128)(2,1)} %tiles.7, bf16[1024,128]{1,0:T(8,128)(2,1)} %rest_0_.1, bf16[1024,128]{1,0:T(8,128)(2,1)} %copy-done.2, ...), custom_call_target="tpu_custom_call" | custom-call | flops 2684354560 | bytes 20971520 | tf_op jit(solution)/shard_map/direct_sums/pallas_call | solution.py:91
  51.7 4.0 %collective-permute-done.7 = bf16[8192,128]{1,0:T(8,128)(2,1)S(1)} collective-permute-done((bf16[8192,128]{1,0:T(8,128)(2,1)}, bf16[8192,128]{1,0:T(8,128)(2,1)S(1)}, u32[]{:S(2)}, u32[]{:S(2)}) %collective-permute-start.7) | collective-permute-done | bytes 2097184 | tf_op jit(solution)/shard_map/ppermute | solution.py:36
  55.7 3.5 %add_convert_fusion.1 = bf16[8192,128]{1,0:T(8,128)(2,1)} fusion(bf16[8192,128]{1,0:T(8,128)(2,1)S(1)} %collective-permute-done.7, bf16[8192,128]{1,0:T(8,128)(2,1)} %get-tuple-element.25), kind=kLoop, calls=%fused_computation.1 | loop fusion | flops 4194304 | bytes 6291456 | tf_op jit(solution)/shard_map/convert_element_type | solution.py:140
  59.2 10.2 %all-to-all-start = ((bf16[8,1024,128]{2,1,0:T(8,128)(2,1)}), bf16[8,1024,128]{2,1,0:T(8,128)(2,1)S(1)}, u32[]{:S(2)}, u32[]{:S(2)}) async-start(bf16[8,1024,128]{2,1,0:T(8,128)(2,1)} %bitcast.1), calls=%async_computation | async-start | bytes 4194304 | tf_op jit(solution)/shard_map/all_to_all | solution.py:129
  69.4 13.3 %mirror_sums.2 = (bf16[1024,128]{1,0:T(8,128)(2,1)}, bf16[1024,128]{1,0:T(8,128)(2,1)}, bf16[1024,128]{1,0:T(8,128)(2,1)}, bf16[1024,128]{1,0:T(8,128)(2,1)}, bf...) custom-call(s32[160]{0:T(256)} %get-tuple-element.49.out_slot, ...), custom_call_target="tpu_custom_call" | custom-call | flops 2684354560 | bytes 20971520 | tf_op jit(solution)/shard_map/mirror_sums/pallas_call | solution.py:91
  82.9 7.3 %collective-permute-start.12 = (bf16[1024,128]{1,0:T(8,128)(2,1)}, bf16[1024,128]{1,0:T(8,128)(2,1)S(1)}, u32[]{:S(2)}, u32[]{:S(2)}) collective-permute-start(bf16[1024,128]{1,0:T(8,128)(2,1)} %get-tuple-element.32), channel_id=1, source_target_pairs={{0,80},{16,64},{32,112},{48,96},{64,16},{80,0},{96,48},{112,32},{1... | collective-permute-start | bytes 786440 | tf_op jit(solution)/shard_map/ppermute | solution.py:25
  90.7 9.9 %collective-permute-done.10 = bf16[1024,128]{1,0:T(8,128)(2,1)S(1)} collective-permute-done((bf16[1024,128]{1,0:T(8,128)(2,1)}, bf16[1024,128]{1,0:T(8,128)(2,1)S(1)}, u32[]{:S(2)}, u32[]{:S(2)}) %collective-permute-start.10) | collective-permute-done | bytes 262176 | tf_op jit(solution)/shard_map/ppermute | solution.py:25
  100.7 6.7 %collective-permute-start.9 = (bf16[1024,128]{1,0:T(8,128)(2,1)}, bf16[1024,128]{1,0:T(8,128)(2,1)}, u32[]{:S(2)}, u32[]{:S(2)}) collective-permute-start(bf16[1024,128]{1,0:T(8,128)(2,1)} %get-tuple-element.29), channel_id=1, source_target_pairs={{0,32},{16,48},{32,64},{48,80},{64,96},{80,112},{96,0},{112,16},{1... | collective-permute-start | bytes 786440 | tf_op jit(solution)/shard_map/ppermute | solution.py:25
  107.4 3.5 %all-to-all-done = bf16[8,1024,128]{2,1,0:T(8,128)(2,1)S(1)} async-done(((bf16[8,1024,128]{2,1,0:T(8,128)(2,1)}), bf16[8,1024,128]{2,1,0:T(8,128)(2,1)S(1)}, u32[]{:S(2)}, u32[]{:S(2)}) %all-to-all-start) | async-done | bytes 2097184 | tf_op jit(solution)/shard_map/all_to_all | solution.py:129
  110.9 5.3 %collective-permute-done.8 = bf16[1024,128]{1,0:T(8,128)(2,1)} collective-permute-done((bf16[1024,128]{1,0:T(8,128)(2,1)}, bf16[1024,128]{1,0:T(8,128)(2,1)}, u32[]{:S(2)}, u32[]{:S(2)}) %collective-permute-start.8) | collective-permute-done | bytes 262176 | tf_op jit(solution)/shard_map/ppermute | solution.py:25
  116.2 2.5 %fusion.2.rest_0_ = bf16[1024,128]{1,0:T(8,128)(2,1)} fusion(bf16[1024,128]{1,0:T(8,128)(2,1)S(1)} %copy-done, bf16[1024,128]{1,0:T(8,128)(2,1)} %collective-permute-done.14, bf16[1024,128]{1,0:T(8,128)(2,1)S(1)} %collective-permute-done.13, bf16[1024,128]{1,0:T(8,128)(2,1)S(1)} %collective-permute-done.12, bf16[1024,128]{1,0:T(8,128)(2,1)S(1)} %collective-permute-done.11, ...), kind=kLoop, calls=%fused_computation.6 | loop fusion | flops 4718592 | bytes 4718592 | tf_op jit(solution)/shard_map/convert_element_type | solution.py:168
  118.7 3.5 %collective-permute-start.15 = (bf16[1024,128]{1,0:T(8,128)(2,1)}, bf16[1024,128]{1,0:T(8,128)(2,1)S(1)}, u32[]{:S(2)}, u32[]{:S(2)}) collective-permute-start(bf16[1024,128]{1,0:T(8,128)(2,1)} %fusion.2.rest_0_), channel_id=1, source_target_pairs={{0,16},{16,0},{32,48},{48,32},{64,80},{80,64},{96,112},{112,96},{1... | collective-permute-start | bytes 786440 | tf_op jit(solution)/shard_map/ppermute | solution.py:25
  124.2 4.6 %collective-permute-done.15.rest_1_ = bf16[1024,128]{1,0:T(8,128)(2,1)S(1)} collective-permute-done((bf16[1024,128]{1,0:T(8,128)(2,1)}, bf16[1024,128]{1,0:T(8,128)(2,1)S(1)}, u32[]{:S(2)}, u32[]{:S(2)}) %collective-permute-start.15) | collective-permute-done | bytes 262176 | tf_op jit(solution)/shard_map/ppermute | solution.py:25
  128.8 5.6 %collective-permute-start.17 = (bf16[1024,128]{1,0:T(8,128)(2,1)S(1)}, bf16[1024,128]{1,0:T(8,128)(2,1)S(1)}, u32[]{:S(2)}, u32[]{:S(2)}) collective-permute-start(bf16[1024,128]{1,0:T(8,128)(2,1)S(1)} %collective-permute-done.15.rest_1_), channel_id=1, source_target_pairs={{0,32},{16,48},{32,64},{48,80},{64,96},{80,112},{96,0},{112,16},{1... | collective-permute-start | bytes 786440 | tf_op jit(solution)/shard_map/ppermute | solution.py:25
  135.3 7.9 %collective-permute-done.20.rest_6_ = bf16[1024,128]{1,0:T(8,128)(2,1)S(1)} collective-permute-done((bf16[1024,128]{1,0:T(8,128)(2,1)}, bf16[1024,128]{1,0:T(8,128)(2,1)S(1)}, u32[]{:S(2)}, u32[]{:S(2)}) %collective-permute-start.20) | collective-permute-done | bytes 262176 | tf_op jit(solution)/shard_map/ppermute | solution.py:25
  143.2 2.9 %collective-permute-done.17.rest_3_ = bf16[1024,128]{1,0:T(8,128)(2,1)S(1)} collective-permute-done((bf16[1024,128]{1,0:T(8,128)(2,1)S(1)}, bf16[1024,128]{1,0:T(8,128)(2,1)S(1)}, u32[]{:S(2)}, u32[]{:S(2)}) %collective-permute-start.17) | collective-permute-done | bytes 262176 | tf_op jit(solution)/shard_map/ppermute | solution.py:25
  146.1 3.4 %collective-permute-done.21.rest_7_ = bf16[1024,128]{1,0:T(8,128)(2,1)S(1)} collective-permute-done((bf16[1024,128]{1,0:T(8,128)(2,1)S(1)}, bf16[1024,128]{1,0:T(8,128)(2,1)S(1)}, u32[]{:S(2)}, u32[]{:S(2)}) %collective-permute-start.21) | collective-permute-done | bytes 262176 | tf_op jit(solution)/shard_map/ppermute | solution.py:25
  150.2 13.4 %direct_sums.3 = (bf16[8192,128]{1,0:T(8,128)(2,1)}, bf16[8192,128]{1,0:T(8,128)(2,1)}) custom-call(s32[160]{0:T(256)} %get-tuple-element.47.out_slot, s32[160]{0:T(256)} %get-tuple-element.50.in_slot, s32[1]{0:T(128)} %copy.6.count, bf16[160,256,256]{2,1,0:T(8,128)(2,1)} %tiles.7, bf16[1024,128]{1,0:T(8,128)(2,1)} %fusion.2.rest_0_, ...), custom_call_target="tpu_custom_call" | custom-call | flops 2684354560 | bytes 20971520 | tf_op jit(solution)/shard_map/direct_sums/pallas_call | solution.py:91
  164.6 4.0 %collective-permute-done.22 = bf16[8192,128]{1,0:T(8,128)(2,1)S(1)} collective-permute-done((bf16[8192,128]{1,0:T(8,128)(2,1)}, bf16[8192,128]{1,0:T(8,128)(2,1)S(1)}, u32[]{:S(2)}, u32[]{:S(2)}) %collective-permute-start.22) | collective-permute-done | bytes 2097184 | tf_op jit(solution)/shard_map/ppermute | solution.py:36
  168.6 3.5 %add_convert_fusion = bf16[8192,128]{1,0:T(8,128)(2,1)} fusion(bf16[8192,128]{1,0:T(8,128)(2,1)S(1)} %collective-permute-done.22, bf16[8192,128]{1,0:T(8,128)(2,1)} %get-tuple-element.35), kind=kLoop, calls=%fused_computation | loop fusion | flops 4194304 | bytes 6291456 | tf_op jit(solution)/shard_map/convert_element_type | solution.py:140
  172.1 8.1 %all-to-all-start.1 = ((bf16[8,1024,128]{2,1,0:T(8,128)(2,1)}), bf16[8,1024,128]{2,1,0:T(8,128)(2,1)S(1)}, u32[]{:S(2)}, u32[]{:S(2)}) async-start(bf16[8,1024,128]{2,1,0:T(8,128)(2,1)} %bitcast.3), calls=%async_computation.1 | async-start | bytes 4194304 | tf_op jit(solution)/shard_map/all_to_all | solution.py:129
  180.2 13.4 %mirror_sums.3 = (bf16[1024,128]{1,0:T(8,128)(2,1)}, bf16[1024,128]{1,0:T(8,128)(2,1)}, bf16[1024,128]{1,0:T(8,128)(2,1)}, bf16[1024,128]{1,0:T(8,128)(2,1)}, bf...) custom-call(s32[160]{0:T(256)} %get-tuple-element.49.out_slot, ...), custom_call_target="tpu_custom_call" | custom-call | flops 2684354560 | bytes 20971520 | tf_op jit(solution)/shard_map/mirror_sums/pallas_call | solution.py:91
  193.8 4.4 %collective-permute-start.24 = (bf16[1024,128]{1,0:T(8,128)(2,1)}, bf16[1024,128]{1,0:T(8,128)(2,1)S(1)}, u32[]{:S(2)}, u32[]{:S(2)}) collective-permute-start(bf16[1024,128]{1,0:T(8,128)(2,1)} %get-tuple-element.39), channel_id=1, source_target_pairs={{0,32},{16,48},{32,64},{48,80},{64,96},{80,112},{96,0},{112,16},{1... | collective-permute-start | bytes 786440 | tf_op jit(solution)/shard_map/ppermute | solution.py:25
  200.8 3.4 %collective-permute-start.27 = (bf16[1024,128]{1,0:T(8,128)(2,1)}, bf16[1024,128]{1,0:T(8,128)(2,1)}, u32[]{:S(2)}, u32[]{:S(2)}) collective-permute-start(bf16[1024,128]{1,0:T(8,128)(2,1)} %get-tuple-element.42), channel_id=1, source_target_pairs={{0,80},{16,64},{32,112},{48,96},{64,16},{80,0},{96,48},{112,32},{1... | collective-permute-start | bytes 786440 | tf_op jit(solution)/shard_map/ppermute | solution.py:25
  204.2 18.1 %collective-permute-done.23 = bf16[1024,128]{1,0:T(8,128)(2,1)S(1)} collective-permute-done((bf16[1024,128]{1,0:T(8,128)(2,1)}, bf16[1024,128]{1,0:T(8,128)(2,1)S(1)}, u32[]{:S(2)}, u32[]{:S(2)}) %collective-permute-start.23) | collective-permute-done | bytes 262176 | tf_op jit(solution)/shard_map/ppermute | solution.py:25
  224.2 8.8 %collective-permute-done.28 = bf16[1024,128]{1,0:T(8,128)(2,1)} collective-permute-done((bf16[1024,128]{1,0:T(8,128)(2,1)}, bf16[1024,128]{1,0:T(8,128)(2,1)}, u32[]{:S(2)}, u32[]{:S(2)}) %collective-permute-start.28) | collective-permute-done | bytes 262176 | tf_op jit(solution)/shard_map/ppermute | solution.py:25
  233.0 5.9 %collective-permute-done.29 = bf16[1024,128]{1,0:T(8,128)(2,1)} collective-permute-done((bf16[1024,128]{1,0:T(8,128)(2,1)}, bf16[1024,128]{1,0:T(8,128)(2,1)}, u32[]{:S(2)}, u32[]{:S(2)}) %collective-permute-start.29) | collective-permute-done | bytes 262176 | tf_op jit(solution)/shard_map/ppermute | solution.py:25
  238.9 2.7 %convert_subtract_fusion = f32[1024,128]{1,0:T(8,128)} fusion(bf16[1024,128]{1,0:T(8,128)(2,1)S(1)} %copy-done, bf16[1024,128]{1,0:T(8,128)(2,1)S(1)} %copy-done.1, bf16[1024,128]{1,0:T(8,128)(2,1)} %collective-permute-done.29, bf16[1024,128]{1,0:T(8,128)(2,1)} %collective-permute-done.28, bf16[1024,128]{1,0:T(8,128)(2,1)} %collective-permute-done.27, ...), kind=kLoop, calls=%fused_computation.2 | loop fusion | flops 4849664 | bytes 5242880 | tf_op jit(solution)/shard_map/sub | solution.py:170
  (79 shorter events, 26.4 us)
Async XLA Ops:
  6.5 62.8 %all-gather.3.cloned.1.call-start = ((), (), s32[]{:S(2)}) async-start(), calls=%async_computation.2 | async-start | bytes 4456448 | tf_op jit(solution)/shard_map/all_gather | solution.py:124
  7.3 9.8 %collective-permute-start = (bf16[1024,128]{1,0:T(8,128)(2,1)}, bf16[1024,128]{1,0:T(8,128)(2,1)S(1)}, u32[]{:S(2)}, u32[]{:S(2)}) collective-permute-start(bf16[1024,128]{1,0:T(8,128)(2,1)} %rest_0_.1), channel_id=1, source_target_pairs={{0,16},{16,0},{32,48},{48,32},{64,80},{80,64},{96,112},{112,96},{1... | collective-permute-start | bytes 786440 | tf_op jit(solution)/shard_map/ppermute | solution.py:25
  9.6 10.4 %collective-permute-start.1 = (bf16[1024,128]{1,0:T(8,128)(2,1)}, bf16[1024,128]{1,0:T(8,128)(2,1)S(1)}, u32[]{:S(2)}, u32[]{:S(2)}) collective-permute-start(bf16[1024,128]{1,0:T(8,128)(2,1)} %rest_0_.1), channel_id=1, source_target_pairs={{0,32},{16,48},{32,64},{48,80},{64,96},{80,112},{96,0},{112,16},{1... | collective-permute-start | bytes 786440 | tf_op jit(solution)/shard_map/ppermute | solution.py:25
  10.1 14.8 %collective-permute-start.3 = (bf16[1024,128]{1,0:T(8,128)(2,1)}, bf16[1024,128]{1,0:T(8,128)(2,1)S(1)}, u32[]{:S(2)}, u32[]{:S(2)}) collective-permute-start(bf16[1024,128]{1,0:T(8,128)(2,1)} %rest_0_.1), channel_id=1, source_target_pairs={{0,64},{16,80},{32,96},{48,112},{64,0},{80,16},{96,32},{112,48},{1... | collective-permute-start | bytes 786440 | tf_op jit(solution)/shard_map/ppermute | solution.py:25
  12.5 14.3 %collective-permute-start.5 = (bf16[1024,128]{1,0:T(8,128)(2,1)}, bf16[1024,128]{1,0:T(8,128)(2,1)S(1)}, u32[]{:S(2)}, u32[]{:S(2)}) collective-permute-start(bf16[1024,128]{1,0:T(8,128)(2,1)} %rest_0_.1), channel_id=1, source_target_pairs={{0,96},{16,112},{32,0},{48,16},{64,32},{80,48},{96,64},{112,80},{1... | collective-permute-start | bytes 786440 | tf_op jit(solution)/shard_map/ppermute | solution.py:25
  17.1 13.3 %collective-permute-start.2 = (bf16[1024,128]{1,0:T(8,128)(2,1)S(1)}, bf16[1024,128]{1,0:T(8,128)(2,1)S(1)}, u32[]{:S(2)}, u32[]{:S(2)}) collective-permute-start(bf16[1024,128]{1,0:T(8,128)(2,1)S(1)} %collective-permute-done.rest_1_), channel_id=1, source_target_pairs={{0,32},{16,48},{32,64},{48,80},{64,96},{80,112},{96,0},{112,16},{1... | collective-permute-start | bytes 786440 | tf_op jit(solution)/shard_map/ppermute | solution.py:25
  17.6 14.8 %collective-permute-start.4 = (bf16[1024,128]{1,0:T(8,128)(2,1)S(1)}, bf16[1024,128]{1,0:T(8,128)(2,1)S(1)}, u32[]{:S(2)}, u32[]{:S(2)}) collective-permute-start(bf16[1024,128]{1,0:T(8,128)(2,1)S(1)} %collective-permute-done.rest_1_), channel_id=1, source_target_pairs={{0,64},{16,80},{32,96},{48,112},{64,0},{80,16},{96,32},{112,48},{1... | collective-permute-start | bytes 786440 | tf_op jit(solution)/shard_map/ppermute | solution.py:25
  20.0 16.2 %collective-permute-start.6 = (bf16[1024,128]{1,0:T(8,128)(2,1)S(1)}, bf16[1024,128]{1,0:T(8,128)(2,1)S(1)}, u32[]{:S(2)}, u32[]{:S(2)}) collective-permute-start(bf16[1024,128]{1,0:T(8,128)(2,1)S(1)} %collective-permute-done.rest_1_), channel_id=1, source_target_pairs={{0,96},{16,112},{32,0},{48,16},{64,32},{80,48},{96,64},{112,80},{1... | collective-permute-start | bytes 786440 | tf_op jit(solution)/shard_map/ppermute | solution.py:25
  59.2 51.7 %all-to-all-start = ((bf16[8,1024,128]{2,1,0:T(8,128)(2,1)}), bf16[8,1024,128]{2,1,0:T(8,128)(2,1)S(1)}, u32[]{:S(2)}, u32[]{:S(2)}) async-start(bf16[8,1024,128]{2,1,0:T(8,128)(2,1)} %bitcast.1), calls=%async_computation | async-start | bytes 4194304 | tf_op jit(solution)/shard_map/all_to_all | solution.py:129
  69.4 110.9 %all-gather.5.cloned.1.call-start = ((), (), s32[]{:S(2)}) async-start(), calls=%async_computation.3 | async-start | bytes 4456448 | tf_op jit(solution)/shard_map/all_gather | solution.py:124
  82.7 18.0 %collective-permute-start.10 = (bf16[1024,128]{1,0:T(8,128)(2,1)}, bf16[1024,128]{1,0:T(8,128)(2,1)S(1)}, u32[]{:S(2)}, u32[]{:S(2)}) collective-permute-start(bf16[1024,128]{1,0:T(8,128)(2,1)} %get-tuple-element.30), channel_id=1, source_target_pairs={{0,48},{16,32},{32,80},{48,64},{64,112},{80,96},{96,16},{112,0},{1... | collective-permute-start | bytes 786440 | tf_op jit(solution)/shard_map/ppermute | solution.py:25
  82.8 17.9 %collective-permute-start.11 = (bf16[1024,128]{1,0:T(8,128)(2,1)}, bf16[1024,128]{1,0:T(8,128)(2,1)S(1)}, u32[]{:S(2)}, u32[]{:S(2)}) collective-permute-start(bf16[1024,128]{1,0:T(8,128)(2,1)} %get-tuple-element.31), channel_id=1, source_target_pairs={{0,64},{16,80},{32,96},{48,112},{64,0},{80,16},{96,32},{112,48},{1... | collective-permute-start | bytes 786440 | tf_op jit(solution)/shard_map/ppermute | solution.py:25
  82.9 28.0 %collective-permute-start.12 = (bf16[1024,128]{1,0:T(8,128)(2,1)}, bf16[1024,128]{1,0:T(8,128)(2,1)S(1)}, u32[]{:S(2)}, u32[]{:S(2)}) collective-permute-start(bf16[1024,128]{1,0:T(8,128)(2,1)} %get-tuple-element.32), channel_id=1, source_target_pairs={{0,80},{16,64},{32,112},{48,96},{64,16},{80,0},{96,48},{112,32},{1... | collective-permute-start | bytes 786440 | tf_op jit(solution)/shard_map/ppermute | solution.py:25
  90.1 20.7 %collective-permute-start.13 = (bf16[1024,128]{1,0:T(8,128)(2,1)}, bf16[1024,128]{1,0:T(8,128)(2,1)S(1)}, u32[]{:S(2)}, u32[]{:S(2)}) collective-permute-start(bf16[1024,128]{1,0:T(8,128)(2,1)} %get-tuple-element.33), channel_id=1, source_target_pairs={{0,96},{16,112},{32,0},{48,16},{64,32},{80,48},{96,64},{112,80},{1... | collective-permute-start | bytes 786440 | tf_op jit(solution)/shard_map/ppermute | solution.py:25
  90.7 20.1 %collective-permute-start.14 = (bf16[1024,128]{1,0:T(8,128)(2,1)}, bf16[1024,128]{1,0:T(8,128)(2,1)}, u32[]{:S(2)}, u32[]{:S(2)}) collective-permute-start(bf16[1024,128]{1,0:T(8,128)(2,1)} %get-tuple-element.34), channel_id=1, source_target_pairs={{0,112},{16,96},{32,16},{48,0},{64,48},{80,32},{96,80},{112,64},{1... | collective-permute-start | bytes 786440 | tf_op jit(solution)/shard_map/ppermute | solution.py:25
  100.7 15.5 %collective-permute-start.8 = (bf16[1024,128]{1,0:T(8,128)(2,1)}, bf16[1024,128]{1,0:T(8,128)(2,1)}, u32[]{:S(2)}, u32[]{:S(2)}) collective-permute-start(bf16[1024,128]{1,0:T(8,128)(2,1)} %get-tuple-element.28), channel_id=1, source_target_pairs={{0,16},{16,0},{32,48},{48,32},{64,80},{80,64},{96,112},{112,96},{1... | collective-permute-start | bytes 786440 | tf_op jit(solution)/shard_map/ppermute | solution.py:25
  100.7 15.5 %collective-permute-start.9 = (bf16[1024,128]{1,0:T(8,128)(2,1)}, bf16[1024,128]{1,0:T(8,128)(2,1)}, u32[]{:S(2)}, u32[]{:S(2)}) collective-permute-start(bf16[1024,128]{1,0:T(8,128)(2,1)} %get-tuple-element.29), channel_id=1, source_target_pairs={{0,32},{16,48},{32,64},{48,80},{64,96},{80,112},{96,0},{112,16},{1... | collective-permute-start | bytes 786440 | tf_op jit(solution)/shard_map/ppermute | solution.py:25
  118.7 10.1 %collective-permute-start.15 = (bf16[1024,128]{1,0:T(8,128)(2,1)}, bf16[1024,128]{1,0:T(8,128)(2,1)S(1)}, u32[]{:S(2)}, u32[]{:S(2)}) collective-permute-start(bf16[1024,128]{1,0:T(8,128)(2,1)} %fusion.2.rest_0_), channel_id=1, source_target_pairs={{0,16},{16,0},{32,48},{48,32},{64,80},{80,64},{96,112},{112,96},{1... | collective-permute-start | bytes 786440 | tf_op jit(solution)/shard_map/ppermute | solution.py:25
  122.2 12.2 %collective-permute-start.16 = (bf16[1024,128]{1,0:T(8,128)(2,1)}, bf16[1024,128]{1,0:T(8,128)(2,1)S(1)}, u32[]{:S(2)}, u32[]{:S(2)}) collective-permute-start(bf16[1024,128]{1,0:T(8,128)(2,1)} %fusion.2.rest_0_), channel_id=1, source_target_pairs={{0,32},{16,48},{32,64},{48,80},{64,96},{80,112},{96,0},{112,16},{1... | collective-permute-start | bytes 786440 | tf_op jit(solution)/shard_map/ppermute | solution.py:25
  123.2 12.1 %collective-permute-start.18 = (bf16[1024,128]{1,0:T(8,128)(2,1)}, bf16[1024,128]{1,0:T(8,128)(2,1)S(1)}, u32[]{:S(2)}, u32[]{:S(2)}) collective-permute-start(bf16[1024,128]{1,0:T(8,128)(2,1)} %fusion.2.rest_0_), channel_id=1, source_target_pairs={{0,64},{16,80},{32,96},{48,112},{64,0},{80,16},{96,32},{112,48},{1... | collective-permute-start | bytes 786440 | tf_op jit(solution)/shard_map/ppermute | solution.py:25
  123.2 20.0 %collective-permute-start.20 = (bf16[1024,128]{1,0:T(8,128)(2,1)}, bf16[1024,128]{1,0:T(8,128)(2,1)S(1)}, u32[]{:S(2)}, u32[]{:S(2)}) collective-permute-start(bf16[1024,128]{1,0:T(8,128)(2,1)} %fusion.2.rest_0_), channel_id=1, source_target_pairs={{0,96},{16,112},{32,0},{48,16},{64,32},{80,48},{96,64},{112,80},{1... | collective-permute-start | bytes 786440 | tf_op jit(solution)/shard_map/ppermute | solution.py:25
  128.8 17.3 %collective-permute-start.17 = (bf16[1024,128]{1,0:T(8,128)(2,1)S(1)}, bf16[1024,128]{1,0:T(8,128)(2,1)S(1)}, u32[]{:S(2)}, u32[]{:S(2)}) collective-permute-start(bf16[1024,128]{1,0:T(8,128)(2,1)S(1)} %collective-permute-done.15.rest_1_), channel_id=1, source_target_pairs={{0,32},{16,48},{32,64},{48,80},{64,96},{80,112},{96,0},{112,16},{1... | collective-permute-start | bytes 786440 | tf_op jit(solution)/shard_map/ppermute | solution.py:25
  134.4 11.7 %collective-permute-start.19 = (bf16[1024,128]{1,0:T(8,128)(2,1)S(1)}, bf16[1024,128]{1,0:T(8,128)(2,1)S(1)}, u32[]{:S(2)}, u32[]{:S(2)}) collective-permute-start(bf16[1024,128]{1,0:T(8,128)(2,1)S(1)} %collective-permute-done.15.rest_1_), channel_id=1, source_target_pairs={{0,64},{16,80},{32,96},{48,112},{64,0},{80,16},{96,32},{112,48},{1... | collective-permute-start | bytes 786440 | tf_op jit(solution)/shard_map/ppermute | solution.py:25
  134.4 15.0 %collective-permute-start.21 = (bf16[1024,128]{1,0:T(8,128)(2,1)S(1)}, bf16[1024,128]{1,0:T(8,128)(2,1)S(1)}, u32[]{:S(2)}, u32[]{:S(2)}) collective-permute-start(bf16[1024,128]{1,0:T(8,128)(2,1)S(1)} %collective-permute-done.15.rest_1_), channel_id=1, source_target_pairs={{0,96},{16,112},{32,0},{48,16},{64,32},{80,48},{96,64},{112,80},{1... | collective-permute-start | bytes 786440 | tf_op jit(solution)/shard_map/ppermute | solution.py:25
  172.1 52.1 %all-to-all-start.1 = ((bf16[8,1024,128]{2,1,0:T(8,128)(2,1)}), bf16[8,1024,128]{2,1,0:T(8,128)(2,1)S(1)}, u32[]{:S(2)}, u32[]{:S(2)}) async-start(bf16[8,1024,128]{2,1,0:T(8,128)(2,1)} %bitcast.3), calls=%async_computation.1 | async-start | bytes 4194304 | tf_op jit(solution)/shard_map/all_to_all | solution.py:129
  193.7 28.6 %collective-permute-start.23 = (bf16[1024,128]{1,0:T(8,128)(2,1)}, bf16[1024,128]{1,0:T(8,128)(2,1)S(1)}, u32[]{:S(2)}, u32[]{:S(2)}) collective-permute-start(bf16[1024,128]{1,0:T(8,128)(2,1)} %get-tuple-element.38), channel_id=1, source_target_pairs={{0,16},{16,0},{32,48},{48,32},{64,80},{80,64},{96,112},{112,96},{1... | collective-permute-start | bytes 786440 | tf_op jit(solution)/shard_map/ppermute | solution.py:25
  193.8 28.4 %collective-permute-start.24 = (bf16[1024,128]{1,0:T(8,128)(2,1)}, bf16[1024,128]{1,0:T(8,128)(2,1)S(1)}, u32[]{:S(2)}, u32[]{:S(2)}) collective-permute-start(bf16[1024,128]{1,0:T(8,128)(2,1)} %get-tuple-element.39), channel_id=1, source_target_pairs={{0,32},{16,48},{32,64},{48,80},{64,96},{80,112},{96,0},{112,16},{1... | collective-permute-start | bytes 786440 | tf_op jit(solution)/shard_map/ppermute | solution.py:25
  198.2 26.0 %collective-permute-start.25 = (bf16[1024,128]{1,0:T(8,128)(2,1)}, bf16[1024,128]{1,0:T(8,128)(2,1)S(1)}, u32[]{:S(2)}, u32[]{:S(2)}) collective-permute-start(bf16[1024,128]{1,0:T(8,128)(2,1)} %get-tuple-element.40), channel_id=1, source_target_pairs={{0,48},{16,32},{32,80},{48,64},{64,112},{80,96},{96,16},{112,0},{1... | collective-permute-start | bytes 786440 | tf_op jit(solution)/shard_map/ppermute | solution.py:25
  199.7 24.5 %collective-permute-start.26 = (bf16[1024,128]{1,0:T(8,128)(2,1)}, bf16[1024,128]{1,0:T(8,128)(2,1)}, u32[]{:S(2)}, u32[]{:S(2)}) collective-permute-start(bf16[1024,128]{1,0:T(8,128)(2,1)} %get-tuple-element.41), channel_id=1, source_target_pairs={{0,64},{16,80},{32,96},{48,112},{64,0},{80,16},{96,32},{112,48},{1... | collective-permute-start | bytes 786440 | tf_op jit(solution)/shard_map/ppermute | solution.py:25
  200.8 23.4 %collective-permute-start.27 = (bf16[1024,128]{1,0:T(8,128)(2,1)}, bf16[1024,128]{1,0:T(8,128)(2,1)}, u32[]{:S(2)}, u32[]{:S(2)}) collective-permute-start(bf16[1024,128]{1,0:T(8,128)(2,1)} %get-tuple-element.42), channel_id=1, source_target_pairs={{0,80},{16,64},{32,112},{48,96},{64,16},{80,0},{96,48},{112,32},{1... | collective-permute-start | bytes 786440 | tf_op jit(solution)/shard_map/ppermute | solution.py:25
  222.3 10.8 %collective-permute-start.28 = (bf16[1024,128]{1,0:T(8,128)(2,1)}, bf16[1024,128]{1,0:T(8,128)(2,1)}, u32[]{:S(2)}, u32[]{:S(2)}) collective-permute-start(bf16[1024,128]{1,0:T(8,128)(2,1)} %get-tuple-element.43), channel_id=1, source_target_pairs={{0,96},{16,112},{32,0},{48,16},{64,32},{80,48},{96,64},{112,80},{1... | collective-permute-start | bytes 786440 | tf_op jit(solution)/shard_map/ppermute | solution.py:25
  222.3 16.6 %collective-permute-start.29 = (bf16[1024,128]{1,0:T(8,128)(2,1)}, bf16[1024,128]{1,0:T(8,128)(2,1)}, u32[]{:S(2)}, u32[]{:S(2)}) collective-permute-start(bf16[1024,128]{1,0:T(8,128)(2,1)} %get-tuple-element.44), channel_id=1, source_target_pairs={{0,112},{16,96},{32,16},{48,0},{64,48},{80,32},{96,80},{112,64},{1... | collective-permute-start | bytes 786440 | tf_op jit(solution)/shard_map/ppermute | solution.py:25
  (18 other events, 245.9 us)
Sparse Core Ops, SparseCore 0:
  9.1 39.6 all-gather.2
  118.8 38.6 all-gather.4

commit v2 on v1

v2 whole, which is shorter than its diff:
```python
import functools

import jax
import jax.numpy as jnp
from jax import lax
from jax.experimental import pallas as pl
from jax.experimental.pallas import tpu as pltpu
from jax.sharding import PartitionSpec as P

center_value = 0.5
radius_value = 1.5

BS = 256
NV = 128
OWN = 4
CHUNK = 16
RING = 3
LIMIT = {False: 48, True: 60}

ROW_STEPS = [(dx, dy) for dx in range(4) for dy in range(2)]
COL_STEPS = [(dz, dy) for dz in range(4) for dy in range(2)]


def send_row(value, step):
    dx, dy = step
    pairs = [(x * 2 + y, (x + dx) % 4 * 2 + (y ^ dy)) for x in range(4) for y in range(2)]
    return lax.ppermute(value, "row", pairs)


def send_col(value, step, dk=0):
    dz, dy = step
    pairs = [
        (z * 4 + y * 2 + k, (z + dz) % 4 * 4 + (y ^ dy) * 2 + (k ^ dk))
        for z in range(4)
        for y in range(2)
        for k in range(2)
    ]
    return lax.ppermute(value, "col", pairs)


def spmv_kernel(mirror, n_in, n_out, out_slot, in_slot, count, tiles, *rest):
    v_in = rest[:n_in]
    outs = rest[n_in : n_in + n_out]
    acc, held, ring, in_sems, ring_sems = rest[n_in + n_out :]
    depth = ring.shape[0]
    steps = (count[0] + CHUNK - 1) // CHUNK

    def fetch(step):
        at = lax.rem(step, depth)
        return pltpu.make_async_copy(
            tiles.at[pl.ds(step * CHUNK, CHUNK)], ring.at[at], ring_sems.at[at]
        )

    part = held.shape[0] // n_in
    copies = [
        pltpu.make_async_copy(v_in[j], held.at[pl.ds(j * part, part)], in_sems.at[j])
        for j in range(n_in)
    ]
    for copy in copies:
        copy.start()
    for step in range(depth - 1):

        @pl.when(step < steps)
        def _():
            fetch(step).start()

    acc[...] = jnp.zeros_like(acc)
    for copy in copies:
        copy.wait()

    @pl.loop(0, steps)
    def _(step):
        @pl.when(step + depth - 1 < steps)
        def _():
            fetch(step + depth - 1).start()

        fetch(step).wait()
        at = lax.rem(step, depth)
        for j in range(CHUNK):
            slot = step * CHUNK + j
            base = pl.multiple_of(in_slot[slot] * BS, BS)
            vec = held[pl.ds(base, BS), :]
            dims = (((0,), (0,)), ((), ())) if mirror else (((1,), (0,)), ((), ()))
            acc[out_slot[slot]] += lax.dot_general(
                ring[at, j], vec, dims, preferred_element_type=jnp.float32
            )

    at = 0
    for out in outs:
        for b in range(out.shape[0] // BS):
            out[b * BS : (b + 1) * BS, :] = acc[at].astype(out.dtype)
            at += 1


def spmv(mirror, tiles, out_slot, in_slot, count, v_in, out_rows):
    slots = tiles.shape[0]
    n_in, n_out = len(v_in), len(out_rows)
    blocks_out = sum(out_rows) // BS
    return pl.pallas_call(
        functools.partial(spmv_kernel, mirror, n_in, n_out),
        in_specs=[pl.BlockSpec(memory_space=pltpu.SMEM)] * 3
        + [pl.BlockSpec(memory_space=pl.ANY)] * (1 + n_in),
        out_specs=[pl.BlockSpec(memory_space=pltpu.VMEM)] * n_out,
        scratch_shapes=[
            pltpu.VMEM((blocks_out + 1, BS, NV), jnp.float32),
            pltpu.VMEM((sum(v.shape[0] for v in v_in), NV), jnp.bfloat16),
            pltpu.VMEM((RING, CHUNK, BS, BS), jnp.bfloat16),
            pltpu.SemaphoreType.DMA((n_in,)),
            pltpu.SemaphoreType.DMA((RING,)),
        ],
        out_shape=[jax.ShapeDtypeStruct((n, NV), jnp.bfloat16) for n in out_rows],
        compiler_params=pltpu.CompilerParams(vmem_limit_bytes=LIMIT[mirror] * 2**20),
        cost_estimate=pl.CostEstimate(
            flops=2 * slots * BS * BS * NV, bytes_accessed=slots * BS * BS * 2, transcendentals=0
        ),
        name="mirror_sums" if mirror else "direct_sums",
    )(out_slot, in_slot, count, tiles, *v_in)


def gather_row(field):
    parts = {(0, 0): field, (0, 1): send_row(field, (0, 1))}
    for dx in (2, 1, 3):
        parts[dx, 0] = send_row(field, (dx, 0))
    for dx in (1, 3):
        parts[dx, 1] = send_row(parts[0, 1], (dx, 0))
    parts[2, 1] = send_row(parts[2, 0], (0, 1))
    return [parts[step] for step in ROW_STEPS]


def gather_col(field):
    return [lax.all_gather(field, "col", axis=0, tiled=True)]


def total(parts):
    return sum(part.astype(jnp.float32) for part in parts)


def rounded(parts):
    return parts[0] if len(parts) == 1 else total(parts).astype(jnp.bfloat16)


def scatter(send, own, beside, up, far, far_beside, down):
    rows = own[0].shape[0]
    passed = send(rounded(far_beside), (0, 1))
    up, down = send(rounded(up), (1, 0)), send(rounded(down), (3, 0))
    far = send(rounded(far + [passed]), (2, 0))
    beside = send(rounded(beside + [up[rows:], down[rows:]]), (0, 1))
    return own + [up[:rows], down[:rows], far, beside]


def apply(field, tiles, slots, count):
    direct_out, direct_in, mirror_out, mirror_in = slots
    rows = OWN * BS
    split = [rows, rows, 2 * rows, rows, rows, 2 * rows]
    row_parts = gather_row(field)
    col_parts = gather_col(field)
    *mine, other = spmv(False, tiles, direct_out, direct_in, count, row_parts, split + [8 * rows])
    theirs = jnp.split(send_col(other, (0, 0), 1), [rows, 2 * rows, 4 * rows, 5 * rows, 6 * rows])
    mirrored = spmv(True, tiles, mirror_out, mirror_in, count, col_parts, split)
    parts = scatter(send_col, *([a, b] for a, b in zip(mine, theirs)))
    parts += scatter(send_row, *([a] for a in mirrored))
    return total(parts)


def local(vectors, tiles, tile_rows, tile_cols, tile_count):
    row_at = lax.axis_index("row")
    col_at = lax.axis_index("col")
    x, yh = row_at // 2, row_at % 2
    z, yl, k = col_at // 4, col_at // 2 % 2, col_at % 2
    live = jnp.arange(tiles.shape[0], dtype=jnp.int32) < tile_count[0]
    own_r = tile_rows // OWN
    oz, oy, ok = own_r // 4, own_r // 2 % 2, own_r % 2
    to_col = ((oz - z) % 4 * 2 + (oy ^ yl) + (ok ^ k) * 8) * OWN + tile_rows % OWN
    from_col = tile_rows
    own_c = tile_cols // OWN
    ox, oh = own_c // 2, own_c % 2
    to_row = ((ox - x) % 4 * 2 + (oh ^ yh)) * OWN + tile_cols % OWN
    from_row = ((x - ox) % 4 * 2 + (oh ^ yh)) * OWN + tile_cols % OWN
    slots = (
        jnp.where(live, to_col, 16 * OWN),
        jnp.where(live, from_row, 0),
        jnp.where(live, to_row, 8 * OWN),
        jnp.where(live, from_col, 0),
    )
    x_float = vectors.astype(jnp.float32)
    applied = apply(vectors, tiles, slots, tile_count)
    first_term = ((applied - center_value * x_float) / radius_value).astype(jnp.bfloat16)
    second = apply(first_term, tiles, slots, tile_count)
    return 2.0 * (second - center_value * first_term.astype(jnp.float32)) / radius_value - x_float


def solution(mesh):
    return jax.shard_map(
        local,
        mesh=mesh,
        in_specs=(
            P(("row", "col"), None),
            P(("row", "col"), None, None),
            P(("row", "col")),
            P(("row", "col")),
            P(("row", "col")),
        ),
        out_specs=P(("row", "col"), None),
        check_vma=False,
    )
```

time: 248 us -> 189 us (0.76)
  waiting for transfers between devices: 94.8 us -> 48 us
  Pallas kernels: 53.5 us -> 34.1 us
  starting transfers between devices: 71 us -> 77.4 us
    ppermute x28 -> x24, waiting for transfers between devices: 82.6 us -> 38.5 us  [send_row(): return lax.ppermute(value, 'row', pairs)]
    pallas_call x4, Pallas kernels: 53.5 us -> 34.1 us  [spmv(): pl.pallas_call(functools.partial(spmv_kernel, mirror, n_in, n_out), in_sp...]
    all_to_all x2 -> x0, starting transfers between devices: 18.3 us -> none  [scatter_col(): lax.all_to_all(chunks, 'col', 0, 0, axis_index_groups=groups, tiled=True)]
    ppermute x2 -> x12, starting transfers between devices: 2.41 us -> 17.7 us  [send_col(): return lax.ppermute(value, 'col', pairs)]
    ppermute x28 -> x24, starting transfers between devices: 50.3 us -> 59.6 us  [send_row(): return lax.ppermute(value, 'row', pairs)]
    all_to_all x2 -> x0, waiting for transfers between devices: 3.49 us -> none  [scatter_col(): lax.all_to_all(chunks, 'col', 0, 0, axis_index_groups=groups, tiled=True)]
    ppermute x2 -> x12, waiting for transfers between devices: 7.99 us -> 8.74 us  [send_col(): return lax.ppermute(value, 'col', pairs)]
    convert_element_type x2 -> x10, other arithmetic: 6.99 us -> 6.46 us  [rounded(): return parts[0] if len(parts) == 1 else total(parts).astype(jnp.bfloat16)]
  transfers between devices with their start and end apart: 34 -> 38, of which waited for: 17 -> 11; matrix products, arithmetic and copies ran while one was open for 3% -> 4% of each run, Pallas kernels for 22% -> 18%
where the time goes in v2:
time: 189 us; the launch traced here: 188 us
  starting transfers between devices  77.4 us (41%)
  waiting for transfers between devices  48 us (25%)
  Pallas kernels  34.1 us (18%)
  between operations  14.3 us (8%)
  other arithmetic  12.2 us (6%)
  local copies, waits for them, and re-layouts  1.94 us (1%)
    ppermute x24, starting transfers between devices, send_row(): return lax.ppermute(value, 'row', pairs)  59.6 us
    ppermute x24, waiting for transfers between devices, send_row(): return lax.ppermute(value, 'row', pairs)  38.5 us
    pallas_call x4, Pallas kernels, spmv(): pl.pallas_call(functools.partial(spmv_kernel, mirror, n_in, n_out), in_sp...  34.1 us
    ppermute x12, starting transfers between devices, send_col(): return lax.ppermute(value, 'col', pairs)  17.7 us
    ppermute x12, waiting for transfers between devices, send_col(): return lax.ppermute(value, 'col', pairs)  8.74 us
    convert_element_type x10, other arithmetic, rounded(): return parts[0] if len(parts) == 1 else total(parts).astype(jnp.bfloat16)  6.46 us
  transfers between devices with their start and end apart: 38, of which 11 were waited for; matrix products, arithmetic and copies ran while one was open for 4% of the time, Pallas kernels for 18%

profile of v2, /device:TPU:14, one launch (start us, length us, event | category | flops | bytes accessed | tf_op | source)
XLA Modules:
  0.0 187.9 jit_solution(10729360335139579111)
XLA Ops:
  8.8 2.3 %collective-permute-start = (bf16[1024,128]{1,0:T(8,128)(2,1)}, bf16[1024,128]{1,0:T(8,128)(2,1)S(1)}, u32[]{:S(2)}, u32[]{:S(2)}) collective-permute-start(bf16[1024,128]{1,0:T(8,128)(2,1)} %rest_0_.1), channel_id=1, source_target_pairs={{0,16},{16,0},{32,48},{48,32},{64,80},{80,64},{96,112},{112,96},{1... | collective-permute-start | bytes 786440 | tf_op jit(solution)/shard_map/ppermute | solution.py:27
  11.1 3.2 %collective-permute-start.1 = (bf16[1024,128]{1,0:T(8,128)(2,1)}, bf16[1024,128]{1,0:T(8,128)(2,1)S(1)}, u32[]{:S(2)}, u32[]{:S(2)}) collective-permute-start(bf16[1024,128]{1,0:T(8,128)(2,1)} %rest_0_.1), channel_id=1, source_target_pairs={{0,32},{16,48},{32,64},{48,80},{64,96},{80,112},{96,0},{112,16},{1... | collective-permute-start | bytes 786440 | tf_op jit(solution)/shard_map/ppermute | solution.py:27
  14.3 4.0 %collective-permute-done.3.rest_4_ = bf16[1024,128]{1,0:T(8,128)(2,1)S(1)} collective-permute-done((bf16[1024,128]{1,0:T(8,128)(2,1)}, bf16[1024,128]{1,0:T(8,128)(2,1)S(1)}, u32[]{:S(2)}, u32[]{:S(2)}) %collective-permute-start.3) | collective-permute-done | bytes 262176 | tf_op jit(solution)/shard_map/ppermute | solution.py:27
  18.3 2.3 %collective-permute-start.4 = (bf16[1024,128]{1,0:T(8,128)(2,1)S(1)}, bf16[1024,128]{1,0:T(8,128)(2,1)S(1)}, u32[]{:S(2)}, u32[]{:S(2)}) collective-permute-start(bf16[1024,128]{1,0:T(8,128)(2,1)S(1)} %collective-permute-done.3.rest_4_), channel_id=1, source_target_pairs={{0,16},{16,0},{32,48},{48,32},{64,80},{80,64},{96,112},{112,96},{1... | collective-permute-start | bytes 786440 | tf_op jit(solution)/shard_map/ppermute | solution.py:27
  21.5 2.4 %collective-permute-start.2 = (bf16[1024,128]{1,0:T(8,128)(2,1)S(1)}, bf16[1024,128]{1,0:T(8,128)(2,1)S(1)}, u32[]{:S(2)}, u32[]{:S(2)}) collective-permute-start(bf16[1024,128]{1,0:T(8,128)(2,1)S(1)} %collective-permute-done.rest_1_), channel_id=1, source_target_pairs={{0,32},{16,48},{32,64},{48,80},{64,96},{80,112},{96,0},{112,16},{1... | collective-permute-start | bytes 786440 | tf_op jit(solution)/shard_map/ppermute | solution.py:27
  25.9 5.7 %collective-permute-done.4.rest_5_ = bf16[1024,128]{1,0:T(8,128)(2,1)S(1)} collective-permute-done((bf16[1024,128]{1,0:T(8,128)(2,1)S(1)}, bf16[1024,128]{1,0:T(8,128)(2,1)S(1)}, u32[]{:S(2)}, u32[]{:S(2)}) %collective-permute-start.4) | collective-permute-done | bytes 262176 | tf_op jit(solution)/shard_map/ppermute | solution.py:27
  32.6 8.1 %direct_sums.2 = (bf16[1024,128]{1,0:T(8,128)(2,1)S(1)}, bf16[1024,128]{1,0:T(8,128)(2,1)S(1)}, bf16[2048,128]{1,0:T(8,128)(2,1)S(1)}, bf16[1024,128]{1,0:T(8,12...) custom-call(s32[160]{0:T(256)S(1)} %get-tuple-element.67.out_slot, ...), custom_call_target="tpu_custom_call" | custom-call | flops 2684354560 | bytes 20971520 | tf_op jit(solution)/shard_map/direct_sums/pallas_call | solution.py:99
  40.7 4.4 %collective-permute-done.7 = bf16[8192,128]{1,0:T(8,128)(2,1)S(1)} collective-permute-done((bf16[8192,128]{1,0:T(8,128)(2,1)}, bf16[8192,128]{1,0:T(8,128)(2,1)S(1)}, u32[]{:S(2)}, u32[]{:S(2)}) %collective-permute-start.7) | collective-permute-done | bytes 2097184 | tf_op jit(solution)/shard_map/ppermute | solution.py:38
  46.4 6.4 %collective-permute-start.9 = (bf16[2048,128]{1,0:T(8,128)(2,1)S(1)}, bf16[2048,128]{1,0:T(8,128)(2,1)S(1)}, u32[]{:S(2)}, u32[]{:S(2)}) collective-permute-start(bf16[2048,128]{1,0:T(8,128)(2,1)S(1)} %get-tuple-element.64), channel_id=1, source_target_pairs={{0,12},{1,13},{2,14},{3,15},{4,0},{5,1},{6,2},{7,3},{8,4},{9,5},{1... | collective-permute-start | bytes 1572872 | tf_op jit(solution)/shard_map/ppermute | solution.py:38
  53.1 9.0 %mirror_sums.2 = (bf16[1024,128]{1,0:T(8,128)(2,1)}, bf16[1024,128]{1,0:T(8,128)(2,1)}, bf16[2048,128]{1,0:T(8,128)(2,1)}, bf16[1024,128]{1,0:T(8,128)(2,1)}, bf...) custom-call(s32[160]{0:T(256)} %get-tuple-element.69.out_slot, s32[160]{0:T(256)} %get-tuple-element.68.in_slot, ...), custom_call_target="tpu_custom_call" | custom-call | flops 2684354560 | bytes 20971520 | tf_op jit(solution)/shard_map/mirror_sums/pallas_call | solution.py:99
  64.2 5.8 %collective-permute-start.15 = (bf16[1024,128]{1,0:T(8,128)(2,1)}, bf16[1024,128]{1,0:T(8,128)(2,1)S(1)}, u32[]{:S(2)}, u32[]{:S(2)}) collective-permute-start(bf16[1024,128]{1,0:T(8,128)(2,1)} %get-tuple-element.42), channel_id=1, source_target_pairs={{0,16},{16,0},{32,48},{48,32},{64,80},{80,64},{96,112},{112,96},{1... | collective-permute-start | bytes 786440 | tf_op jit(solution)/shard_map/ppermute | solution.py:27
  72.1 3.2 %collective-permute-start.12 = (bf16[1024,128]{1,0:T(8,128)(2,1)S(1)}, bf16[1024,128]{1,0:T(8,128)(2,1)S(1)}, u32[]{:S(2)}, u32[]{:S(2)}) collective-permute-start(bf16[1024,128]{1,0:T(8,128)(2,1)S(1)} %get-tuple-element.62), channel_id=1, source_target_pairs={{0,2},{1,3},{2,0},{3,1},{4,6},{5,7},{6,4},{7,5},{8,10},{9,11},{10,... | collective-permute-start | bytes 786440 | tf_op jit(solution)/shard_map/ppermute | solution.py:38
  78.7 11.0 %collective-permute-start.17 = (bf16[1024,128]{1,0:T(8,128)(2,1)S(1)}, bf16[1024,128]{1,0:T(8,128)(2,1)S(1)}, u32[]{:S(2)}, u32[]{:S(2)}) collective-permute-start(bf16[1024,128]{1,0:T(8,128)(2,1)S(1)} %add_convert_fusion.9), channel_id=1, source_target_pairs={{0,16},{16,0},{32,48},{48,32},{64,80},{80,64},{96,112},{112,96},{1... | collective-permute-start | bytes 786440 | tf_op jit(solution)/shard_map/ppermute | solution.py:27
  89.6 4.3 %collective-permute-done.17 = bf16[1024,128]{1,0:T(8,128)(2,1)S(1)} collective-permute-done((bf16[1024,128]{1,0:T(8,128)(2,1)S(1)}, bf16[1024,128]{1,0:T(8,128)(2,1)S(1)}, u32[]{:S(2)}, u32[]{:S(2)}) %collective-permute-start.17) | collective-permute-done | bytes 262176 | tf_op jit(solution)/shard_map/ppermute | solution.py:27
  94.0 2.1 %fusion.2.rest_0_ = bf16[1024,128]{1,0:T(8,128)(2,1)} fusion(bf16[1024,128]{1,0:T(8,128)(2,1)S(1)} %copy-done.1, bf16[1024,128]{1,0:T(8,128)(2,1)S(1)} %collective-permute-done.17, bf16[1024,128]{1,0:T(8,128)(2,1)S(1)} %collective-permute-done.16, bf16[1024,128]{1,0:T(8,128)(2,1)S(1)} %copy-done.9, bf16[1024,128]{1,0:T(8,128)(2,1)S(1)} %collective-permute-done.12, ...), kind=kLoop, calls=%fused_computation.8 | loop fusion | flops 3407872 | bytes 3407872 | tf_op jit(solution)/shard_map/convert_element_type | solution.py:187
  96.2 3.6 %collective-permute-start.18 = (bf16[1024,128]{1,0:T(8,128)(2,1)}, bf16[1024,128]{1,0:T(8,128)(2,1)S(1)}, u32[]{:S(2)}, u32[]{:S(2)}) collective-permute-start(bf16[1024,128]{1,0:T(8,128)(2,1)} %fusion.2.rest_0_), channel_id=1, source_target_pairs={{0,16},{16,0},{32,48},{48,32},{64,80},{80,64},{96,112},{112,96},{1... | collective-permute-start | bytes 786440 | tf_op jit(solution)/shard_map/ppermute | solution.py:27
  100.3 2.8 %collective-permute-start.19 = (bf16[1024,128]{1,0:T(8,128)(2,1)}, bf16[1024,128]{1,0:T(8,128)(2,1)S(1)}, u32[]{:S(2)}, u32[]{:S(2)}) collective-permute-start(bf16[1024,128]{1,0:T(8,128)(2,1)} %fusion.2.rest_0_), channel_id=1, source_target_pairs={{0,32},{16,48},{32,64},{48,80},{64,96},{80,112},{96,0},{112,16},{1... | collective-permute-start | bytes 786440 | tf_op jit(solution)/shard_map/ppermute | solution.py:27
  103.0 3.2 %collective-permute-done.21.rest_4_ = bf16[1024,128]{1,0:T(8,128)(2,1)S(1)} collective-permute-done((bf16[1024,128]{1,0:T(8,128)(2,1)}, bf16[1024,128]{1,0:T(8,128)(2,1)S(1)}, u32[]{:S(2)}, u32[]{:S(2)}) %collective-permute-start.21) | collective-permute-done | bytes 262176 | tf_op jit(solution)/shard_map/ppermute | solution.py:27
  106.2 4.4 %collective-permute-start.22 = (bf16[1024,128]{1,0:T(8,128)(2,1)S(1)}, bf16[1024,128]{1,0:T(8,128)(2,1)S(1)}, u32[]{:S(2)}, u32[]{:S(2)}) collective-permute-start(bf16[1024,128]{1,0:T(8,128)(2,1)S(1)} %collective-permute-done.21.rest_4_), channel_id=1, source_target_pairs={{0,16},{16,0},{32,48},{48,32},{64,80},{80,64},{96,112},{112,96},{1... | collective-permute-start | bytes 786440 | tf_op jit(solution)/shard_map/ppermute | solution.py:27
  110.6 3.2 %collective-permute-start.20 = (bf16[1024,128]{1,0:T(8,128)(2,1)S(1)}, bf16[1024,128]{1,0:T(8,128)(2,1)S(1)}, u32[]{:S(2)}, u32[]{:S(2)}) collective-permute-start(bf16[1024,128]{1,0:T(8,128)(2,1)S(1)} %collective-permute-done.18.rest_1_), channel_id=1, source_target_pairs={{0,32},{16,48},{32,64},{48,80},{64,96},{80,112},{96,0},{112,16},{1... | collective-permute-start | bytes 786440 | tf_op jit(solution)/shard_map/ppermute | solution.py:27
  113.9 6.3 %collective-permute-done.22.rest_5_ = bf16[1024,128]{1,0:T(8,128)(2,1)S(1)} collective-permute-done((bf16[1024,128]{1,0:T(8,128)(2,1)S(1)}, bf16[1024,128]{1,0:T(8,128)(2,1)S(1)}, u32[]{:S(2)}, u32[]{:S(2)}) %collective-permute-start.22) | collective-permute-done | bytes 262176 | tf_op jit(solution)/shard_map/ppermute | solution.py:27
  121.1 8.1 %direct_sums.3 = (bf16[1024,128]{1,0:T(8,128)(2,1)S(1)}, bf16[1024,128]{1,0:T(8,128)(2,1)S(1)}, bf16[2048,128]{1,0:T(8,128)(2,1)S(1)}, bf16[1024,128]{1,0:T(8,12...) custom-call(s32[160]{0:T(256)S(1)} %get-tuple-element.67.out_slot, ...), custom_call_target="tpu_custom_call" | custom-call | flops 2684354560 | bytes 20971520 | tf_op jit(solution)/shard_map/direct_sums/pallas_call | solution.py:99
  129.3 4.4 %collective-permute-done.25 = bf16[8192,128]{1,0:T(8,128)(2,1)S(1)} collective-permute-done((bf16[8192,128]{1,0:T(8,128)(2,1)}, bf16[8192,128]{1,0:T(8,128)(2,1)S(1)}, u32[]{:S(2)}, u32[]{:S(2)}) %collective-permute-start.25) | collective-permute-done | bytes 2097184 | tf_op jit(solution)/shard_map/ppermute | solution.py:38
  134.9 3.2 %collective-permute-start.27 = (bf16[2048,128]{1,0:T(8,128)(2,1)}, bf16[2048,128]{1,0:T(8,128)(2,1)}, u32[]{:S(2)}, u32[]{:S(2)}) collective-permute-start(bf16[2048,128]{1,0:T(8,128)(2,1)} %get-tuple-element.60), channel_id=1, source_target_pairs={{0,12},{1,13},{2,14},{3,15},{4,0},{5,1},{6,2},{7,3},{8,4},{9,5},{1... | collective-permute-start | bytes 1572872 | tf_op jit(solution)/shard_map/ppermute | solution.py:38
  139.0 9.0 %mirror_sums.3 = (bf16[1024,128]{1,0:T(8,128)(2,1)}, bf16[1024,128]{1,0:T(8,128)(2,1)}, bf16[2048,128]{1,0:T(8,128)(2,1)}, bf16[1024,128]{1,0:T(8,128)(2,1)}, bf...) custom-call(s32[160]{0:T(256)} %get-tuple-element.69.out_slot, s32[160]{0:T(256)} %get-tuple-element.68.in_slot, ...), custom_call_target="tpu_custom_call" | custom-call | flops 2684354560 | bytes 20971520 | tf_op jit(solution)/shard_map/mirror_sums/pallas_call | solution.py:99
  150.1 4.1 %collective-permute-start.33 = (bf16[1024,128]{1,0:T(8,128)(2,1)}, bf16[1024,128]{1,0:T(8,128)(2,1)S(1)}, u32[]{:S(2)}, u32[]{:S(2)}) collective-permute-start(bf16[1024,128]{1,0:T(8,128)(2,1)} %get-tuple-element.55), channel_id=1, source_target_pairs={{0,16},{16,0},{32,48},{48,32},{64,80},{80,64},{96,112},{112,96},{1... | collective-permute-start | bytes 786440 | tf_op jit(solution)/shard_map/ppermute | solution.py:27
  156.2 3.1 %collective-permute-start.30 = (bf16[1024,128]{1,0:T(8,128)(2,1)S(1)}, bf16[1024,128]{1,0:T(8,128)(2,1)S(1)}, u32[]{:S(2)}, u32[]{:S(2)}) collective-permute-start(bf16[1024,128]{1,0:T(8,128)(2,1)S(1)} %get-tuple-element.58), channel_id=1, source_target_pairs={{0,2},{1,3},{2,0},{3,1},{4,6},{5,7},{6,4},{7,5},{8,10},{9,11},{10,... | collective-permute-start | bytes 786440 | tf_op jit(solution)/shard_map/ppermute | solution.py:38
  161.6 3.0 %collective-permute-start.34 = (bf16[1024,128]{1,0:T(8,128)(2,1)S(1)}, bf16[1024,128]{1,0:T(8,128)(2,1)S(1)}, u32[]{:S(2)}, u32[]{:S(2)}) collective-permute-start(bf16[1024,128]{1,0:T(8,128)(2,1)S(1)} %add_convert_fusion.5), channel_id=1, source_target_pairs={{0,64},{16,80},{32,96},{48,112},{64,0},{80,16},{96,32},{112,48},{1... | collective-permute-start | bytes 786440 | tf_op jit(solution)/shard_map/ppermute | solution.py:27
  164.6 6.1 %collective-permute-done.32 = bf16[2048,128]{1,0:T(8,128)(2,1)S(1)} collective-permute-done((bf16[2048,128]{1,0:T(8,128)(2,1)}, bf16[2048,128]{1,0:T(8,128)(2,1)S(1)}, u32[]{:S(2)}, u32[]{:S(2)}) %collective-permute-start.32) | collective-permute-done | bytes 524320 | tf_op jit(solution)/shard_map/ppermute | solution.py:27
  170.8 3.2 %collective-permute-start.35 = (bf16[1024,128]{1,0:T(8,128)(2,1)S(1)}, bf16[1024,128]{1,0:T(8,128)(2,1)S(1)}, u32[]{:S(2)}, u32[]{:S(2)}) collective-permute-start(bf16[1024,128]{1,0:T(8,128)(2,1)S(1)} %add_convert_fusion.4), channel_id=1, source_target_pairs={{0,16},{16,0},{32,48},{48,32},{64,80},{80,64},{96,112},{112,96},{1... | collective-permute-start | bytes 786440 | tf_op jit(solution)/shard_map/ppermute | solution.py:27
  174.0 4.8 %collective-permute-done.35 = bf16[1024,128]{1,0:T(8,128)(2,1)S(1)} collective-permute-done((bf16[1024,128]{1,0:T(8,128)(2,1)S(1)}, bf16[1024,128]{1,0:T(8,128)(2,1)S(1)}, u32[]{:S(2)}, u32[]{:S(2)}) %collective-permute-start.35) | collective-permute-done | bytes 262176 | tf_op jit(solution)/shard_map/ppermute | solution.py:27
  178.8 2.3 %convert_subtract_fusion = f32[1024,128]{1,0:T(8,128)} fusion(bf16[1024,128]{1,0:T(8,128)(2,1)S(1)} %copy-done.1, bf16[1024,128]{1,0:T(8,128)(2,1)S(1)} %copy-done.3, bf16[1024,128]{1,0:T(8,128)(2,1)S(1)} %collective-permute-done.35, bf16[1024,128]{1,0:T(8,128)(2,1)S(1)} %collective-permute-done.34, bf16[1024,128]{1,0:T(8,128)(2,1)S(1)} %copy-done.10, ...), kind=kLoop, calls=%fused_computation.4 | loop fusion | flops 3538944 | bytes 3932160 | tf_op jit(solution)/shard_map/sub | solution.py:189
  (85 shorter events, 24.7 us)
Async XLA Ops:
  6.5 46.5 %all-gather.3.cloned.1.call-start = ((), (), s32[]{:S(2)}) async-start(), calls=%async_computation | async-start | bytes 4456448 | tf_op jit(solution)/shard_map/all_gather | solution.py:131
  7.3 131.7 %all-gather.5.cloned.1.call-start = ((), (), s32[]{:S(2)}) async-start(), calls=%async_computation.1 | async-start | bytes 4456448 | tf_op jit(solution)/shard_map/all_gather | solution.py:131
  7.3 11.0 %collective-permute-start.3 = (bf16[1024,128]{1,0:T(8,128)(2,1)}, bf16[1024,128]{1,0:T(8,128)(2,1)S(1)}, u32[]{:S(2)}, u32[]{:S(2)}) collective-permute-start(bf16[1024,128]{1,0:T(8,128)(2,1)} %rest_0_.1), channel_id=1, source_target_pairs={{0,64},{16,80},{32,96},{48,112},{64,0},{80,16},{96,32},{112,48},{1... | collective-permute-start | bytes 786440 | tf_op jit(solution)/shard_map/ppermute | solution.py:27
  8.8 11.8 %collective-permute-start = (bf16[1024,128]{1,0:T(8,128)(2,1)}, bf16[1024,128]{1,0:T(8,128)(2,1)S(1)}, u32[]{:S(2)}, u32[]{:S(2)}) collective-permute-start(bf16[1024,128]{1,0:T(8,128)(2,1)} %rest_0_.1), channel_id=1, source_target_pairs={{0,16},{16,0},{32,48},{48,32},{64,80},{80,64},{96,112},{112,96},{1... | collective-permute-start | bytes 786440 | tf_op jit(solution)/shard_map/ppermute | solution.py:27
  11.1 14.8 %collective-permute-start.5 = (bf16[1024,128]{1,0:T(8,128)(2,1)}, bf16[1024,128]{1,0:T(8,128)(2,1)S(1)}, u32[]{:S(2)}, u32[]{:S(2)}) collective-permute-start(bf16[1024,128]{1,0:T(8,128)(2,1)} %rest_0_.1), channel_id=1, source_target_pairs={{0,96},{16,112},{32,0},{48,16},{64,32},{80,48},{96,64},{112,80},{1... | collective-permute-start | bytes 786440 | tf_op jit(solution)/shard_map/ppermute | solution.py:27
  11.1 14.8 %collective-permute-start.1 = (bf16[1024,128]{1,0:T(8,128)(2,1)}, bf16[1024,128]{1,0:T(8,128)(2,1)S(1)}, u32[]{:S(2)}, u32[]{:S(2)}) collective-permute-start(bf16[1024,128]{1,0:T(8,128)(2,1)} %rest_0_.1), channel_id=1, source_target_pairs={{0,32},{16,48},{32,64},{48,80},{64,96},{80,112},{96,0},{112,16},{1... | collective-permute-start | bytes 786440 | tf_op jit(solution)/shard_map/ppermute | solution.py:27
  18.3 13.3 %collective-permute-start.4 = (bf16[1024,128]{1,0:T(8,128)(2,1)S(1)}, bf16[1024,128]{1,0:T(8,128)(2,1)S(1)}, u32[]{:S(2)}, u32[]{:S(2)}) collective-permute-start(bf16[1024,128]{1,0:T(8,128)(2,1)S(1)} %collective-permute-done.3.rest_4_), channel_id=1, source_target_pairs={{0,16},{16,0},{32,48},{48,32},{64,80},{80,64},{96,112},{112,96},{1... | collective-permute-start | bytes 786440 | tf_op jit(solution)/shard_map/ppermute | solution.py:27
  20.6 11.0 %collective-permute-start.6 = (bf16[1024,128]{1,0:T(8,128)(2,1)S(1)}, bf16[1024,128]{1,0:T(8,128)(2,1)S(1)}, u32[]{:S(2)}, u32[]{:S(2)}) collective-permute-start(bf16[1024,128]{1,0:T(8,128)(2,1)S(1)} %collective-permute-done.rest_1_), channel_id=1, source_target_pairs={{0,96},{16,112},{32,0},{48,16},{64,32},{80,48},{96,64},{112,80},{1... | collective-permute-start | bytes 786440 | tf_op jit(solution)/shard_map/ppermute | solution.py:27
  21.5 10.1 %collective-permute-start.2 = (bf16[1024,128]{1,0:T(8,128)(2,1)S(1)}, bf16[1024,128]{1,0:T(8,128)(2,1)S(1)}, u32[]{:S(2)}, u32[]{:S(2)}) collective-permute-start(bf16[1024,128]{1,0:T(8,128)(2,1)S(1)} %collective-permute-done.rest_1_), channel_id=1, source_target_pairs={{0,32},{16,48},{32,64},{48,80},{64,96},{80,112},{96,0},{112,16},{1... | collective-permute-start | bytes 786440 | tf_op jit(solution)/shard_map/ppermute | solution.py:27
  46.4 23.6 %collective-permute-start.8 = (bf16[2048,128]{1,0:T(8,128)(2,1)}, bf16[2048,128]{1,0:T(8,128)(2,1)S(1)}, u32[]{:S(2)}, u32[]{:S(2)}) collective-permute-start(bf16[2048,128]{1,0:T(8,128)(2,1)} %get-tuple-element.63), channel_id=1, source_target_pairs={{0,4},{1,5},{2,6},{3,7},{4,8},{5,9},{6,10},{7,11},{8,12},{9,13},{1... | collective-permute-start | bytes 1572872 | tf_op jit(solution)/shard_map/ppermute | solution.py:38
  46.4 23.6 %collective-permute-start.9 = (bf16[2048,128]{1,0:T(8,128)(2,1)S(1)}, bf16[2048,128]{1,0:T(8,128)(2,1)S(1)}, u32[]{:S(2)}, u32[]{:S(2)}) collective-permute-start(bf16[2048,128]{1,0:T(8,128)(2,1)S(1)} %get-tuple-element.64), channel_id=1, source_target_pairs={{0,12},{1,13},{2,14},{3,15},{4,0},{5,1},{6,2},{7,3},{8,4},{9,5},{1... | collective-permute-start | bytes 1572872 | tf_op jit(solution)/shard_map/ppermute | solution.py:38
  52.9 11.3 %collective-permute-start.10 = (bf16[1024,128]{1,0:T(8,128)(2,1)S(1)}, bf16[1024,128]{1,0:T(8,128)(2,1)S(1)}, u32[]{:S(2)}, u32[]{:S(2)}) collective-permute-start(bf16[1024,128]{1,0:T(8,128)(2,1)S(1)} %add_convert_fusion.13), channel_id=1, source_target_pairs={{0,2},{1,3},{2,0},{3,1},{4,6},{5,7},{6,4},{7,5},{8,10},{9,11},{10,... | collective-permute-start | bytes 786440 | tf_op jit(solution)/shard_map/ppermute | solution.py:38
  62.1 16.4 %collective-permute-start.13 = (bf16[2048,128]{1,0:T(8,128)(2,1)}, bf16[2048,128]{1,0:T(8,128)(2,1)S(1)}, u32[]{:S(2)}, u32[]{:S(2)}) collective-permute-start(bf16[2048,128]{1,0:T(8,128)(2,1)} %get-tuple-element.39), channel_id=1, source_target_pairs={{0,32},{16,48},{32,64},{48,80},{64,96},{80,112},{96,0},{112,16},{1... | collective-permute-start | bytes 1572872 | tf_op jit(solution)/shard_map/ppermute | solution.py:27
  62.2 16.4 %collective-permute-start.14 = (bf16[2048,128]{1,0:T(8,128)(2,1)}, bf16[2048,128]{1,0:T(8,128)(2,1)S(1)}, u32[]{:S(2)}, u32[]{:S(2)}) collective-permute-start(bf16[2048,128]{1,0:T(8,128)(2,1)} %get-tuple-element.40), channel_id=1, source_target_pairs={{0,96},{16,112},{32,0},{48,16},{64,32},{80,48},{96,64},{112,80},{1... | collective-permute-start | bytes 1572872 | tf_op jit(solution)/shard_map/ppermute | solution.py:27
  64.2 13.0 %collective-permute-start.15 = (bf16[1024,128]{1,0:T(8,128)(2,1)}, bf16[1024,128]{1,0:T(8,128)(2,1)S(1)}, u32[]{:S(2)}, u32[]{:S(2)}) collective-permute-start(bf16[1024,128]{1,0:T(8,128)(2,1)} %get-tuple-element.42), channel_id=1, source_target_pairs={{0,16},{16,0},{32,48},{48,32},{64,80},{80,64},{96,112},{112,96},{1... | collective-permute-start | bytes 786440 | tf_op jit(solution)/shard_map/ppermute | solution.py:27
  71.4 18.3 %collective-permute-start.11 = (bf16[1024,128]{1,0:T(8,128)(2,1)S(1)}, bf16[1024,128]{1,0:T(8,128)(2,1)S(1)}, u32[]{:S(2)}, u32[]{:S(2)}) collective-permute-start(bf16[1024,128]{1,0:T(8,128)(2,1)S(1)} %get-tuple-element.61), channel_id=1, source_target_pairs={{0,8},{1,9},{2,10},{3,11},{4,12},{5,13},{6,14},{7,15},{8,0},{9,1},... | collective-permute-start | bytes 786440 | tf_op jit(solution)/shard_map/ppermute | solution.py:38
  72.1 17.5 %collective-permute-start.12 = (bf16[1024,128]{1,0:T(8,128)(2,1)S(1)}, bf16[1024,128]{1,0:T(8,128)(2,1)S(1)}, u32[]{:S(2)}, u32[]{:S(2)}) collective-permute-start(bf16[1024,128]{1,0:T(8,128)(2,1)S(1)} %get-tuple-element.62), channel_id=1, source_target_pairs={{0,2},{1,3},{2,0},{3,1},{4,6},{5,7},{6,4},{7,5},{8,10},{9,11},{10,... | collective-permute-start | bytes 786440 | tf_op jit(solution)/shard_map/ppermute | solution.py:38
  77.3 12.3 %collective-permute-start.16 = (bf16[1024,128]{1,0:T(8,128)(2,1)S(1)}, bf16[1024,128]{1,0:T(8,128)(2,1)S(1)}, u32[]{:S(2)}, u32[]{:S(2)}) collective-permute-start(bf16[1024,128]{1,0:T(8,128)(2,1)S(1)} %add_convert_fusion.10), channel_id=1, source_target_pairs={{0,64},{16,80},{32,96},{48,112},{64,0},{80,16},{96,32},{112,48},{1... | collective-permute-start | bytes 786440 | tf_op jit(solution)/shard_map/ppermute | solution.py:27
  78.7 15.3 %collective-permute-start.17 = (bf16[1024,128]{1,0:T(8,128)(2,1)S(1)}, bf16[1024,128]{1,0:T(8,128)(2,1)S(1)}, u32[]{:S(2)}, u32[]{:S(2)}) collective-permute-start(bf16[1024,128]{1,0:T(8,128)(2,1)S(1)} %add_convert_fusion.9), channel_id=1, source_target_pairs={{0,16},{16,0},{32,48},{48,32},{64,80},{80,64},{96,112},{112,96},{1... | collective-permute-start | bytes 786440 | tf_op jit(solution)/shard_map/ppermute | solution.py:27
  96.2 14.4 %collective-permute-start.18 = (bf16[1024,128]{1,0:T(8,128)(2,1)}, bf16[1024,128]{1,0:T(8,128)(2,1)S(1)}, u32[]{:S(2)}, u32[]{:S(2)}) collective-permute-start(bf16[1024,128]{1,0:T(8,128)(2,1)} %fusion.2.rest_0_), channel_id=1, source_target_pairs={{0,16},{16,0},{32,48},{48,32},{64,80},{80,64},{96,112},{112,96},{1... | collective-permute-start | bytes 786440 | tf_op jit(solution)/shard_map/ppermute | solution.py:27
  99.8 14.1 %collective-permute-start.23 = (bf16[1024,128]{1,0:T(8,128)(2,1)}, bf16[1024,128]{1,0:T(8,128)(2,1)S(1)}, u32[]{:S(2)}, u32[]{:S(2)}) collective-permute-start(bf16[1024,128]{1,0:T(8,128)(2,1)} %fusion.2.rest_0_), channel_id=1, source_target_pairs={{0,96},{16,112},{32,0},{48,16},{64,32},{80,48},{96,64},{112,80},{1... | collective-permute-start | bytes 786440 | tf_op jit(solution)/shard_map/ppermute | solution.py:27
  100.3 13.6 %collective-permute-start.19 = (bf16[1024,128]{1,0:T(8,128)(2,1)}, bf16[1024,128]{1,0:T(8,128)(2,1)S(1)}, u32[]{:S(2)}, u32[]{:S(2)}) collective-permute-start(bf16[1024,128]{1,0:T(8,128)(2,1)} %fusion.2.rest_0_), channel_id=1, source_target_pairs={{0,32},{16,48},{32,64},{48,80},{64,96},{80,112},{96,0},{112,16},{1... | collective-permute-start | bytes 786440 | tf_op jit(solution)/shard_map/ppermute | solution.py:27
  106.2 13.9 %collective-permute-start.22 = (bf16[1024,128]{1,0:T(8,128)(2,1)S(1)}, bf16[1024,128]{1,0:T(8,128)(2,1)S(1)}, u32[]{:S(2)}, u32[]{:S(2)}) collective-permute-start(bf16[1024,128]{1,0:T(8,128)(2,1)S(1)} %collective-permute-done.21.rest_4_), channel_id=1, source_target_pairs={{0,16},{16,0},{32,48},{48,32},{64,80},{80,64},{96,112},{112,96},{1... | collective-permute-start | bytes 786440 | tf_op jit(solution)/shard_map/ppermute | solution.py:27
  134.9 19.2 %collective-permute-start.26 = (bf16[2048,128]{1,0:T(8,128)(2,1)}, bf16[2048,128]{1,0:T(8,128)(2,1)}, u32[]{:S(2)}, u32[]{:S(2)}) collective-permute-start(bf16[2048,128]{1,0:T(8,128)(2,1)} %get-tuple-element.59), channel_id=1, source_target_pairs={{0,4},{1,5},{2,6},{3,7},{4,8},{5,9},{6,10},{7,11},{8,12},{9,13},{1... | collective-permute-start | bytes 1572872 | tf_op jit(solution)/shard_map/ppermute | solution.py:38
  134.9 19.2 %collective-permute-start.27 = (bf16[2048,128]{1,0:T(8,128)(2,1)}, bf16[2048,128]{1,0:T(8,128)(2,1)}, u32[]{:S(2)}, u32[]{:S(2)}) collective-permute-start(bf16[2048,128]{1,0:T(8,128)(2,1)} %get-tuple-element.60), channel_id=1, source_target_pairs={{0,12},{1,13},{2,14},{3,15},{4,0},{5,1},{6,2},{7,3},{8,4},{9,5},{1... | collective-permute-start | bytes 1572872 | tf_op jit(solution)/shard_map/ppermute | solution.py:38
  139.0 11.1 %collective-permute-start.28 = (bf16[1024,128]{1,0:T(8,128)(2,1)}, bf16[1024,128]{1,0:T(8,128)(2,1)S(1)}, u32[]{:S(2)}, u32[]{:S(2)}) collective-permute-start(bf16[1024,128]{1,0:T(8,128)(2,1)} %add_convert_fusion.8), channel_id=1, source_target_pairs={{0,2},{1,3},{2,0},{3,1},{4,6},{5,7},{6,4},{7,5},{8,10},{9,11},{10,... | collective-permute-start | bytes 786440 | tf_op jit(solution)/shard_map/ppermute | solution.py:38
  148.0 16.6 %collective-permute-start.31 = (bf16[2048,128]{1,0:T(8,128)(2,1)}, bf16[2048,128]{1,0:T(8,128)(2,1)S(1)}, u32[]{:S(2)}, u32[]{:S(2)}) collective-permute-start(bf16[2048,128]{1,0:T(8,128)(2,1)} %get-tuple-element.52), channel_id=1, source_target_pairs={{0,32},{16,48},{32,64},{48,80},{64,96},{80,112},{96,0},{112,16},{1... | collective-permute-start | bytes 1572872 | tf_op jit(solution)/shard_map/ppermute | solution.py:27
  148.1 22.6 %collective-permute-start.32 = (bf16[2048,128]{1,0:T(8,128)(2,1)}, bf16[2048,128]{1,0:T(8,128)(2,1)S(1)}, u32[]{:S(2)}, u32[]{:S(2)}) collective-permute-start(bf16[2048,128]{1,0:T(8,128)(2,1)} %get-tuple-element.53), channel_id=1, source_target_pairs={{0,96},{16,112},{32,0},{48,16},{64,32},{80,48},{96,64},{112,80},{1... | collective-permute-start | bytes 1572872 | tf_op jit(solution)/shard_map/ppermute | solution.py:27
  150.1 11.4 %collective-permute-start.33 = (bf16[1024,128]{1,0:T(8,128)(2,1)}, bf16[1024,128]{1,0:T(8,128)(2,1)S(1)}, u32[]{:S(2)}, u32[]{:S(2)}) collective-permute-start(bf16[1024,128]{1,0:T(8,128)(2,1)} %get-tuple-element.55), channel_id=1, source_target_pairs={{0,16},{16,0},{32,48},{48,32},{64,80},{80,64},{96,112},{112,96},{1... | collective-permute-start | bytes 786440 | tf_op jit(solution)/shard_map/ppermute | solution.py:27
  155.5 18.5 %collective-permute-start.29 = (bf16[1024,128]{1,0:T(8,128)(2,1)S(1)}, bf16[1024,128]{1,0:T(8,128)(2,1)S(1)}, u32[]{:S(2)}, u32[]{:S(2)}) collective-permute-start(bf16[1024,128]{1,0:T(8,128)(2,1)S(1)} %get-tuple-element.57), channel_id=1, source_target_pairs={{0,8},{1,9},{2,10},{3,11},{4,12},{5,13},{6,14},{7,15},{8,0},{9,1},... | collective-permute-start | bytes 786440 | tf_op jit(solution)/shard_map/ppermute | solution.py:38
  156.2 17.7 %collective-permute-start.30 = (bf16[1024,128]{1,0:T(8,128)(2,1)S(1)}, bf16[1024,128]{1,0:T(8,128)(2,1)S(1)}, u32[]{:S(2)}, u32[]{:S(2)}) collective-permute-start(bf16[1024,128]{1,0:T(8,128)(2,1)S(1)} %get-tuple-element.58), channel_id=1, source_target_pairs={{0,2},{1,3},{2,0},{3,1},{4,6},{5,7},{6,4},{7,5},{8,10},{9,11},{10,... | collective-permute-start | bytes 786440 | tf_op jit(solution)/shard_map/ppermute | solution.py:38
  161.6 12.4 %collective-permute-start.34 = (bf16[1024,128]{1,0:T(8,128)(2,1)S(1)}, bf16[1024,128]{1,0:T(8,128)(2,1)S(1)}, u32[]{:S(2)}, u32[]{:S(2)}) collective-permute-start(bf16[1024,128]{1,0:T(8,128)(2,1)S(1)} %add_convert_fusion.5), channel_id=1, source_target_pairs={{0,64},{16,80},{32,96},{48,112},{64,0},{80,16},{96,32},{112,48},{1... | collective-permute-start | bytes 786440 | tf_op jit(solution)/shard_map/ppermute | solution.py:27
  (17 other events, 220.7 us)
Sparse Core Ops, SparseCore 0:
  9.1 43.9 all-gather.2
  96.2 39.5 all-gather.4

commit v3 on v2

--- a/solution.py
+++ b/solution.py
@@ -38,18 +38,28 @@
     return lax.ppermute(value, "col", pairs)
 
 
-def spmv_kernel(mirror, n_in, n_out, out_slot, in_slot, count, tiles, *rest):
+def spmv_kernel(mirror, n_in, n_out, order, out_slot, in_slot, begin, stop, tiles, *rest):
     v_in = rest[:n_in]
     outs = rest[n_in : n_in + n_out]
     acc, held, ring, in_sems, ring_sems = rest[n_in + n_out :]
     depth = ring.shape[0]
-    steps = (count[0] + CHUNK - 1) // CHUNK
+    slots = tiles.shape[0]
+    unused = acc.shape[0] - 1
+    first, end = begin[0], stop[0]
+    steps = (end - first + CHUNK - 1) // CHUNK
+
+    def place(step, j):
+        return jnp.minimum(first + step * CHUNK + j, slots - 1)
 
     def fetch(step):
         at = lax.rem(step, depth)
-        return pltpu.make_async_copy(
-            tiles.at[pl.ds(step * CHUNK, CHUNK)], ring.at[at], ring_sems.at[at]
-        )
+        if not mirror:
+            whole = tiles.at[pl.ds(step * CHUNK, CHUNK)]
+            pltpu.make_async_copy(whole, ring.at[at], ring_sems.at[at]).start()
+            return
+        for j in range(CHUNK):
+            tile = tiles.at[order[place(step, j)]]
+            pltpu.make_async_copy(tile, ring.at[at, j], ring_sems.at[at]).start()
 
     part = held.shape[0] // n_in
     copies = [
@@ -62,7 +72,7 @@
 
         @pl.when(step < steps)
         def _():
-            fetch(step).start()
+            fetch(step)
 
     acc[...] = jnp.zeros_like(acc)
     for copy in copies:
@@ -72,16 +82,17 @@
     def _(step):
         @pl.when(step + depth - 1 < steps)
         def _():
-            fetch(step + depth - 1).start()
-
-        fetch(step).wait()
+            fetch(step + depth - 1)
+
         at = lax.rem(step, depth)
+        pltpu.make_async_copy(tiles.at[pl.ds(0, CHUNK)], ring.at[at], ring_sems.at[at]).wait()
         for j in range(CHUNK):
-            slot = step * CHUNK + j
+            slot = place(step, j)
+            out = jnp.where(first + step * CHUNK + j < end, out_slot[slot], unused)
             base = pl.multiple_of(in_slot[slot] * BS, BS)
             vec = held[pl.ds(base, BS), :]
             dims = (((0,), (0,)), ((), ())) if mirror else (((1,), (0,)), ((), ()))
-            acc[out_slot[slot]] += lax.dot_general(
+            acc[out] += lax.dot_general(
                 ring[at, j], vec, dims, preferred_element_type=jnp.float32
             )
 
@@ -92,13 +103,13 @@
             at += 1
 
 
-def spmv(mirror, tiles, out_slot, in_slot, count, v_in, out_rows):
+def spmv(mirror, tiles, order, out_slot, in_slot, begin, stop, v_in, out_rows):
     slots = tiles.shape[0]
     n_in, n_out = len(v_in), len(out_rows)
     blocks_out = sum(out_rows) // BS
     return pl.pallas_call(
         functools.partial(spmv_kernel, mirror, n_in, n_out),
-        in_specs=[pl.BlockSpec(memory_space=pltpu.SMEM)] * 3
+        in_specs=[pl.BlockSpec(memory_space=pltpu.SMEM)] * 5
         + [pl.BlockSpec(memory_space=pl.ANY)] * (1 + n_in),
         out_specs=[pl.BlockSpec(memory_space=pltpu.VMEM)] * n_out,
         scratch_shapes=[
@@ -114,7 +125,7 @@
             flops=2 * slots * BS * BS * NV, bytes_accessed=slots * BS * BS * 2, transcendentals=0
         ),
         name="mirror_sums" if mirror else "direct_sums",
-    )(out_slot, in_slot, count, tiles, *v_in)
+    )(order, out_slot, in_slot, begin, stop, tiles, *v_in)
 
 
 def gather_row(field):
@@ -148,17 +159,18 @@
     return own + [up[:rows], down[:rows], far, beside]
 
 
-def apply(field, tiles, slots, count):
-    direct_out, direct_in, mirror_out, mirror_in = slots
+def apply(field, tiles, direct, mirror, first, rest):
     rows = OWN * BS
     split = [rows, rows, 2 * rows, rows, rows, 2 * rows]
     row_parts = gather_row(field)
     col_parts = gather_col(field)
-    *mine, other = spmv(False, tiles, direct_out, direct_in, count, row_parts, split + [8 * rows])
+    *mine, other = spmv(False, tiles, *direct, row_parts, split + [8 * rows])
     theirs = jnp.split(send_col(other, (0, 0), 1), [rows, 2 * rows, 4 * rows, 5 * rows, 6 * rows])
-    mirrored = spmv(True, tiles, mirror_out, mirror_in, count, col_parts, split)
+    early = spmv(True, tiles, *mirror, *first, col_parts, [2 * rows, 2 * rows, rows])
+    rest, up, down, far_beside = lax.optimization_barrier((rest, *early))
+    own, beside, far = spmv(True, tiles, *mirror, *rest, col_parts, [rows] * 3)
     parts = scatter(send_col, *([a, b] for a, b in zip(mine, theirs)))
-    parts += scatter(send_row, *([a] for a in mirrored))
+    parts += scatter(send_row, [own], [beside], [up], [far], [far_beside], [down])
     return total(parts)
 
 
@@ -174,18 +186,37 @@
     from_col = tile_rows
     own_c = tile_cols // OWN
     ox, oh = own_c // 2, own_c % 2
-    to_row = ((ox - x) % 4 * 2 + (oh ^ yh)) * OWN + tile_cols % OWN
+    dx = (ox - x) % 4
+    dy = oh ^ yh
+    to_row = jnp.where(dx % 2 == 1, dx // 2 * 2 + dy, jnp.where(dx == 0, dy, 2 + dy * 2))
+    to_row = to_row * OWN + tile_cols % OWN
     from_row = ((x - ox) % 4 * 2 + (oh ^ yh)) * OWN + tile_cols % OWN
-    slots = (
-        jnp.where(live, to_col, 16 * OWN),
-        jnp.where(live, from_row, 0),
-        jnp.where(live, to_row, 8 * OWN),
-        jnp.where(live, from_col, 0),
+    at = jnp.arange(tiles.shape[0], dtype=jnp.int32)
+    early = (dx % 2 == 1) | ((dx == 2) & (dy == 1))
+    group = jnp.where(live, jnp.where(early, 0, 1), 2)
+    ahead = (group[None, :] < group[:, None]) | (
+        (group[None, :] == group[:, None]) & (at[None, :] < at[:, None])
     )
+    place = jnp.sum(ahead.astype(jnp.int32), axis=1)
+    chosen = place[None, :] == at[:, None]
+
+    def ordered(values):
+        return jnp.sum(jnp.where(chosen, values[None, :], 0), axis=1)
+
+    early_count = jnp.sum((group == 0).astype(jnp.int32), keepdims=True)
+    none = jnp.zeros((1,), jnp.int32)
+    direct = (at, jnp.where(live, to_col, 0), jnp.where(live, from_row, 0), none, tile_count)
+    mirror = (
+        ordered(at),
+        ordered(jnp.where(live, to_row, 0)),
+        ordered(jnp.where(live, from_col, 0)),
+    )
+    direct, mirror, early_count = lax.optimization_barrier((direct, mirror, early_count))
+    first, rest = (none, early_count), (early_count, tile_count)
     x_float = vectors.astype(jnp.float32)
-    applied = apply(vectors, tiles, slots, tile_count)
+    applied = apply(vectors, tiles, direct, mirror, first, rest)
     first_term = ((applied - center_value * x_float) / radius_value).astype(jnp.bfloat16)
-    second = apply(first_term, tiles, slots, tile_count)
+    second = apply(first_term, tiles, direct, mirror, first, rest)
     return 2.0 * (second - center_value * first_term.astype(jnp.float32)) / radius_value - x_float
 
 

time: 189 us -> 190 us (level)
  starting transfers between devices: 77.4 us -> 61.7 us
  Pallas kernels: 34.1 us -> 42.6 us
  other arithmetic: 12.2 us -> 18.2 us
    ppermute x24, starting transfers between devices: 59.6 us -> 36.9 us  [send_row(): return lax.ppermute(value, 'row', pairs)]
    pallas_call x4 -> x6, Pallas kernels: 34.1 us -> 42.6 us  [spmv(): pl.pallas_call(functools.partial(spmv_kernel, mirror, n_in, n_out), in_sp...]
    ppermute x12, starting transfers between devices: 17.7 us -> 24.7 us  [send_col(): return lax.ppermute(value, 'col', pairs)]
    convert_element_type x10, other arithmetic: 6.46 us -> 10.2 us  [rounded(): return parts[0] if len(parts) == 1 else total(parts).astype(jnp.bfloat16)]
    reduce_sum x0 -> x3, other arithmetic: none -> 2.3 us  [the longest x1 1.32 us: local(): early_count = jnp.sum((group == 0).astype(jnp.int32), keepdims=True)]
  transfers between devices with their start and end apart: 38 -> 38, of which waited for: 11 -> 13; matrix products, arithmetic and copies ran while one was open for 4% -> 7% of each run, Pallas kernels for 18% -> 23%
where the time goes in v3:
time: 190 us; the launch traced here: 188 us
  starting transfers between devices  61.7 us (32%)
  waiting for transfers between devices  48.8 us (26%)
  Pallas kernels  42.6 us (22%)
  other arithmetic  18.2 us (10%)
  between operations  14.3 us (8%)
  local copies, waits for them, and re-layouts  1.92 us (1%)
    pallas_call x6, Pallas kernels, spmv(): pl.pallas_call(functools.partial(spmv_kernel, mirror, n_in, n_out), in_sp...  42.6 us
    ppermute x24, waiting for transfers between devices, send_row(): return lax.ppermute(value, 'row', pairs)  39.3 us
    ppermute x24, starting transfers between devices, send_row(): return lax.ppermute(value, 'row', pairs)  36.9 us
    ppermute x12, starting transfers between devices, send_col(): return lax.ppermute(value, 'col', pairs)  24.7 us
    convert_element_type x10, other arithmetic, rounded(): return parts[0] if len(parts) == 1 else total(parts).astype(jnp.bfloat16)  10.2 us
    ppermute x12, waiting for transfers between devices, send_col(): return lax.ppermute(value, 'col', pairs)  8.82 us
  transfers between devices with their start and end apart: 38, of which 13 were waited for; matrix products, arithmetic and copies ran while one was open for 7% of the time, Pallas kernels for 23%

profile of v3, /device:TPU:14, one launch (start us, length us, event | category | flops | bytes accessed | tf_op | source)
XLA Modules:
  0.0 187.5 jit_solution(1492439533501039010)
XLA Ops:
  7.3 2.4 %collective-permute-start = (bf16[1024,128]{1,0:T(8,128)(2,1)}, bf16[1024,128]{1,0:T(8,128)(2,1)S(1)}, u32[]{:S(2)}, u32[]{:S(2)}) collective-permute-start(bf16[1024,128]{1,0:T(8,128)(2,1)} %rest_0_.1), channel_id=1, source_target_pairs={{0,16},{16,0},{32,48},{48,32},{64,80},{80,64},{96,112},{112,96},{1... | collective-permute-start | bytes 786440 | tf_op jit(solution)/shard_map/ppermute | solution.py:27
  11.1 3.2 %collective-permute-start.1 = (bf16[1024,128]{1,0:T(8,128)(2,1)}, bf16[1024,128]{1,0:T(8,128)(2,1)S(1)}, u32[]{:S(2)}, u32[]{:S(2)}) collective-permute-start(bf16[1024,128]{1,0:T(8,128)(2,1)} %rest_0_.1), channel_id=1, source_target_pairs={{0,32},{16,48},{32,64},{48,80},{64,96},{80,112},{96,0},{112,16},{1... | collective-permute-start | bytes 786440 | tf_op jit(solution)/shard_map/ppermute | solution.py:27
  18.0 2.4 %collective-permute-start.2 = (bf16[1024,128]{1,0:T(8,128)(2,1)S(1)}, bf16[1024,128]{1,0:T(8,128)(2,1)S(1)}, u32[]{:S(2)}, u32[]{:S(2)}) collective-permute-start(bf16[1024,128]{1,0:T(8,128)(2,1)S(1)} %collective-permute-done.rest_1_), channel_id=1, source_target_pairs={{0,32},{16,48},{32,64},{48,80},{64,96},{80,112},{96,0},{112,16},{1... | collective-permute-start | bytes 786440 | tf_op jit(solution)/shard_map/ppermute | solution.py:27
  20.7 2.0 %collective-permute-start.4 = (bf16[1024,128]{1,0:T(8,128)(2,1)S(1)}, bf16[1024,128]{1,0:T(8,128)(2,1)S(1)}, u32[]{:S(2)}, u32[]{:S(2)}) collective-permute-start(bf16[1024,128]{1,0:T(8,128)(2,1)S(1)} %collective-permute-done.3.rest_4_), channel_id=1, source_target_pairs={{0,16},{16,0},{32,48},{48,32},{64,80},{80,64},{96,112},{112,96},{1... | collective-permute-start | bytes 786440 | tf_op jit(solution)/shard_map/ppermute | solution.py:27
  24.9 11.0 %collective-permute-done.4.rest_5_ = bf16[1024,128]{1,0:T(8,128)(2,1)S(1)} collective-permute-done((bf16[1024,128]{1,0:T(8,128)(2,1)S(1)}, bf16[1024,128]{1,0:T(8,128)(2,1)S(1)}, u32[]{:S(2)}, u32[]{:S(2)}) %collective-permute-start.4) | collective-permute-done | bytes 262176 | tf_op jit(solution)/shard_map/ppermute | solution.py:27
  36.9 7.4 %direct_sums.2 = (bf16[1024,128]{1,0:T(8,128)(2,1)S(1)}, bf16[1024,128]{1,0:T(8,128)(2,1)S(1)}, bf16[2048,128]{1,0:T(8,128)(2,1)S(1)}, bf16[1024,128]{1,0:T(8,12...) custom-call(s32[160]{0:T(256)S(1)} %iota.12.order, ...), custom_call_target="tpu_custom_call" | custom-call | flops 2684354560 | bytes 20971520 | tf_op jit(solution)/shard_map/direct_sums/pallas_call | solution.py:110
  44.3 4.4 %collective-permute-done.7 = bf16[8192,128]{1,0:T(8,128)(2,1)S(1)} collective-permute-done((bf16[8192,128]{1,0:T(8,128)(2,1)}, bf16[8192,128]{1,0:T(8,128)(2,1)S(1)}, u32[]{:S(2)}, u32[]{:S(2)}) %collective-permute-start.7) | collective-permute-done | bytes 2097184 | tf_op jit(solution)/shard_map/ppermute | solution.py:38
  49.1 6.6 %collective-permute-start.9 = (bf16[2048,128]{1,0:T(8,128)(2,1)S(1)}, bf16[2048,128]{1,0:T(8,128)(2,1)S(1)}, u32[]{:S(2)}, u32[]{:S(2)}) collective-permute-start(bf16[2048,128]{1,0:T(8,128)(2,1)S(1)} %get-tuple-element.108), channel_id=1, source_target_pairs={{0,12},{1,13},{2,14},{3,15},{4,0},{5,1},{6,2},{7,3},{8,4},{9,5},{1... | collective-permute-start | bytes 1572872 | tf_op jit(solution)/shard_map/ppermute | solution.py:38
  56.9 7.4 %mirror_sums.4 = (bf16[2048,128]{1,0:T(8,128)(2,1)}, bf16[2048,128]{1,0:T(8,128)(2,1)}, bf16[1024,128]{1,0:T(8,128)(2,1)}) custom-call(s32[160]{0:T(256)} %get-tuple-element.62.order, s32[160]{0:T(256)} %get-tuple-element.63.out_slot, s32[160]{0:T(256)} %get-tuple-element.64.in_slot, s32[1]{0:T(128)} %constant.175.clone.1.begin, s32[1]{0:T(128)} %bitcast.1.stop.begin, ...), custom_call_target="tpu_custom_call" | custom-call | flops 2684354560 | bytes 20971520 | tf_op jit(solution)/shard_map/mirror_sums/pallas_call | solution.py:110
  64.3 3.6 %collective-permute-start.15 = (bf16[1024,128]{1,0:T(8,128)(2,1)}, bf16[1024,128]{1,0:T(8,128)(2,1)}, u32[]{:S(2)}, u32[]{:S(2)}) collective-permute-start(bf16[1024,128]{1,0:T(8,128)(2,1)} %get-tuple-element.75), channel_id=1, source_target_pairs={{0,16},{16,0},{32,48},{48,32},{64,80},{80,64},{96,112},{112,96},{1... | collective-permute-start | bytes 786440 | tf_op jit(solution)/shard_map/ppermute | solution.py:27
  68.0 2.0 %collective-permute-start.14 = (bf16[2048,128]{1,0:T(8,128)(2,1)}, bf16[2048,128]{1,0:T(8,128)(2,1)}, u32[]{:S(2)}, u32[]{:S(2)}) collective-permute-start(bf16[2048,128]{1,0:T(8,128)(2,1)} %get-tuple-element.73), channel_id=1, source_target_pairs={{0,96},{16,112},{32,0},{48,16},{64,32},{80,48},{96,64},{112,80},{1... | collective-permute-start | bytes 1572872 | tf_op jit(solution)/shard_map/ppermute | solution.py:27
  72.1 3.3 %collective-permute-start.12 = (bf16[1024,128]{1,0:T(8,128)(2,1)S(1)}, bf16[1024,128]{1,0:T(8,128)(2,1)S(1)}, u32[]{:S(2)}, u32[]{:S(2)}) collective-permute-start(bf16[1024,128]{1,0:T(8,128)(2,1)S(1)} %get-tuple-element.106), channel_id=1, source_target_pairs={{0,2},{1,3},{2,0},{3,1},{4,6},{5,7},{6,4},{7,5},{8,10},{9,11},{10,... | collective-permute-start | bytes 786440 | tf_op jit(solution)/shard_map/ppermute | solution.py:38
  75.3 6.5 %mirror_sums.5 = (bf16[1024,128]{1,0:T(8,128)(2,1)}, bf16[1024,128]{1,0:T(8,128)(2,1)}, bf16[1024,128]{1,0:T(8,128)(2,1)}) custom-call(s32[160]{0:T(256)} %get-tuple-element.62.order, s32[160]{0:T(256)} %get-tuple-element.63.out_slot, s32[160]{0:T(256)} %get-tuple-element.64.in_slot, s32[1]{0:T(128)} %bitcast.1.stop.begin, s32[1]{0:T(128)} %copy.6.stop, ...), custom_call_target="tpu_custom_call" | custom-call | flops 2684354560 | bytes 20971520 | tf_op jit(solution)/shard_map/mirror_sums/pallas_call | solution.py:110
  85.1 5.8 %collective-permute-done.16 = bf16[1024,128]{1,0:T(8,128)(2,1)S(1)} collective-permute-done((bf16[1024,128]{1,0:T(8,128)(2,1)S(1)}, bf16[1024,128]{1,0:T(8,128)(2,1)S(1)}, u32[]{:S(2)}, u32[]{:S(2)}) %collective-permute-start.16) | collective-permute-done | bytes 262176 | tf_op jit(solution)/shard_map/ppermute | solution.py:27
  92.7 2.3 %fusion.2.rest_0_ = bf16[1024,128]{1,0:T(8,128)(2,1)} fusion(bf16[1024,128]{1,0:T(8,128)(2,1)S(1)} %copy-done.1, bf16[1024,128]{1,0:T(8,128)(2,1)S(1)} %collective-permute-done.17, bf16[1024,128]{1,0:T(8,128)(2,1)S(1)} %collective-permute-done.16, bf16[1024,128]{1,0:T(8,128)(2,1)} %get-tuple-element.71, bf16[1024,128]{1,0:T(8,128)(2,1)S(1)} %collective-permute-done.12, ...), kind=kLoop, calls=%fused_computation.8 | loop fusion | flops 3407872 | bytes 3407872 | tf_op jit(solution)/shard_map/convert_element_type | solution.py:218
  95.0 3.2 %collective-permute-start.21 = (bf16[1024,128]{1,0:T(8,128)(2,1)}, bf16[1024,128]{1,0:T(8,128)(2,1)S(1)}, u32[]{:S(2)}, u32[]{:S(2)}) collective-permute-start(bf16[1024,128]{1,0:T(8,128)(2,1)} %fusion.2.rest_0_), channel_id=1, source_target_pairs={{0,64},{16,80},{32,96},{48,112},{64,0},{80,16},{96,32},{112,48},{1... | collective-permute-start | bytes 786440 | tf_op jit(solution)/shard_map/ppermute | solution.py:27
  99.2 3.0 %collective-permute-start.19 = (bf16[1024,128]{1,0:T(8,128)(2,1)}, bf16[1024,128]{1,0:T(8,128)(2,1)S(1)}, u32[]{:S(2)}, u32[]{:S(2)}) collective-permute-start(bf16[1024,128]{1,0:T(8,128)(2,1)} %fusion.2.rest_0_), channel_id=1, source_target_pairs={{0,32},{16,48},{32,64},{48,80},{64,96},{80,112},{96,0},{112,16},{1... | collective-permute-start | bytes 786440 | tf_op jit(solution)/shard_map/ppermute | solution.py:27
  102.2 3.8 %collective-permute-done.21.rest_4_ = bf16[1024,128]{1,0:T(8,128)(2,1)S(1)} collective-permute-done((bf16[1024,128]{1,0:T(8,128)(2,1)}, bf16[1024,128]{1,0:T(8,128)(2,1)S(1)}, u32[]{:S(2)}, u32[]{:S(2)}) %collective-permute-start.21) | collective-permute-done | bytes 262176 | tf_op jit(solution)/shard_map/ppermute | solution.py:27
  107.6 2.9 %collective-permute-done.18.rest_1_ = bf16[1024,128]{1,0:T(8,128)(2,1)S(1)} collective-permute-done((bf16[1024,128]{1,0:T(8,128)(2,1)}, bf16[1024,128]{1,0:T(8,128)(2,1)S(1)}, u32[]{:S(2)}, u32[]{:S(2)}) %collective-permute-start.18) | collective-permute-done | bytes 262176 | tf_op jit(solution)/shard_map/ppermute | solution.py:27
  110.9 2.8 %collective-permute-start.20 = (bf16[1024,128]{1,0:T(8,128)(2,1)S(1)}, bf16[1024,128]{1,0:T(8,128)(2,1)S(1)}, u32[]{:S(2)}, u32[]{:S(2)}) collective-permute-start(bf16[1024,128]{1,0:T(8,128)(2,1)S(1)} %collective-permute-done.18.rest_1_), channel_id=1, source_target_pairs={{0,32},{16,48},{32,64},{48,80},{64,96},{80,112},{96,0},{112,16},{1... | collective-permute-start | bytes 786440 | tf_op jit(solution)/shard_map/ppermute | solution.py:27
  113.7 5.8 %collective-permute-done.22.rest_5_ = bf16[1024,128]{1,0:T(8,128)(2,1)S(1)} collective-permute-done((bf16[1024,128]{1,0:T(8,128)(2,1)S(1)}, bf16[1024,128]{1,0:T(8,128)(2,1)S(1)}, u32[]{:S(2)}, u32[]{:S(2)}) %collective-permute-start.22) | collective-permute-done | bytes 262176 | tf_op jit(solution)/shard_map/ppermute | solution.py:27
  120.5 7.4 %direct_sums.3 = (bf16[1024,128]{1,0:T(8,128)(2,1)S(1)}, bf16[1024,128]{1,0:T(8,128)(2,1)S(1)}, bf16[2048,128]{1,0:T(8,128)(2,1)S(1)}, bf16[1024,128]{1,0:T(8,12...) custom-call(s32[160]{0:T(256)S(1)} %iota.12.order, ...), custom_call_target="tpu_custom_call" | custom-call | flops 2684354560 | bytes 20971520 | tf_op jit(solution)/shard_map/direct_sums/pallas_call | solution.py:110
  128.0 4.4 %collective-permute-done.25 = bf16[8192,128]{1,0:T(8,128)(2,1)S(1)} collective-permute-done((bf16[8192,128]{1,0:T(8,128)(2,1)}, bf16[8192,128]{1,0:T(8,128)(2,1)S(1)}, u32[]{:S(2)}, u32[]{:S(2)}) %collective-permute-start.25) | collective-permute-done | bytes 2097184 | tf_op jit(solution)/shard_map/ppermute | solution.py:38
  133.7 4.6 %collective-permute-start.27 = (bf16[2048,128]{1,0:T(8,128)(2,1)}, bf16[2048,128]{1,0:T(8,128)(2,1)}, u32[]{:S(2)}, u32[]{:S(2)}) collective-permute-start(bf16[2048,128]{1,0:T(8,128)(2,1)} %get-tuple-element.104), channel_id=1, source_target_pairs={{0,12},{1,13},{2,14},{3,15},{4,0},{5,1},{6,2},{7,3},{8,4},{9,5},{1... | collective-permute-start | bytes 1572872 | tf_op jit(solution)/shard_map/ppermute | solution.py:38
  139.1 4.0 %collective-permute-start.28 = (bf16[1024,128]{1,0:T(8,128)(2,1)}, bf16[1024,128]{1,0:T(8,128)(2,1)}, u32[]{:S(2)}, u32[]{:S(2)}) collective-permute-start(bf16[1024,128]{1,0:T(8,128)(2,1)} %add_convert_fusion.8), channel_id=1, source_target_pairs={{0,2},{1,3},{2,0},{3,1},{4,6},{5,7},{6,4},{7,5},{8,10},{9,11},{10,... | collective-permute-start | bytes 786440 | tf_op jit(solution)/shard_map/ppermute | solution.py:38
  143.0 7.4 %mirror_sums.6 = (bf16[2048,128]{1,0:T(8,128)(2,1)}, bf16[2048,128]{1,0:T(8,128)(2,1)}, bf16[1024,128]{1,0:T(8,128)(2,1)}) custom-call(s32[160]{0:T(256)} %get-tuple-element.62.order, s32[160]{0:T(256)} %get-tuple-element.63.out_slot, s32[160]{0:T(256)} %get-tuple-element.64.in_slot, s32[1]{0:T(128)} %constant.175.clone.1.begin, s32[1]{0:T(128)} %bitcast.1.stop.begin, ...), custom_call_target="tpu_custom_call" | custom-call | flops 2684354560 | bytes 20971520 | tf_op jit(solution)/shard_map/mirror_sums/pallas_call | solution.py:110
  152.5 2.0 %collective-permute-start.32 = (bf16[2048,128]{1,0:T(8,128)(2,1)}, bf16[2048,128]{1,0:T(8,128)(2,1)}, u32[]{:S(2)}, u32[]{:S(2)}) collective-permute-start(bf16[2048,128]{1,0:T(8,128)(2,1)} %get-tuple-element.91), channel_id=1, source_target_pairs={{0,96},{16,112},{32,0},{48,16},{64,32},{80,48},{96,64},{112,80},{1... | collective-permute-start | bytes 1572872 | tf_op jit(solution)/shard_map/ppermute | solution.py:27
  154.5 2.1 %add_convert_fusion.7 = (bf16[1024,128]{1,0:T(8,128)(2,1)}, bf16[1024,128]{1,0:T(8,128)(2,1)S(1)}) fusion(bf16[1024,128]{1,0:T(8,128)(2,1)} %collective-permute-done.28, bf16[1024,128]{1,0:T(8,128)(2,1)S(1)} %get-tuple-element.81, bf16[8192,128]{1,0:T(8,128)(2,1)S(1)} %collective-permute-done.25, bf16[2048,128]{1,0:T(8,128)(2,1)} %collective-permute-done.27, ...), kind=kLoop, calls=%fused_computation.12 | loop fusion | flops 1835008 | bytes 2359296 | tf_op jit(solution)/shard_map/convert_element_type | solution.py:150
  157.2 3.4 %collective-permute-start.30 = (bf16[1024,128]{1,0:T(8,128)(2,1)S(1)}, bf16[1024,128]{1,0:T(8,128)(2,1)}, u32[]{:S(2)}, u32[]{:S(2)}) collective-permute-start(bf16[1024,128]{1,0:T(8,128)(2,1)S(1)} %get-tuple-element.102), channel_id=1, source_target_pairs={{0,2},{1,3},{2,0},{3,1},{4,6},{5,7},{6,4},{7,5},{8,10},{9,11},{10,... | collective-permute-start | bytes 786440 | tf_op jit(solution)/shard_map/ppermute | solution.py:38
  160.7 6.5 %mirror_sums.7 = (bf16[1024,128]{1,0:T(8,128)(2,1)}, bf16[1024,128]{1,0:T(8,128)(2,1)}, bf16[1024,128]{1,0:T(8,128)(2,1)}) custom-call(s32[160]{0:T(256)} %get-tuple-element.62.order, s32[160]{0:T(256)} %get-tuple-element.63.out_slot, s32[160]{0:T(256)} %get-tuple-element.64.in_slot, s32[1]{0:T(128)} %bitcast.1.stop.begin, s32[1]{0:T(128)} %copy.6.stop, ...), custom_call_target="tpu_custom_call" | custom-call | flops 2684354560 | bytes 20971520 | tf_op jit(solution)/shard_map/mirror_sums/pallas_call | solution.py:110
  171.5 4.8 %collective-permute-done.34 = bf16[1024,128]{1,0:T(8,128)(2,1)S(1)} collective-permute-done((bf16[1024,128]{1,0:T(8,128)(2,1)S(1)}, bf16[1024,128]{1,0:T(8,128)(2,1)S(1)}, u32[]{:S(2)}, u32[]{:S(2)}) %collective-permute-start.34) | collective-permute-done | bytes 262176 | tf_op jit(solution)/shard_map/ppermute | solution.py:27
  178.0 2.7 %convert_subtract_fusion = f32[1024,128]{1,0:T(8,128)} fusion(bf16[1024,128]{1,0:T(8,128)(2,1)S(1)} %copy-done.1, bf16[1024,128]{1,0:T(8,128)(2,1)S(1)} %copy-done.3, bf16[1024,128]{1,0:T(8,128)(2,1)S(1)} %collective-permute-done.35, bf16[1024,128]{1,0:T(8,128)(2,1)S(1)} %collective-permute-done.34, bf16[1024,128]{1,0:T(8,128)(2,1)} %get-tuple-element.89, ...), kind=kLoop, calls=%fused_computation.4 | loop fusion | flops 3538944 | bytes 3932160 | tf_op jit(solution)/shard_map/sub | solution.py:220
  (79 shorter events, 32.0 us)
Async XLA Ops:
  6.5 50.4 %all-gather.3.cloned.1.call-start = ((), (), s32[]{:S(2)}) async-start(), calls=%async_computation | async-start | bytes 4456448 | tf_op jit(solution)/shard_map/all_gather | solution.py:142
  7.3 135.8 %all-gather.5.cloned.1.call-start = ((), (), s32[]{:S(2)}) async-start(), calls=%async_computation.1 | async-start | bytes 4456448 | tf_op jit(solution)/shard_map/all_gather | solution.py:142
  7.3 9.8 %collective-permute-start = (bf16[1024,128]{1,0:T(8,128)(2,1)}, bf16[1024,128]{1,0:T(8,128)(2,1)S(1)}, u32[]{:S(2)}, u32[]{:S(2)}) collective-permute-start(bf16[1024,128]{1,0:T(8,128)(2,1)} %rest_0_.1), channel_id=1, source_target_pairs={{0,16},{16,0},{32,48},{48,32},{64,80},{80,64},{96,112},{112,96},{1... | collective-permute-start | bytes 786440 | tf_op jit(solution)/shard_map/ppermute | solution.py:27
  9.7 11.0 %collective-permute-start.3 = (bf16[1024,128]{1,0:T(8,128)(2,1)}, bf16[1024,128]{1,0:T(8,128)(2,1)S(1)}, u32[]{:S(2)}, u32[]{:S(2)}) collective-permute-start(bf16[1024,128]{1,0:T(8,128)(2,1)} %rest_0_.1), channel_id=1, source_target_pairs={{0,64},{16,80},{32,96},{48,112},{64,0},{80,16},{96,32},{112,48},{1... | collective-permute-start | bytes 786440 | tf_op jit(solution)/shard_map/ppermute | solution.py:27
  11.1 13.8 %collective-permute-start.5 = (bf16[1024,128]{1,0:T(8,128)(2,1)}, bf16[1024,128]{1,0:T(8,128)(2,1)S(1)}, u32[]{:S(2)}, u32[]{:S(2)}) collective-permute-start(bf16[1024,128]{1,0:T(8,128)(2,1)} %rest_0_.1), channel_id=1, source_target_pairs={{0,96},{16,112},{32,0},{48,16},{64,32},{80,48},{96,64},{112,80},{1... | collective-permute-start | bytes 786440 | tf_op jit(solution)/shard_map/ppermute | solution.py:27
  11.1 13.8 %collective-permute-start.1 = (bf16[1024,128]{1,0:T(8,128)(2,1)}, bf16[1024,128]{1,0:T(8,128)(2,1)S(1)}, u32[]{:S(2)}, u32[]{:S(2)}) collective-permute-start(bf16[1024,128]{1,0:T(8,128)(2,1)} %rest_0_.1), channel_id=1, source_target_pairs={{0,32},{16,48},{32,64},{48,80},{64,96},{80,112},{96,0},{112,16},{1... | collective-permute-start | bytes 786440 | tf_op jit(solution)/shard_map/ppermute | solution.py:27
  17.1 18.8 %collective-permute-start.6 = (bf16[1024,128]{1,0:T(8,128)(2,1)S(1)}, bf16[1024,128]{1,0:T(8,128)(2,1)S(1)}, u32[]{:S(2)}, u32[]{:S(2)}) collective-permute-start(bf16[1024,128]{1,0:T(8,128)(2,1)S(1)} %collective-permute-done.rest_1_), channel_id=1, source_target_pairs={{0,96},{16,112},{32,0},{48,16},{64,32},{80,48},{96,64},{112,80},{1... | collective-permute-start | bytes 786440 | tf_op jit(solution)/shard_map/ppermute | solution.py:27
  18.0 17.9 %collective-permute-start.2 = (bf16[1024,128]{1,0:T(8,128)(2,1)S(1)}, bf16[1024,128]{1,0:T(8,128)(2,1)S(1)}, u32[]{:S(2)}, u32[]{:S(2)}) collective-permute-start(bf16[1024,128]{1,0:T(8,128)(2,1)S(1)} %collective-permute-done.rest_1_), channel_id=1, source_target_pairs={{0,32},{16,48},{32,64},{48,80},{64,96},{80,112},{96,0},{112,16},{1... | collective-permute-start | bytes 786440 | tf_op jit(solution)/shard_map/ppermute | solution.py:27
  20.7 15.2 %collective-permute-start.4 = (bf16[1024,128]{1,0:T(8,128)(2,1)S(1)}, bf16[1024,128]{1,0:T(8,128)(2,1)S(1)}, u32[]{:S(2)}, u32[]{:S(2)}) collective-permute-start(bf16[1024,128]{1,0:T(8,128)(2,1)S(1)} %collective-permute-done.3.rest_4_), channel_id=1, source_target_pairs={{0,16},{16,0},{32,48},{48,32},{64,80},{80,64},{96,112},{112,96},{1... | collective-permute-start | bytes 786440 | tf_op jit(solution)/shard_map/ppermute | solution.py:27
  49.0 21.0 %collective-permute-start.8 = (bf16[2048,128]{1,0:T(8,128)(2,1)S(1)}, bf16[2048,128]{1,0:T(8,128)(2,1)S(1)}, u32[]{:S(2)}, u32[]{:S(2)}) collective-permute-start(bf16[2048,128]{1,0:T(8,128)(2,1)S(1)} %get-tuple-element.107), channel_id=1, source_target_pairs={{0,4},{1,5},{2,6},{3,7},{4,8},{5,9},{6,10},{7,11},{8,12},{9,13},{1... | collective-permute-start | bytes 1572872 | tf_op jit(solution)/shard_map/ppermute | solution.py:38
  49.1 20.9 %collective-permute-start.9 = (bf16[2048,128]{1,0:T(8,128)(2,1)S(1)}, bf16[2048,128]{1,0:T(8,128)(2,1)S(1)}, u32[]{:S(2)}, u32[]{:S(2)}) collective-permute-start(bf16[2048,128]{1,0:T(8,128)(2,1)S(1)} %get-tuple-element.108), channel_id=1, source_target_pairs={{0,12},{1,13},{2,14},{3,15},{4,0},{5,1},{6,2},{7,3},{8,4},{9,5},{1... | collective-permute-start | bytes 1572872 | tf_op jit(solution)/shard_map/ppermute | solution.py:38
  55.7 12.3 %collective-permute-start.10 = (bf16[1024,128]{1,0:T(8,128)(2,1)S(1)}, bf16[1024,128]{1,0:T(8,128)(2,1)S(1)}, u32[]{:S(2)}, u32[]{:S(2)}) collective-permute-start(bf16[1024,128]{1,0:T(8,128)(2,1)S(1)} %add_convert_fusion.13), channel_id=1, source_target_pairs={{0,2},{1,3},{2,0},{3,1},{4,6},{5,7},{6,4},{7,5},{8,10},{9,11},{10,... | collective-permute-start | bytes 786440 | tf_op jit(solution)/shard_map/ppermute | solution.py:38
  64.3 17.5 %collective-permute-start.15 = (bf16[1024,128]{1,0:T(8,128)(2,1)}, bf16[1024,128]{1,0:T(8,128)(2,1)}, u32[]{:S(2)}, u32[]{:S(2)}) collective-permute-start(bf16[1024,128]{1,0:T(8,128)(2,1)} %get-tuple-element.75), channel_id=1, source_target_pairs={{0,16},{16,0},{32,48},{48,32},{64,80},{80,64},{96,112},{112,96},{1... | collective-permute-start | bytes 786440 | tf_op jit(solution)/shard_map/ppermute | solution.py:27
  68.0 15.1 %collective-permute-start.13 = (bf16[2048,128]{1,0:T(8,128)(2,1)}, bf16[2048,128]{1,0:T(8,128)(2,1)S(1)}, u32[]{:S(2)}, u32[]{:S(2)}) collective-permute-start(bf16[2048,128]{1,0:T(8,128)(2,1)} %get-tuple-element.72), channel_id=1, source_target_pairs={{0,32},{16,48},{32,64},{48,80},{64,96},{80,112},{96,0},{112,16},{1... | collective-permute-start | bytes 1572872 | tf_op jit(solution)/shard_map/ppermute | solution.py:27
  68.0 15.1 %collective-permute-start.14 = (bf16[2048,128]{1,0:T(8,128)(2,1)}, bf16[2048,128]{1,0:T(8,128)(2,1)}, u32[]{:S(2)}, u32[]{:S(2)}) collective-permute-start(bf16[2048,128]{1,0:T(8,128)(2,1)} %get-tuple-element.73), channel_id=1, source_target_pairs={{0,96},{16,112},{32,0},{48,16},{64,32},{80,48},{96,64},{112,80},{1... | collective-permute-start | bytes 1572872 | tf_op jit(solution)/shard_map/ppermute | solution.py:27
  71.3 13.8 %collective-permute-start.11 = (bf16[1024,128]{1,0:T(8,128)(2,1)S(1)}, bf16[1024,128]{1,0:T(8,128)(2,1)S(1)}, u32[]{:S(2)}, u32[]{:S(2)}) collective-permute-start(bf16[1024,128]{1,0:T(8,128)(2,1)S(1)} %get-tuple-element.105), channel_id=1, source_target_pairs={{0,8},{1,9},{2,10},{3,11},{4,12},{5,13},{6,14},{7,15},{8,0},{9,1},... | collective-permute-start | bytes 786440 | tf_op jit(solution)/shard_map/ppermute | solution.py:38
  72.1 13.0 %collective-permute-start.12 = (bf16[1024,128]{1,0:T(8,128)(2,1)S(1)}, bf16[1024,128]{1,0:T(8,128)(2,1)S(1)}, u32[]{:S(2)}, u32[]{:S(2)}) collective-permute-start(bf16[1024,128]{1,0:T(8,128)(2,1)S(1)} %get-tuple-element.106), channel_id=1, source_target_pairs={{0,2},{1,3},{2,0},{3,1},{4,6},{5,7},{6,4},{7,5},{8,10},{9,11},{10,... | collective-permute-start | bytes 786440 | tf_op jit(solution)/shard_map/ppermute | solution.py:38
  95.0 11.0 %collective-permute-start.21 = (bf16[1024,128]{1,0:T(8,128)(2,1)}, bf16[1024,128]{1,0:T(8,128)(2,1)S(1)}, u32[]{:S(2)}, u32[]{:S(2)}) collective-permute-start(bf16[1024,128]{1,0:T(8,128)(2,1)} %fusion.2.rest_0_), channel_id=1, source_target_pairs={{0,64},{16,80},{32,96},{48,112},{64,0},{80,16},{96,32},{112,48},{1... | collective-permute-start | bytes 786440 | tf_op jit(solution)/shard_map/ppermute | solution.py:27
  98.2 12.2 %collective-permute-start.18 = (bf16[1024,128]{1,0:T(8,128)(2,1)}, bf16[1024,128]{1,0:T(8,128)(2,1)S(1)}, u32[]{:S(2)}, u32[]{:S(2)}) collective-permute-start(bf16[1024,128]{1,0:T(8,128)(2,1)} %fusion.2.rest_0_), channel_id=1, source_target_pairs={{0,16},{16,0},{32,48},{48,32},{64,80},{80,64},{96,112},{112,96},{1... | collective-permute-start | bytes 786440 | tf_op jit(solution)/shard_map/ppermute | solution.py:27
  99.0 14.7 %collective-permute-start.23 = (bf16[1024,128]{1,0:T(8,128)(2,1)}, bf16[1024,128]{1,0:T(8,128)(2,1)S(1)}, u32[]{:S(2)}, u32[]{:S(2)}) collective-permute-start(bf16[1024,128]{1,0:T(8,128)(2,1)} %fusion.2.rest_0_), channel_id=1, source_target_pairs={{0,96},{16,112},{32,0},{48,16},{64,32},{80,48},{96,64},{112,80},{1... | collective-permute-start | bytes 786440 | tf_op jit(solution)/shard_map/ppermute | solution.py:27
  99.2 14.5 %collective-permute-start.19 = (bf16[1024,128]{1,0:T(8,128)(2,1)}, bf16[1024,128]{1,0:T(8,128)(2,1)S(1)}, u32[]{:S(2)}, u32[]{:S(2)}) collective-permute-start(bf16[1024,128]{1,0:T(8,128)(2,1)} %fusion.2.rest_0_), channel_id=1, source_target_pairs={{0,32},{16,48},{32,64},{48,80},{64,96},{80,112},{96,0},{112,16},{1... | collective-permute-start | bytes 786440 | tf_op jit(solution)/shard_map/ppermute | solution.py:27
  106.1 13.5 %collective-permute-start.22 = (bf16[1024,128]{1,0:T(8,128)(2,1)S(1)}, bf16[1024,128]{1,0:T(8,128)(2,1)S(1)}, u32[]{:S(2)}, u32[]{:S(2)}) collective-permute-start(bf16[1024,128]{1,0:T(8,128)(2,1)S(1)} %collective-permute-done.21.rest_4_), channel_id=1, source_target_pairs={{0,16},{16,0},{32,48},{48,32},{64,80},{80,64},{96,112},{112,96},{1... | collective-permute-start | bytes 786440 | tf_op jit(solution)/shard_map/ppermute | solution.py:27
  110.5 9.0 %collective-permute-start.24 = (bf16[1024,128]{1,0:T(8,128)(2,1)S(1)}, bf16[1024,128]{1,0:T(8,128)(2,1)S(1)}, u32[]{:S(2)}, u32[]{:S(2)}) collective-permute-start(bf16[1024,128]{1,0:T(8,128)(2,1)S(1)} %collective-permute-done.18.rest_1_), channel_id=1, source_target_pairs={{0,96},{16,112},{32,0},{48,16},{64,32},{80,48},{96,64},{112,80},{1... | collective-permute-start | bytes 786440 | tf_op jit(solution)/shard_map/ppermute | solution.py:27
  110.9 8.6 %collective-permute-start.20 = (bf16[1024,128]{1,0:T(8,128)(2,1)S(1)}, bf16[1024,128]{1,0:T(8,128)(2,1)S(1)}, u32[]{:S(2)}, u32[]{:S(2)}) collective-permute-start(bf16[1024,128]{1,0:T(8,128)(2,1)S(1)} %collective-permute-done.18.rest_1_), channel_id=1, source_target_pairs={{0,32},{16,48},{32,64},{48,80},{64,96},{80,112},{96,0},{112,16},{1... | collective-permute-start | bytes 786440 | tf_op jit(solution)/shard_map/ppermute | solution.py:27
  133.7 20.8 %collective-permute-start.26 = (bf16[2048,128]{1,0:T(8,128)(2,1)}, bf16[2048,128]{1,0:T(8,128)(2,1)}, u32[]{:S(2)}, u32[]{:S(2)}) collective-permute-start(bf16[2048,128]{1,0:T(8,128)(2,1)} %get-tuple-element.103), channel_id=1, source_target_pairs={{0,4},{1,5},{2,6},{3,7},{4,8},{5,9},{6,10},{7,11},{8,12},{9,13},{1... | collective-permute-start | bytes 1572872 | tf_op jit(solution)/shard_map/ppermute | solution.py:38
  133.7 20.8 %collective-permute-start.27 = (bf16[2048,128]{1,0:T(8,128)(2,1)}, bf16[2048,128]{1,0:T(8,128)(2,1)}, u32[]{:S(2)}, u32[]{:S(2)}) collective-permute-start(bf16[2048,128]{1,0:T(8,128)(2,1)} %get-tuple-element.104), channel_id=1, source_target_pairs={{0,12},{1,13},{2,14},{3,15},{4,0},{5,1},{6,2},{7,3},{8,4},{9,5},{1... | collective-permute-start | bytes 1572872 | tf_op jit(solution)/shard_map/ppermute | solution.py:38
  139.1 13.4 %collective-permute-start.28 = (bf16[1024,128]{1,0:T(8,128)(2,1)}, bf16[1024,128]{1,0:T(8,128)(2,1)}, u32[]{:S(2)}, u32[]{:S(2)}) collective-permute-start(bf16[1024,128]{1,0:T(8,128)(2,1)} %add_convert_fusion.8), channel_id=1, source_target_pairs={{0,2},{1,3},{2,0},{3,1},{4,6},{5,7},{6,4},{7,5},{8,10},{9,11},{10,... | collective-permute-start | bytes 786440 | tf_op jit(solution)/shard_map/ppermute | solution.py:38
  150.5 16.7 %collective-permute-start.33 = (bf16[1024,128]{1,0:T(8,128)(2,1)}, bf16[1024,128]{1,0:T(8,128)(2,1)S(1)}, u32[]{:S(2)}, u32[]{:S(2)}) collective-permute-start(bf16[1024,128]{1,0:T(8,128)(2,1)} %get-tuple-element.93), channel_id=1, source_target_pairs={{0,16},{16,0},{32,48},{48,32},{64,80},{80,64},{96,112},{112,96},{1... | collective-permute-start | bytes 786440 | tf_op jit(solution)/shard_map/ppermute | solution.py:27
  152.5 15.8 %collective-permute-start.31 = (bf16[2048,128]{1,0:T(8,128)(2,1)}, bf16[2048,128]{1,0:T(8,128)(2,1)}, u32[]{:S(2)}, u32[]{:S(2)}) collective-permute-start(bf16[2048,128]{1,0:T(8,128)(2,1)} %get-tuple-element.90), channel_id=1, source_target_pairs={{0,32},{16,48},{32,64},{48,80},{64,96},{80,112},{96,0},{112,16},{1... | collective-permute-start | bytes 1572872 | tf_op jit(solution)/shard_map/ppermute | solution.py:27
  152.5 15.8 %collective-permute-start.32 = (bf16[2048,128]{1,0:T(8,128)(2,1)}, bf16[2048,128]{1,0:T(8,128)(2,1)}, u32[]{:S(2)}, u32[]{:S(2)}) collective-permute-start(bf16[2048,128]{1,0:T(8,128)(2,1)} %get-tuple-element.91), channel_id=1, source_target_pairs={{0,96},{16,112},{32,0},{48,16},{64,32},{80,48},{96,64},{112,80},{1... | collective-permute-start | bytes 1572872 | tf_op jit(solution)/shard_map/ppermute | solution.py:27
  156.6 14.9 %collective-permute-start.29 = (bf16[1024,128]{1,0:T(8,128)(2,1)}, bf16[1024,128]{1,0:T(8,128)(2,1)}, u32[]{:S(2)}, u32[]{:S(2)}) collective-permute-start(bf16[1024,128]{1,0:T(8,128)(2,1)} %get-tuple-element.101), channel_id=1, source_target_pairs={{0,8},{1,9},{2,10},{3,11},{4,12},{5,13},{6,14},{7,15},{8,0},{9,1},... | collective-permute-start | bytes 786440 | tf_op jit(solution)/shard_map/ppermute | solution.py:38
  157.2 14.2 %collective-permute-start.30 = (bf16[1024,128]{1,0:T(8,128)(2,1)S(1)}, bf16[1024,128]{1,0:T(8,128)(2,1)}, u32[]{:S(2)}, u32[]{:S(2)}) collective-permute-start(bf16[1024,128]{1,0:T(8,128)(2,1)S(1)} %get-tuple-element.102), channel_id=1, source_target_pairs={{0,2},{1,3},{2,0},{3,1},{4,6},{5,7},{6,4},{7,5},{8,10},{9,11},{10,... | collective-permute-start | bytes 786440 | tf_op jit(solution)/shard_map/ppermute | solution.py:38
  (11 other events, 92.2 us)
Sparse Core Ops, SparseCore 0:
  9.1 43.5 all-gather.2
  95.1 41.1 all-gather.4

commit v4 on v3

--- a/solution.py
+++ b/solution.py
@@ -38,14 +38,14 @@
     return lax.ppermute(value, "col", pairs)
 
 
-def spmv_kernel(mirror, n_in, n_out, order, out_slot, in_slot, begin, stop, tiles, *rest):
+def spmv_kernel(mirror, n_in, n_out, order, out_slot, in_slot, bounds, tiles, *rest):
     v_in = rest[:n_in]
     outs = rest[n_in : n_in + n_out]
     acc, held, ring, in_sems, ring_sems = rest[n_in + n_out :]
     depth = ring.shape[0]
     slots = tiles.shape[0]
     unused = acc.shape[0] - 1
-    first, end = begin[0], stop[0]
+    first, end = bounds[0], bounds[1]
     steps = (end - first + CHUNK - 1) // CHUNK
 
     def place(step, j):
@@ -103,13 +103,13 @@
             at += 1
 
 
-def spmv(mirror, tiles, order, out_slot, in_slot, begin, stop, v_in, out_rows):
+def spmv(mirror, tiles, order, out_slot, in_slot, bounds, v_in, out_rows):
     slots = tiles.shape[0]
     n_in, n_out = len(v_in), len(out_rows)
     blocks_out = sum(out_rows) // BS
     return pl.pallas_call(
         functools.partial(spmv_kernel, mirror, n_in, n_out),
-        in_specs=[pl.BlockSpec(memory_space=pltpu.SMEM)] * 5
+        in_specs=[pl.BlockSpec(memory_space=pltpu.SMEM)] * 4
         + [pl.BlockSpec(memory_space=pl.ANY)] * (1 + n_in),
         out_specs=[pl.BlockSpec(memory_space=pltpu.VMEM)] * n_out,
         scratch_shapes=[
@@ -125,7 +125,7 @@
             flops=2 * slots * BS * BS * NV, bytes_accessed=slots * BS * BS * 2, transcendentals=0
         ),
         name="mirror_sums" if mirror else "direct_sums",
-    )(order, out_slot, in_slot, begin, stop, tiles, *v_in)
+    )(order, out_slot, in_slot, bounds, tiles, *v_in)
 
 
 def gather_row(field):
@@ -166,9 +166,9 @@
     col_parts = gather_col(field)
     *mine, other = spmv(False, tiles, *direct, row_parts, split + [8 * rows])
     theirs = jnp.split(send_col(other, (0, 0), 1), [rows, 2 * rows, 4 * rows, 5 * rows, 6 * rows])
-    early = spmv(True, tiles, *mirror, *first, col_parts, [2 * rows, 2 * rows, rows])
+    early = spmv(True, tiles, *mirror, first, col_parts, [2 * rows, 2 * rows, rows])
     rest, up, down, far_beside = lax.optimization_barrier((rest, *early))
-    own, beside, far = spmv(True, tiles, *mirror, *rest, col_parts, [rows] * 3)
+    own, beside, far = spmv(True, tiles, *mirror, rest, col_parts, [rows] * 3)
     parts = scatter(send_col, *([a, b] for a, b in zip(mine, theirs)))
     parts += scatter(send_row, [own], [beside], [up], [far], [far_beside], [down])
     return total(parts)
@@ -203,16 +203,18 @@
     def ordered(values):
         return jnp.sum(jnp.where(chosen, values[None, :], 0), axis=1)
 
-    early_count = jnp.sum((group == 0).astype(jnp.int32), keepdims=True)
-    none = jnp.zeros((1,), jnp.int32)
-    direct = (at, jnp.where(live, to_col, 0), jnp.where(live, from_row, 0), none, tile_count)
+    live_count = tile_count[0]
+    early_count = jnp.sum((group == 0).astype(jnp.int32))
+    zero = jnp.zeros((), jnp.int32)
+    whole = jnp.stack([zero, live_count])
+    first = jnp.stack([zero, early_count])
+    rest = jnp.stack([early_count, live_count])
+    direct = (at, jnp.where(live, to_col, 0), jnp.where(live, from_row, 0), whole)
     mirror = (
         ordered(at),
         ordered(jnp.where(live, to_row, 0)),
         ordered(jnp.where(live, from_col, 0)),
     )
-    direct, mirror, early_count = lax.optimization_barrier((direct, mirror, early_count))
-    first, rest = (none, early_count), (early_count, tile_count)
     x_float = vectors.astype(jnp.float32)
     applied = apply(vectors, tiles, direct, mirror, first, rest)
     first_term = ((applied - center_value * x_float) / radius_value).astype(jnp.bfloat16)

time: 190 us -> 190 us (level)
  starting transfers between devices: 61.7 us -> 48.9 us
  Pallas kernels: 42.6 us -> 48.7 us
  waiting for transfers between devices: 48.8 us -> 54.1 us
  other arithmetic: 18.2 us -> 20.7 us
    ppermute x24, waiting for transfers between devices: 39.3 us -> 47.1 us  [send_row(): return lax.ppermute(value, 'row', pairs)]
    ppermute x24, starting transfers between devices: 36.9 us -> 29.9 us  [send_row(): return lax.ppermute(value, 'row', pairs)]
    pallas_call x6, Pallas kernels: 42.6 us -> 48.7 us  [spmv(): pl.pallas_call(functools.partial(spmv_kernel, mirror, n_in, n_out), in_sp...]
    ppermute x12, starting transfers between devices: 24.7 us -> 19 us  [send_col(): return lax.ppermute(value, 'col', pairs)]
    ppermute x12, waiting for transfers between devices: 8.82 us -> 6.21 us  [send_col(): return lax.ppermute(value, 'col', pairs)]
    another operation x0 -> x3, other arithmetic: none -> 2.51 us  [the longest x1 1.26 us: local(): first = jnp.stack([zero, early_count])]
  transfers between devices with their start and end apart: 38 -> 38, of which waited for: 13 -> 13; matrix products, arithmetic and copies ran while one was open for 7% -> 8% of each run, Pallas kernels for 23% -> 26%
where the time goes in v4:
time: 190 us; the launch traced here: 189 us
  waiting for transfers between devices  54.1 us (28%)
  starting transfers between devices  48.9 us (26%)
  Pallas kernels  48.7 us (26%)
  other arithmetic  20.7 us (11%)
  between operations  14.2 us (7%)
  local copies, waits for them, and re-layouts  1.91 us (1%)
    pallas_call x6, Pallas kernels, spmv(): pl.pallas_call(functools.partial(spmv_kernel, mirror, n_in, n_out), in_sp...  48.7 us
    ppermute x24, waiting for transfers between devices, send_row(): return lax.ppermute(value, 'row', pairs)  47.1 us
    ppermute x24, starting transfers between devices, send_row(): return lax.ppermute(value, 'row', pairs)  29.9 us
    ppermute x12, starting transfers between devices, send_col(): return lax.ppermute(value, 'col', pairs)  19 us
    convert_element_type x10, other arithmetic, rounded(): return parts[0] if len(parts) == 1 else total(parts).astype(jnp.bfloat16)  10.8 us
    ppermute x12, waiting for transfers between devices, send_col(): return lax.ppermute(value, 'col', pairs)  6.21 us
  transfers between devices with their start and end apart: 38, of which 13 were waited for; matrix products, arithmetic and copies ran while one was open for 8% of the time, Pallas kernels for 26%

profile of v4, /device:TPU:14, one launch (start us, length us, event | category | flops | bytes accessed | tf_op | source)
XLA Modules:
  0.0 188.6 jit_solution(12961582301226868306)
XLA Ops:
  7.3 2.4 %collective-permute-start = (bf16[1024,128]{1,0:T(8,128)(2,1)}, bf16[1024,128]{1,0:T(8,128)(2,1)S(1)}, u32[]{:S(2)}, u32[]{:S(2)}) collective-permute-start(bf16[1024,128]{1,0:T(8,128)(2,1)} %rest_0_.1), channel_id=1, source_target_pairs={{0,16},{16,0},{32,48},{48,32},{64,80},{80,64},{96,112},{112,96},{1... | collective-permute-start | bytes 786440 | tf_op jit(solution)/shard_map/ppermute | solution.py:27
  11.1 3.2 %collective-permute-start.1 = (bf16[1024,128]{1,0:T(8,128)(2,1)}, bf16[1024,128]{1,0:T(8,128)(2,1)S(1)}, u32[]{:S(2)}, u32[]{:S(2)}) collective-permute-start(bf16[1024,128]{1,0:T(8,128)(2,1)} %rest_0_.1), channel_id=1, source_target_pairs={{0,32},{16,48},{32,64},{48,80},{64,96},{80,112},{96,0},{112,16},{1... | collective-permute-start | bytes 786440 | tf_op jit(solution)/shard_map/ppermute | solution.py:27
  15.0 2.2 %collective-permute-done.rest_1_ = bf16[1024,128]{1,0:T(8,128)(2,1)S(1)} collective-permute-done((bf16[1024,128]{1,0:T(8,128)(2,1)}, bf16[1024,128]{1,0:T(8,128)(2,1)S(1)}, u32[]{:S(2)}, u32[]{:S(2)}) %collective-permute-start) | collective-permute-done | bytes 262176 | tf_op jit(solution)/shard_map/ppermute | solution.py:27
  18.0 2.4 %collective-permute-start.2 = (bf16[1024,128]{1,0:T(8,128)(2,1)S(1)}, bf16[1024,128]{1,0:T(8,128)(2,1)S(1)}, u32[]{:S(2)}, u32[]{:S(2)}) collective-permute-start(bf16[1024,128]{1,0:T(8,128)(2,1)S(1)} %collective-permute-done.rest_1_), channel_id=1, source_target_pairs={{0,32},{16,48},{32,64},{48,80},{64,96},{80,112},{96,0},{112,16},{1... | collective-permute-start | bytes 786440 | tf_op jit(solution)/shard_map/ppermute | solution.py:27
  20.7 2.0 %collective-permute-start.4 = (bf16[1024,128]{1,0:T(8,128)(2,1)S(1)}, bf16[1024,128]{1,0:T(8,128)(2,1)S(1)}, u32[]{:S(2)}, u32[]{:S(2)}) collective-permute-start(bf16[1024,128]{1,0:T(8,128)(2,1)S(1)} %collective-permute-done.3.rest_4_), channel_id=1, source_target_pairs={{0,16},{16,0},{32,48},{48,32},{64,80},{80,64},{96,112},{112,96},{1... | collective-permute-start | bytes 786440 | tf_op jit(solution)/shard_map/ppermute | solution.py:27
  24.9 11.0 %collective-permute-done.4.rest_5_ = bf16[1024,128]{1,0:T(8,128)(2,1)S(1)} collective-permute-done((bf16[1024,128]{1,0:T(8,128)(2,1)S(1)}, bf16[1024,128]{1,0:T(8,128)(2,1)S(1)}, u32[]{:S(2)}, u32[]{:S(2)}) %collective-permute-start.4) | collective-permute-done | bytes 262176 | tf_op jit(solution)/shard_map/ppermute | solution.py:27
  36.9 9.9 %direct_sums.2 = (bf16[1024,128]{1,0:T(8,128)(2,1)S(1)}, bf16[1024,128]{1,0:T(8,128)(2,1)S(1)}, bf16[2048,128]{1,0:T(8,128)(2,1)S(1)}, bf16[1024,128]{1,0:T(8,12...) custom-call(s32[160]{0:T(256)S(1)} %iota.16.order, ...), custom_call_target="tpu_custom_call" | custom-call | flops 2684354560 | bytes 20971520 | tf_op jit(solution)/shard_map/direct_sums/pallas_call | solution.py:110
  51.6 3.2 %collective-permute-start.9 = (bf16[2048,128]{1,0:T(8,128)(2,1)S(1)}, bf16[2048,128]{1,0:T(8,128)(2,1)S(1)}, u32[]{:S(2)}, u32[]{:S(2)}) collective-permute-start(bf16[2048,128]{1,0:T(8,128)(2,1)S(1)} %get-tuple-element.87), channel_id=1, source_target_pairs={{0,12},{1,13},{2,14},{3,15},{4,0},{5,1},{6,2},{7,3},{8,4},{9,5},{1... | collective-permute-start | bytes 1572872 | tf_op jit(solution)/shard_map/ppermute | solution.py:38
  58.1 7.8 %mirror_sums.4 = (bf16[2048,128]{1,0:T(8,128)(2,1)}, bf16[2048,128]{1,0:T(8,128)(2,1)}, bf16[1024,128]{1,0:T(8,128)(2,1)}) custom-call(s32[160]{0:T(256)} %get-tuple-element.75.order, s32[160]{0:T(256)} %get-tuple-element.74.out_slot, s32[160]{0:T(256)} %get-tuple-element.73.in_slot, s32[2]{0:T(128)} %pad_add_fusion.bounds, bf16[160,256,256]{2,1,0:T(8,128)(2,1)} %tiles.11, ...), custom_call_target="tpu_custom_call" | custom-call | flops 2684354560 | bytes 20971520 | tf_op jit(solution)/shard_map/mirror_sums/pallas_call | solution.py:110
  67.1 1.6 collective-permute-start.14
  70.0 1.6 collective-permute-start.11
  71.6 2.2 %collective-permute-start.12 = (bf16[1024,128]{1,0:T(8,128)(2,1)S(1)}, bf16[1024,128]{1,0:T(8,128)(2,1)S(1)}, u32[]{:S(2)}, u32[]{:S(2)}) collective-permute-start(bf16[1024,128]{1,0:T(8,128)(2,1)S(1)} %get-tuple-element.85), channel_id=1, source_target_pairs={{0,2},{1,3},{2,0},{3,1},{4,6},{5,7},{6,4},{7,5},{8,10},{9,11},{10,... | collective-permute-start | bytes 786440 | tf_op jit(solution)/shard_map/ppermute | solution.py:38
  73.7 6.7 %mirror_sums.5 = (bf16[1024,128]{1,0:T(8,128)(2,1)}, bf16[1024,128]{1,0:T(8,128)(2,1)}, bf16[1024,128]{1,0:T(8,128)(2,1)}) custom-call(s32[160]{0:T(256)} %get-tuple-element.75.order, s32[160]{0:T(256)} %get-tuple-element.74.out_slot, s32[160]{0:T(256)} %get-tuple-element.73.in_slot, s32[2]{0:T(128)} %pad_add_fusion.2.bounds, bf16[160,256,256]{2,1,0:T(8,128)(2,1)} %tiles.11, ...), custom_call_target="tpu_custom_call" | custom-call | flops 2684354560 | bytes 20971520 | tf_op jit(solution)/shard_map/mirror_sums/pallas_call | solution.py:110
  83.6 1.8 collective-permute-start.17
  85.3 4.2 %collective-permute-done.16 = bf16[1024,128]{1,0:T(8,128)(2,1)S(1)} collective-permute-done((bf16[1024,128]{1,0:T(8,128)(2,1)S(1)}, bf16[1024,128]{1,0:T(8,128)(2,1)S(1)}, u32[]{:S(2)}, u32[]{:S(2)}) %collective-permute-start.16) | collective-permute-done | bytes 262176 | tf_op jit(solution)/shard_map/ppermute | solution.py:27
  89.5 4.4 %collective-permute-done.17 = bf16[1024,128]{1,0:T(8,128)(2,1)S(1)} collective-permute-done((bf16[1024,128]{1,0:T(8,128)(2,1)S(1)}, bf16[1024,128]{1,0:T(8,128)(2,1)S(1)}, u32[]{:S(2)}, u32[]{:S(2)}) %collective-permute-start.17) | collective-permute-done | bytes 262176 | tf_op jit(solution)/shard_map/ppermute | solution.py:27
  93.8 2.3 %fusion.2.rest_0_ = bf16[1024,128]{1,0:T(8,128)(2,1)} fusion(bf16[1024,128]{1,0:T(8,128)(2,1)S(1)} %copy-done.1, bf16[1024,128]{1,0:T(8,128)(2,1)S(1)} %collective-permute-done.17, bf16[1024,128]{1,0:T(8,128)(2,1)S(1)} %collective-permute-done.16, bf16[1024,128]{1,0:T(8,128)(2,1)} %get-tuple-element.50, bf16[1024,128]{1,0:T(8,128)(2,1)S(1)} %collective-permute-done.12, ...), kind=kLoop, calls=%fused_computation.8 | loop fusion | flops 3407872 | bytes 3407872 | tf_op jit(solution)/shard_map/convert_element_type | solution.py:220
  98.7 2.4 %collective-permute-start.19 = (bf16[1024,128]{1,0:T(8,128)(2,1)}, bf16[1024,128]{1,0:T(8,128)(2,1)S(1)}, u32[]{:S(2)}, u32[]{:S(2)}) collective-permute-start(bf16[1024,128]{1,0:T(8,128)(2,1)} %fusion.2.rest_0_), channel_id=1, source_target_pairs={{0,32},{16,48},{32,64},{48,80},{64,96},{80,112},{96,0},{112,16},{1... | collective-permute-start | bytes 786440 | tf_op jit(solution)/shard_map/ppermute | solution.py:27
  101.1 6.1 %collective-permute-done.21.rest_4_ = bf16[1024,128]{1,0:T(8,128)(2,1)S(1)} collective-permute-done((bf16[1024,128]{1,0:T(8,128)(2,1)}, bf16[1024,128]{1,0:T(8,128)(2,1)S(1)}, u32[]{:S(2)}, u32[]{:S(2)}) %collective-permute-start.21) | collective-permute-done | bytes 262176 | tf_op jit(solution)/shard_map/ppermute | solution.py:27
  107.2 3.2 %collective-permute-start.20 = (bf16[1024,128]{1,0:T(8,128)(2,1)S(1)}, bf16[1024,128]{1,0:T(8,128)(2,1)S(1)}, u32[]{:S(2)}, u32[]{:S(2)}) collective-permute-start(bf16[1024,128]{1,0:T(8,128)(2,1)S(1)} %collective-permute-done.18.rest_1_), channel_id=1, source_target_pairs={{0,32},{16,48},{32,64},{48,80},{64,96},{80,112},{96,0},{112,16},{1... | collective-permute-start | bytes 786440 | tf_op jit(solution)/shard_map/ppermute | solution.py:27
  111.4 9.0 %collective-permute-done.22.rest_5_ = bf16[1024,128]{1,0:T(8,128)(2,1)S(1)} collective-permute-done((bf16[1024,128]{1,0:T(8,128)(2,1)S(1)}, bf16[1024,128]{1,0:T(8,128)(2,1)S(1)}, u32[]{:S(2)}, u32[]{:S(2)}) %collective-permute-start.22) | collective-permute-done | bytes 262176 | tf_op jit(solution)/shard_map/ppermute | solution.py:27
  121.3 9.8 %direct_sums.3 = (bf16[1024,128]{1,0:T(8,128)(2,1)S(1)}, bf16[1024,128]{1,0:T(8,128)(2,1)S(1)}, bf16[2048,128]{1,0:T(8,128)(2,1)S(1)}, bf16[1024,128]{1,0:T(8,12...) custom-call(s32[160]{0:T(256)S(1)} %iota.14.order, ...), custom_call_target="tpu_custom_call" | custom-call | flops 2684354560 | bytes 20971520 | tf_op jit(solution)/shard_map/direct_sums/pallas_call | solution.py:110
  131.3 4.7 %collective-permute-done.25 = bf16[8192,128]{1,0:T(8,128)(2,1)S(1)} collective-permute-done((bf16[8192,128]{1,0:T(8,128)(2,1)}, bf16[8192,128]{1,0:T(8,128)(2,1)S(1)}, u32[]{:S(2)}, u32[]{:S(2)}) %collective-permute-start.25) | collective-permute-done | bytes 2097184 | tf_op jit(solution)/shard_map/ppermute | solution.py:38
  137.3 3.2 %collective-permute-start.27 = (bf16[2048,128]{1,0:T(8,128)(2,1)}, bf16[2048,128]{1,0:T(8,128)(2,1)}, u32[]{:S(2)}, u32[]{:S(2)}) collective-permute-start(bf16[2048,128]{1,0:T(8,128)(2,1)} %get-tuple-element.83), channel_id=1, source_target_pairs={{0,12},{1,13},{2,14},{3,15},{4,0},{5,1},{6,2},{7,3},{8,4},{9,5},{1... | collective-permute-start | bytes 1572872 | tf_op jit(solution)/shard_map/ppermute | solution.py:38
  141.3 2.6 %collective-permute-start.28 = (bf16[1024,128]{1,0:T(8,128)(2,1)}, bf16[1024,128]{1,0:T(8,128)(2,1)}, u32[]{:S(2)}, u32[]{:S(2)}) collective-permute-start(bf16[1024,128]{1,0:T(8,128)(2,1)} %add_convert_fusion.8), channel_id=1, source_target_pairs={{0,2},{1,3},{2,0},{3,1},{4,6},{5,7},{6,4},{7,5},{8,10},{9,11},{10,... | collective-permute-start | bytes 786440 | tf_op jit(solution)/shard_map/ppermute | solution.py:38
  143.8 7.8 %mirror_sums.6 = (bf16[2048,128]{1,0:T(8,128)(2,1)}, bf16[2048,128]{1,0:T(8,128)(2,1)}, bf16[1024,128]{1,0:T(8,128)(2,1)}) custom-call(s32[160]{0:T(256)} %get-tuple-element.75.order, s32[160]{0:T(256)} %get-tuple-element.74.out_slot, s32[160]{0:T(256)} %get-tuple-element.73.in_slot, s32[2]{0:T(128)} %pad_add_fusion.bounds, bf16[160,256,256]{2,1,0:T(8,128)(2,1)} %tiles.11, ...), custom_call_target="tpu_custom_call" | custom-call | flops 2684354560 | bytes 20971520 | tf_op jit(solution)/shard_map/mirror_sums/pallas_call | solution.py:110
  153.8 2.1 %add_convert_fusion.7 = (bf16[1024,128]{1,0:T(8,128)(2,1)}, bf16[1024,128]{1,0:T(8,128)(2,1)S(1)}) fusion(bf16[1024,128]{1,0:T(8,128)(2,1)} %collective-permute-done.28, bf16[1024,128]{1,0:T(8,128)(2,1)S(1)} %get-tuple-element.60, bf16[8192,128]{1,0:T(8,128)(2,1)S(1)} %collective-permute-done.25, bf16[2048,128]{1,0:T(8,128)(2,1)} %collective-permute-done.27, ...), kind=kLoop, calls=%fused_computation.12 | loop fusion | flops 1835008 | bytes 2359296 | tf_op jit(solution)/shard_map/convert_element_type | solution.py:150
  156.5 4.1 %collective-permute-start.30 = (bf16[1024,128]{1,0:T(8,128)(2,1)S(1)}, bf16[1024,128]{1,0:T(8,128)(2,1)}, u32[]{:S(2)}, u32[]{:S(2)}) collective-permute-start(bf16[1024,128]{1,0:T(8,128)(2,1)S(1)} %get-tuple-element.81), channel_id=1, source_target_pairs={{0,2},{1,3},{2,0},{3,1},{4,6},{5,7},{6,4},{7,5},{8,10},{9,11},{10,... | collective-permute-start | bytes 786440 | tf_op jit(solution)/shard_map/ppermute | solution.py:38
  160.6 6.7 %mirror_sums.7 = (bf16[1024,128]{1,0:T(8,128)(2,1)}, bf16[1024,128]{1,0:T(8,128)(2,1)}, bf16[1024,128]{1,0:T(8,128)(2,1)}) custom-call(s32[160]{0:T(256)} %get-tuple-element.75.order, s32[160]{0:T(256)} %get-tuple-element.74.out_slot, s32[160]{0:T(256)} %get-tuple-element.73.in_slot, s32[2]{0:T(128)} %pad_add_fusion.2.bounds, bf16[160,256,256]{2,1,0:T(8,128)(2,1)} %tiles.11, ...), custom_call_target="tpu_custom_call" | custom-call | flops 2684354560 | bytes 20971520 | tf_op jit(solution)/shard_map/mirror_sums/pallas_call | solution.py:110
  171.4 5.2 %collective-permute-done.34 = bf16[1024,128]{1,0:T(8,128)(2,1)S(1)} collective-permute-done((bf16[1024,128]{1,0:T(8,128)(2,1)S(1)}, bf16[1024,128]{1,0:T(8,128)(2,1)S(1)}, u32[]{:S(2)}, u32[]{:S(2)}) %collective-permute-start.34) | collective-permute-done | bytes 262176 | tf_op jit(solution)/shard_map/ppermute | solution.py:27
  176.6 2.5 %collective-permute-done.35 = bf16[1024,128]{1,0:T(8,128)(2,1)S(1)} collective-permute-done((bf16[1024,128]{1,0:T(8,128)(2,1)S(1)}, bf16[1024,128]{1,0:T(8,128)(2,1)S(1)}, u32[]{:S(2)}, u32[]{:S(2)}) %collective-permute-start.35) | collective-permute-done | bytes 262176 | tf_op jit(solution)/shard_map/ppermute | solution.py:27
  179.1 2.7 %convert_subtract_fusion = f32[1024,128]{1,0:T(8,128)} fusion(bf16[1024,128]{1,0:T(8,128)(2,1)S(1)} %copy-done.1, bf16[1024,128]{1,0:T(8,128)(2,1)S(1)} %copy-done.3, bf16[1024,128]{1,0:T(8,128)(2,1)S(1)} %collective-permute-done.35, bf16[1024,128]{1,0:T(8,128)(2,1)S(1)} %collective-permute-done.34, bf16[1024,128]{1,0:T(8,128)(2,1)} %get-tuple-element.67, ...), kind=kLoop, calls=%fused_computation.4 | loop fusion | flops 3538944 | bytes 3932160 | tf_op jit(solution)/shard_map/sub | solution.py:222
  (85 shorter events, 33.6 us)
Async XLA Ops:
  6.5 51.6 %all-gather.3.cloned.1.call-start = ((), (), s32[]{:S(2)}) async-start(), calls=%async_computation | async-start | bytes 4456448 | tf_op jit(solution)/shard_map/all_gather | solution.py:142
  7.3 136.6 %all-gather.5.cloned.1.call-start = ((), (), s32[]{:S(2)}) async-start(), calls=%async_computation.1 | async-start | bytes 4456448 | tf_op jit(solution)/shard_map/all_gather | solution.py:142
  9.7 11.0 %collective-permute-start.3 = (bf16[1024,128]{1,0:T(8,128)(2,1)}, bf16[1024,128]{1,0:T(8,128)(2,1)S(1)}, u32[]{:S(2)}, u32[]{:S(2)}) collective-permute-start(bf16[1024,128]{1,0:T(8,128)(2,1)} %rest_0_.1), channel_id=1, source_target_pairs={{0,64},{16,80},{32,96},{48,112},{64,0},{80,16},{96,32},{112,48},{1... | collective-permute-start | bytes 786440 | tf_op jit(solution)/shard_map/ppermute | solution.py:27
  11.1 13.8 %collective-permute-start.5 = (bf16[1024,128]{1,0:T(8,128)(2,1)}, bf16[1024,128]{1,0:T(8,128)(2,1)S(1)}, u32[]{:S(2)}, u32[]{:S(2)}) collective-permute-start(bf16[1024,128]{1,0:T(8,128)(2,1)} %rest_0_.1), channel_id=1, source_target_pairs={{0,96},{16,112},{32,0},{48,16},{64,32},{80,48},{96,64},{112,80},{1... | collective-permute-start | bytes 786440 | tf_op jit(solution)/shard_map/ppermute | solution.py:27
  11.1 13.8 %collective-permute-start.1 = (bf16[1024,128]{1,0:T(8,128)(2,1)}, bf16[1024,128]{1,0:T(8,128)(2,1)S(1)}, u32[]{:S(2)}, u32[]{:S(2)}) collective-permute-start(bf16[1024,128]{1,0:T(8,128)(2,1)} %rest_0_.1), channel_id=1, source_target_pairs={{0,32},{16,48},{32,64},{48,80},{64,96},{80,112},{96,0},{112,16},{1... | collective-permute-start | bytes 786440 | tf_op jit(solution)/shard_map/ppermute | solution.py:27
  17.1 18.8 %collective-permute-start.6 = (bf16[1024,128]{1,0:T(8,128)(2,1)S(1)}, bf16[1024,128]{1,0:T(8,128)(2,1)S(1)}, u32[]{:S(2)}, u32[]{:S(2)}) collective-permute-start(bf16[1024,128]{1,0:T(8,128)(2,1)S(1)} %collective-permute-done.rest_1_), channel_id=1, source_target_pairs={{0,96},{16,112},{32,0},{48,16},{64,32},{80,48},{96,64},{112,80},{1... | collective-permute-start | bytes 786440 | tf_op jit(solution)/shard_map/ppermute | solution.py:27
  18.0 17.9 %collective-permute-start.2 = (bf16[1024,128]{1,0:T(8,128)(2,1)S(1)}, bf16[1024,128]{1,0:T(8,128)(2,1)S(1)}, u32[]{:S(2)}, u32[]{:S(2)}) collective-permute-start(bf16[1024,128]{1,0:T(8,128)(2,1)S(1)} %collective-permute-done.rest_1_), channel_id=1, source_target_pairs={{0,32},{16,48},{32,64},{48,80},{64,96},{80,112},{96,0},{112,16},{1... | collective-permute-start | bytes 786440 | tf_op jit(solution)/shard_map/ppermute | solution.py:27
  20.7 15.2 %collective-permute-start.4 = (bf16[1024,128]{1,0:T(8,128)(2,1)S(1)}, bf16[1024,128]{1,0:T(8,128)(2,1)S(1)}, u32[]{:S(2)}, u32[]{:S(2)}) collective-permute-start(bf16[1024,128]{1,0:T(8,128)(2,1)S(1)} %collective-permute-done.3.rest_4_), channel_id=1, source_target_pairs={{0,16},{16,0},{32,48},{48,32},{64,80},{80,64},{96,112},{112,96},{1... | collective-permute-start | bytes 786440 | tf_op jit(solution)/shard_map/ppermute | solution.py:27
  51.5 17.2 %collective-permute-start.8 = (bf16[2048,128]{1,0:T(8,128)(2,1)S(1)}, bf16[2048,128]{1,0:T(8,128)(2,1)S(1)}, u32[]{:S(2)}, u32[]{:S(2)}) collective-permute-start(bf16[2048,128]{1,0:T(8,128)(2,1)S(1)} %get-tuple-element.86), channel_id=1, source_target_pairs={{0,4},{1,5},{2,6},{3,7},{4,8},{5,9},{6,10},{7,11},{8,12},{9,13},{1... | collective-permute-start | bytes 1572872 | tf_op jit(solution)/shard_map/ppermute | solution.py:38
  51.6 17.1 %collective-permute-start.9 = (bf16[2048,128]{1,0:T(8,128)(2,1)S(1)}, bf16[2048,128]{1,0:T(8,128)(2,1)S(1)}, u32[]{:S(2)}, u32[]{:S(2)}) collective-permute-start(bf16[2048,128]{1,0:T(8,128)(2,1)S(1)} %get-tuple-element.87), channel_id=1, source_target_pairs={{0,12},{1,13},{2,14},{3,15},{4,0},{5,1},{6,2},{7,3},{8,4},{9,5},{1... | collective-permute-start | bytes 1572872 | tf_op jit(solution)/shard_map/ppermute | solution.py:38
  55.6 11.5 %collective-permute-start.10 = (bf16[1024,128]{1,0:T(8,128)(2,1)}, bf16[1024,128]{1,0:T(8,128)(2,1)S(1)}, u32[]{:S(2)}, u32[]{:S(2)}) collective-permute-start(bf16[1024,128]{1,0:T(8,128)(2,1)} %add_convert_fusion.13), channel_id=1, source_target_pairs={{0,2},{1,3},{2,0},{3,1},{4,6},{5,7},{6,4},{7,5},{8,10},{9,11},{10,... | collective-permute-start | bytes 786440 | tf_op jit(solution)/shard_map/ppermute | solution.py:38
  65.9 14.5 %collective-permute-start.15 = (bf16[1024,128]{1,0:T(8,128)(2,1)}, bf16[1024,128]{1,0:T(8,128)(2,1)S(1)}, u32[]{:S(2)}, u32[]{:S(2)}) collective-permute-start(bf16[1024,128]{1,0:T(8,128)(2,1)} %get-tuple-element.54), channel_id=1, source_target_pairs={{0,16},{16,0},{32,48},{48,32},{64,80},{80,64},{96,112},{112,96},{1... | collective-permute-start | bytes 786440 | tf_op jit(solution)/shard_map/ppermute | solution.py:27
  66.7 15.7 %collective-permute-start.13 = (bf16[2048,128]{1,0:T(8,128)(2,1)}, bf16[2048,128]{1,0:T(8,128)(2,1)S(1)}, u32[]{:S(2)}, u32[]{:S(2)}) collective-permute-start(bf16[2048,128]{1,0:T(8,128)(2,1)} %get-tuple-element.51), channel_id=1, source_target_pairs={{0,32},{16,48},{32,64},{48,80},{64,96},{80,112},{96,0},{112,16},{1... | collective-permute-start | bytes 1572872 | tf_op jit(solution)/shard_map/ppermute | solution.py:27
  67.1 15.3 %collective-permute-start.14 = (bf16[2048,128]{1,0:T(8,128)(2,1)}, bf16[2048,128]{1,0:T(8,128)(2,1)}, u32[]{:S(2)}, u32[]{:S(2)}) collective-permute-start(bf16[2048,128]{1,0:T(8,128)(2,1)} %get-tuple-element.52), channel_id=1, source_target_pairs={{0,96},{16,112},{32,0},{48,16},{64,32},{80,48},{96,64},{112,80},{1... | collective-permute-start | bytes 1572872 | tf_op jit(solution)/shard_map/ppermute | solution.py:27
  70.0 15.3 %collective-permute-start.11 = (bf16[1024,128]{1,0:T(8,128)(2,1)S(1)}, bf16[1024,128]{1,0:T(8,128)(2,1)S(1)}, u32[]{:S(2)}, u32[]{:S(2)}) collective-permute-start(bf16[1024,128]{1,0:T(8,128)(2,1)S(1)} %get-tuple-element.84), channel_id=1, source_target_pairs={{0,8},{1,9},{2,10},{3,11},{4,12},{5,13},{6,14},{7,15},{8,0},{9,1},... | collective-permute-start | bytes 786440 | tf_op jit(solution)/shard_map/ppermute | solution.py:38
  71.6 13.7 %collective-permute-start.12 = (bf16[1024,128]{1,0:T(8,128)(2,1)S(1)}, bf16[1024,128]{1,0:T(8,128)(2,1)S(1)}, u32[]{:S(2)}, u32[]{:S(2)}) collective-permute-start(bf16[1024,128]{1,0:T(8,128)(2,1)S(1)} %get-tuple-element.85), channel_id=1, source_target_pairs={{0,2},{1,3},{2,0},{3,1},{4,6},{5,7},{6,4},{7,5},{8,10},{9,11},{10,... | collective-permute-start | bytes 786440 | tf_op jit(solution)/shard_map/ppermute | solution.py:38
  83.6 10.3 %collective-permute-start.17 = (bf16[1024,128]{1,0:T(8,128)(2,1)S(1)}, bf16[1024,128]{1,0:T(8,128)(2,1)S(1)}, u32[]{:S(2)}, u32[]{:S(2)}) collective-permute-start(bf16[1024,128]{1,0:T(8,128)(2,1)S(1)} %add_convert_fusion.9), channel_id=1, source_target_pairs={{0,16},{16,0},{32,48},{48,32},{64,80},{80,64},{96,112},{112,96},{1... | collective-permute-start | bytes 786440 | tf_op jit(solution)/shard_map/ppermute | solution.py:27
  96.1 11.0 %collective-permute-start.21 = (bf16[1024,128]{1,0:T(8,128)(2,1)}, bf16[1024,128]{1,0:T(8,128)(2,1)S(1)}, u32[]{:S(2)}, u32[]{:S(2)}) collective-permute-start(bf16[1024,128]{1,0:T(8,128)(2,1)} %fusion.2.rest_0_), channel_id=1, source_target_pairs={{0,64},{16,80},{32,96},{48,112},{64,0},{80,16},{96,32},{112,48},{1... | collective-permute-start | bytes 786440 | tf_op jit(solution)/shard_map/ppermute | solution.py:27
  96.8 10.4 %collective-permute-start.18 = (bf16[1024,128]{1,0:T(8,128)(2,1)}, bf16[1024,128]{1,0:T(8,128)(2,1)S(1)}, u32[]{:S(2)}, u32[]{:S(2)}) collective-permute-start(bf16[1024,128]{1,0:T(8,128)(2,1)} %fusion.2.rest_0_), channel_id=1, source_target_pairs={{0,16},{16,0},{32,48},{48,32},{64,80},{80,64},{96,112},{112,96},{1... | collective-permute-start | bytes 786440 | tf_op jit(solution)/shard_map/ppermute | solution.py:27
  97.8 13.5 %collective-permute-start.23 = (bf16[1024,128]{1,0:T(8,128)(2,1)}, bf16[1024,128]{1,0:T(8,128)(2,1)S(1)}, u32[]{:S(2)}, u32[]{:S(2)}) collective-permute-start(bf16[1024,128]{1,0:T(8,128)(2,1)} %fusion.2.rest_0_), channel_id=1, source_target_pairs={{0,96},{16,112},{32,0},{48,16},{64,32},{80,48},{96,64},{112,80},{1... | collective-permute-start | bytes 786440 | tf_op jit(solution)/shard_map/ppermute | solution.py:27
  98.7 12.7 %collective-permute-start.19 = (bf16[1024,128]{1,0:T(8,128)(2,1)}, bf16[1024,128]{1,0:T(8,128)(2,1)S(1)}, u32[]{:S(2)}, u32[]{:S(2)}) collective-permute-start(bf16[1024,128]{1,0:T(8,128)(2,1)} %fusion.2.rest_0_), channel_id=1, source_target_pairs={{0,32},{16,48},{32,64},{48,80},{64,96},{80,112},{96,0},{112,16},{1... | collective-permute-start | bytes 786440 | tf_op jit(solution)/shard_map/ppermute | solution.py:27
  107.2 13.2 %collective-permute-start.22 = (bf16[1024,128]{1,0:T(8,128)(2,1)S(1)}, bf16[1024,128]{1,0:T(8,128)(2,1)S(1)}, u32[]{:S(2)}, u32[]{:S(2)}) collective-permute-start(bf16[1024,128]{1,0:T(8,128)(2,1)S(1)} %collective-permute-done.21.rest_4_), channel_id=1, source_target_pairs={{0,16},{16,0},{32,48},{48,32},{64,80},{80,64},{96,112},{112,96},{1... | collective-permute-start | bytes 786440 | tf_op jit(solution)/shard_map/ppermute | solution.py:27
  107.2 13.2 %collective-permute-start.24 = (bf16[1024,128]{1,0:T(8,128)(2,1)S(1)}, bf16[1024,128]{1,0:T(8,128)(2,1)S(1)}, u32[]{:S(2)}, u32[]{:S(2)}) collective-permute-start(bf16[1024,128]{1,0:T(8,128)(2,1)S(1)} %collective-permute-done.18.rest_1_), channel_id=1, source_target_pairs={{0,96},{16,112},{32,0},{48,16},{64,32},{80,48},{96,64},{112,80},{1... | collective-permute-start | bytes 786440 | tf_op jit(solution)/shard_map/ppermute | solution.py:27
  107.2 13.2 %collective-permute-start.20 = (bf16[1024,128]{1,0:T(8,128)(2,1)S(1)}, bf16[1024,128]{1,0:T(8,128)(2,1)S(1)}, u32[]{:S(2)}, u32[]{:S(2)}) collective-permute-start(bf16[1024,128]{1,0:T(8,128)(2,1)S(1)} %collective-permute-done.18.rest_1_), channel_id=1, source_target_pairs={{0,32},{16,48},{32,64},{48,80},{64,96},{80,112},{96,0},{112,16},{1... | collective-permute-start | bytes 786440 | tf_op jit(solution)/shard_map/ppermute | solution.py:27
  137.3 16.5 %collective-permute-start.26 = (bf16[2048,128]{1,0:T(8,128)(2,1)}, bf16[2048,128]{1,0:T(8,128)(2,1)}, u32[]{:S(2)}, u32[]{:S(2)}) collective-permute-start(bf16[2048,128]{1,0:T(8,128)(2,1)} %get-tuple-element.82), channel_id=1, source_target_pairs={{0,4},{1,5},{2,6},{3,7},{4,8},{5,9},{6,10},{7,11},{8,12},{9,13},{1... | collective-permute-start | bytes 1572872 | tf_op jit(solution)/shard_map/ppermute | solution.py:38
  137.3 16.5 %collective-permute-start.27 = (bf16[2048,128]{1,0:T(8,128)(2,1)}, bf16[2048,128]{1,0:T(8,128)(2,1)}, u32[]{:S(2)}, u32[]{:S(2)}) collective-permute-start(bf16[2048,128]{1,0:T(8,128)(2,1)} %get-tuple-element.83), channel_id=1, source_target_pairs={{0,12},{1,13},{2,14},{3,15},{4,0},{5,1},{6,2},{7,3},{8,4},{9,5},{1... | collective-permute-start | bytes 1572872 | tf_op jit(solution)/shard_map/ppermute | solution.py:38
  141.3 11.7 %collective-permute-start.28 = (bf16[1024,128]{1,0:T(8,128)(2,1)}, bf16[1024,128]{1,0:T(8,128)(2,1)}, u32[]{:S(2)}, u32[]{:S(2)}) collective-permute-start(bf16[1024,128]{1,0:T(8,128)(2,1)} %add_convert_fusion.8), channel_id=1, source_target_pairs={{0,2},{1,3},{2,0},{3,1},{4,6},{5,7},{6,4},{7,5},{8,10},{9,11},{10,... | collective-permute-start | bytes 786440 | tf_op jit(solution)/shard_map/ppermute | solution.py:38
  151.6 15.7 %collective-permute-start.33 = (bf16[1024,128]{1,0:T(8,128)(2,1)}, bf16[1024,128]{1,0:T(8,128)(2,1)S(1)}, u32[]{:S(2)}, u32[]{:S(2)}) collective-permute-start(bf16[1024,128]{1,0:T(8,128)(2,1)} %get-tuple-element.71), channel_id=1, source_target_pairs={{0,16},{16,0},{32,48},{48,32},{64,80},{80,64},{96,112},{112,96},{1... | collective-permute-start | bytes 786440 | tf_op jit(solution)/shard_map/ppermute | solution.py:27
  151.7 18.2 %collective-permute-start.31 = (bf16[2048,128]{1,0:T(8,128)(2,1)}, bf16[2048,128]{1,0:T(8,128)(2,1)}, u32[]{:S(2)}, u32[]{:S(2)}) collective-permute-start(bf16[2048,128]{1,0:T(8,128)(2,1)} %get-tuple-element.68), channel_id=1, source_target_pairs={{0,32},{16,48},{32,64},{48,80},{64,96},{80,112},{96,0},{112,16},{1... | collective-permute-start | bytes 1572872 | tf_op jit(solution)/shard_map/ppermute | solution.py:27
  152.9 17.0 %collective-permute-start.32 = (bf16[2048,128]{1,0:T(8,128)(2,1)}, bf16[2048,128]{1,0:T(8,128)(2,1)}, u32[]{:S(2)}, u32[]{:S(2)}) collective-permute-start(bf16[2048,128]{1,0:T(8,128)(2,1)} %get-tuple-element.69), channel_id=1, source_target_pairs={{0,96},{16,112},{32,0},{48,16},{64,32},{80,48},{96,64},{112,80},{1... | collective-permute-start | bytes 1572872 | tf_op jit(solution)/shard_map/ppermute | solution.py:27
  155.9 15.5 %collective-permute-start.29 = (bf16[1024,128]{1,0:T(8,128)(2,1)}, bf16[1024,128]{1,0:T(8,128)(2,1)}, u32[]{:S(2)}, u32[]{:S(2)}) collective-permute-start(bf16[1024,128]{1,0:T(8,128)(2,1)} %get-tuple-element.80), channel_id=1, source_target_pairs={{0,8},{1,9},{2,10},{3,11},{4,12},{5,13},{6,14},{7,15},{8,0},{9,1},... | collective-permute-start | bytes 786440 | tf_op jit(solution)/shard_map/ppermute | solution.py:38
  156.5 14.9 %collective-permute-start.30 = (bf16[1024,128]{1,0:T(8,128)(2,1)S(1)}, bf16[1024,128]{1,0:T(8,128)(2,1)}, u32[]{:S(2)}, u32[]{:S(2)}) collective-permute-start(bf16[1024,128]{1,0:T(8,128)(2,1)S(1)} %get-tuple-element.81), channel_id=1, source_target_pairs={{0,2},{1,3},{2,0},{3,1},{4,6},{5,7},{6,4},{7,5},{8,10},{9,11},{10,... | collective-permute-start | bytes 786440 | tf_op jit(solution)/shard_map/ppermute | solution.py:38
  (12 other events, 104.4 us)
Sparse Core Ops, SparseCore 0:
  9.1 43.5 all-gather.2
  96.3 41.6 all-gather.4

commit v5 on v2

--- a/solution.py
+++ b/solution.py
@@ -14,7 +14,7 @@
 NV = 128
 OWN = 4
 CHUNK = 16
-RING = 3
+RING = 4
 LIMIT = {False: 48, True: 60}
 
 ROW_STEPS = [(dx, dy) for dx in range(4) for dy in range(2)]

time: 189 us -> 190 us (level)
    ppermute x12, starting transfers between devices: 17.7 us -> 21.8 us  [send_col(): return lax.ppermute(value, 'col', pairs)]
    ppermute x24, starting transfers between devices: 59.6 us -> 55.7 us  [send_row(): return lax.ppermute(value, 'row', pairs)]
  transfers between devices with their start and end apart: 38 -> 38, of which waited for: 11 -> 13; matrix products, arithmetic and copies ran while one was open for 4% -> 4% of each run, Pallas kernels for 18% -> 18%
where the time goes in v5:
time: 190 us; the launch traced here: 189 us
  starting transfers between devices  77.5 us (41%)
  waiting for transfers between devices  49.3 us (26%)
  Pallas kernels  34.1 us (18%)
  between operations  14.3 us (8%)
  other arithmetic  12.2 us (6%)
  local copies, waits for them, and re-layouts  1.95 us (1%)
    ppermute x24, starting transfers between devices, send_row(): return lax.ppermute(value, 'row', pairs)  55.7 us
    ppermute x24, waiting for transfers between devices, send_row(): return lax.ppermute(value, 'row', pairs)  39.8 us
    pallas_call x4, Pallas kernels, spmv(): pl.pallas_call(functools.partial(spmv_kernel, mirror, n_in, n_out), in_sp...  34.1 us
    ppermute x12, starting transfers between devices, send_col(): return lax.ppermute(value, 'col', pairs)  21.8 us
    ppermute x12, waiting for transfers between devices, send_col(): return lax.ppermute(value, 'col', pairs)  8.74 us
    convert_element_type x10, other arithmetic, rounded(): return parts[0] if len(parts) == 1 else total(parts).astype(jnp.bfloat16)  6.46 us
  transfers between devices with their start and end apart: 38, of which 13 were waited for; matrix products, arithmetic and copies ran while one was open for 4% of the time, Pallas kernels for 18%

profile of v5, /device:TPU:14, one launch (start us, length us, event | category | flops | bytes accessed | tf_op | source)
XLA Modules:
  0.0 189.4 jit_solution(6942568848416488148)
XLA Ops:
  8.8 2.3 %collective-permute-start = (bf16[1024,128]{1,0:T(8,128)(2,1)}, bf16[1024,128]{1,0:T(8,128)(2,1)S(1)}, u32[]{:S(2)}, u32[]{:S(2)}) collective-permute-start(bf16[1024,128]{1,0:T(8,128)(2,1)} %rest_0_.1), channel_id=1, source_target_pairs={{0,16},{16,0},{32,48},{48,32},{64,80},{80,64},{96,112},{112,96},{1... | collective-permute-start | bytes 786440 | tf_op jit(solution)/shard_map/ppermute | solution.py:27
  11.1 3.2 %collective-permute-start.1 = (bf16[1024,128]{1,0:T(8,128)(2,1)}, bf16[1024,128]{1,0:T(8,128)(2,1)S(1)}, u32[]{:S(2)}, u32[]{:S(2)}) collective-permute-start(bf16[1024,128]{1,0:T(8,128)(2,1)} %rest_0_.1), channel_id=1, source_target_pairs={{0,32},{16,48},{32,64},{48,80},{64,96},{80,112},{96,0},{112,16},{1... | collective-permute-start | bytes 786440 | tf_op jit(solution)/shard_map/ppermute | solution.py:27
  14.3 4.0 %collective-permute-done.3.rest_4_ = bf16[1024,128]{1,0:T(8,128)(2,1)S(1)} collective-permute-done((bf16[1024,128]{1,0:T(8,128)(2,1)}, bf16[1024,128]{1,0:T(8,128)(2,1)S(1)}, u32[]{:S(2)}, u32[]{:S(2)}) %collective-permute-start.3) | collective-permute-done | bytes 262176 | tf_op jit(solution)/shard_map/ppermute | solution.py:27
  18.3 2.3 %collective-permute-start.4 = (bf16[1024,128]{1,0:T(8,128)(2,1)S(1)}, bf16[1024,128]{1,0:T(8,128)(2,1)S(1)}, u32[]{:S(2)}, u32[]{:S(2)}) collective-permute-start(bf16[1024,128]{1,0:T(8,128)(2,1)S(1)} %collective-permute-done.3.rest_4_), channel_id=1, source_target_pairs={{0,16},{16,0},{32,48},{48,32},{64,80},{80,64},{96,112},{112,96},{1... | collective-permute-start | bytes 786440 | tf_op jit(solution)/shard_map/ppermute | solution.py:27
  21.5 2.4 %collective-permute-start.2 = (bf16[1024,128]{1,0:T(8,128)(2,1)S(1)}, bf16[1024,128]{1,0:T(8,128)(2,1)S(1)}, u32[]{:S(2)}, u32[]{:S(2)}) collective-permute-start(bf16[1024,128]{1,0:T(8,128)(2,1)S(1)} %collective-permute-done.rest_1_), channel_id=1, source_target_pairs={{0,32},{16,48},{32,64},{48,80},{64,96},{80,112},{96,0},{112,16},{1... | collective-permute-start | bytes 786440 | tf_op jit(solution)/shard_map/ppermute | solution.py:27
  25.9 5.7 %collective-permute-done.4.rest_5_ = bf16[1024,128]{1,0:T(8,128)(2,1)S(1)} collective-permute-done((bf16[1024,128]{1,0:T(8,128)(2,1)S(1)}, bf16[1024,128]{1,0:T(8,128)(2,1)S(1)}, u32[]{:S(2)}, u32[]{:S(2)}) %collective-permute-start.4) | collective-permute-done | bytes 262176 | tf_op jit(solution)/shard_map/ppermute | solution.py:27
  32.6 7.7 %direct_sums.2 = (bf16[1024,128]{1,0:T(8,128)(2,1)S(1)}, bf16[1024,128]{1,0:T(8,128)(2,1)S(1)}, bf16[2048,128]{1,0:T(8,128)(2,1)S(1)}, bf16[1024,128]{1,0:T(8,12...) custom-call(s32[160]{0:T(256)S(1)} %get-tuple-element.67.out_slot, ...), custom_call_target="tpu_custom_call" | custom-call | flops 2684354560 | bytes 20971520 | tf_op jit(solution)/shard_map/direct_sums/pallas_call | solution.py:99
  40.4 4.4 %collective-permute-done.7 = bf16[8192,128]{1,0:T(8,128)(2,1)S(1)} collective-permute-done((bf16[8192,128]{1,0:T(8,128)(2,1)}, bf16[8192,128]{1,0:T(8,128)(2,1)S(1)}, u32[]{:S(2)}, u32[]{:S(2)}) %collective-permute-start.7) | collective-permute-done | bytes 2097184 | tf_op jit(solution)/shard_map/ppermute | solution.py:38
  46.1 8.2 %collective-permute-start.9 = (bf16[2048,128]{1,0:T(8,128)(2,1)S(1)}, bf16[2048,128]{1,0:T(8,128)(2,1)S(1)}, u32[]{:S(2)}, u32[]{:S(2)}) collective-permute-start(bf16[2048,128]{1,0:T(8,128)(2,1)S(1)} %get-tuple-element.64), channel_id=1, source_target_pairs={{0,12},{1,13},{2,14},{3,15},{4,0},{5,1},{6,2},{7,3},{8,4},{9,5},{1... | collective-permute-start | bytes 1572872 | tf_op jit(solution)/shard_map/ppermute | solution.py:38
  54.5 9.3 %mirror_sums.2 = (bf16[1024,128]{1,0:T(8,128)(2,1)}, bf16[1024,128]{1,0:T(8,128)(2,1)}, bf16[2048,128]{1,0:T(8,128)(2,1)}, bf16[1024,128]{1,0:T(8,128)(2,1)}, bf...) custom-call(s32[160]{0:T(256)} %get-tuple-element.69.out_slot, s32[160]{0:T(256)} %get-tuple-element.68.in_slot, ...), custom_call_target="tpu_custom_call" | custom-call | flops 2684354560 | bytes 20971520 | tf_op jit(solution)/shard_map/mirror_sums/pallas_call | solution.py:99
  64.0 2.0 %collective-permute-start.14 = (bf16[2048,128]{1,0:T(8,128)(2,1)}, bf16[2048,128]{1,0:T(8,128)(2,1)S(1)}, u32[]{:S(2)}, u32[]{:S(2)}) collective-permute-start(bf16[2048,128]{1,0:T(8,128)(2,1)} %get-tuple-element.40), channel_id=1, source_target_pairs={{0,96},{16,112},{32,0},{48,16},{64,32},{80,48},{96,64},{112,80},{1... | collective-permute-start | bytes 1572872 | tf_op jit(solution)/shard_map/ppermute | solution.py:27
  66.0 3.8 %collective-permute-start.15 = (bf16[1024,128]{1,0:T(8,128)(2,1)}, bf16[1024,128]{1,0:T(8,128)(2,1)S(1)}, u32[]{:S(2)}, u32[]{:S(2)}) collective-permute-start(bf16[1024,128]{1,0:T(8,128)(2,1)} %get-tuple-element.42), channel_id=1, source_target_pairs={{0,16},{16,0},{32,48},{48,32},{64,80},{80,64},{96,112},{112,96},{1... | collective-permute-start | bytes 786440 | tf_op jit(solution)/shard_map/ppermute | solution.py:27
  73.2 3.9 %collective-permute-done.15 = bf16[1024,128]{1,0:T(8,128)(2,1)S(1)} collective-permute-done((bf16[1024,128]{1,0:T(8,128)(2,1)}, bf16[1024,128]{1,0:T(8,128)(2,1)S(1)}, u32[]{:S(2)}, u32[]{:S(2)}) %collective-permute-start.15) | collective-permute-done | bytes 262176 | tf_op jit(solution)/shard_map/ppermute | solution.py:27
  80.0 5.7 %collective-permute-start.17 = (bf16[1024,128]{1,0:T(8,128)(2,1)S(1)}, bf16[1024,128]{1,0:T(8,128)(2,1)S(1)}, u32[]{:S(2)}, u32[]{:S(2)}) collective-permute-start(bf16[1024,128]{1,0:T(8,128)(2,1)S(1)} %add_convert_fusion.9), channel_id=1, source_target_pairs={{0,16},{16,0},{32,48},{48,32},{64,80},{80,64},{96,112},{112,96},{1... | collective-permute-start | bytes 786440 | tf_op jit(solution)/shard_map/ppermute | solution.py:27
  86.4 3.6 %collective-permute-done.17 = bf16[1024,128]{1,0:T(8,128)(2,1)S(1)} collective-permute-done((bf16[1024,128]{1,0:T(8,128)(2,1)S(1)}, bf16[1024,128]{1,0:T(8,128)(2,1)S(1)}, u32[]{:S(2)}, u32[]{:S(2)}) %collective-permute-start.17) | collective-permute-done | bytes 262176 | tf_op jit(solution)/shard_map/ppermute | solution.py:27
  90.0 2.1 %fusion.2.rest_0_ = bf16[1024,128]{1,0:T(8,128)(2,1)} fusion(bf16[1024,128]{1,0:T(8,128)(2,1)S(1)} %copy-done.1, bf16[1024,128]{1,0:T(8,128)(2,1)S(1)} %collective-permute-done.17, bf16[1024,128]{1,0:T(8,128)(2,1)S(1)} %collective-permute-done.16, bf16[1024,128]{1,0:T(8,128)(2,1)S(1)} %copy-done.9, bf16[1024,128]{1,0:T(8,128)(2,1)S(1)} %collective-permute-done.12, ...), kind=kLoop, calls=%fused_computation.8 | loop fusion | flops 3407872 | bytes 3407872 | tf_op jit(solution)/shard_map/convert_element_type | solution.py:187
  93.1 2.8 %collective-permute-start.18 = (bf16[1024,128]{1,0:T(8,128)(2,1)}, bf16[1024,128]{1,0:T(8,128)(2,1)S(1)}, u32[]{:S(2)}, u32[]{:S(2)}) collective-permute-start(bf16[1024,128]{1,0:T(8,128)(2,1)} %fusion.2.rest_0_), channel_id=1, source_target_pairs={{0,16},{16,0},{32,48},{48,32},{64,80},{80,64},{96,112},{112,96},{1... | collective-permute-start | bytes 786440 | tf_op jit(solution)/shard_map/ppermute | solution.py:27
  96.3 2.8 %collective-permute-start.19 = (bf16[1024,128]{1,0:T(8,128)(2,1)}, bf16[1024,128]{1,0:T(8,128)(2,1)S(1)}, u32[]{:S(2)}, u32[]{:S(2)}) collective-permute-start(bf16[1024,128]{1,0:T(8,128)(2,1)} %fusion.2.rest_0_), channel_id=1, source_target_pairs={{0,32},{16,48},{32,64},{48,80},{64,96},{80,112},{96,0},{112,16},{1... | collective-permute-start | bytes 786440 | tf_op jit(solution)/shard_map/ppermute | solution.py:27
  99.1 3.3 %collective-permute-done.21.rest_4_ = bf16[1024,128]{1,0:T(8,128)(2,1)S(1)} collective-permute-done((bf16[1024,128]{1,0:T(8,128)(2,1)}, bf16[1024,128]{1,0:T(8,128)(2,1)S(1)}, u32[]{:S(2)}, u32[]{:S(2)}) %collective-permute-start.21) | collective-permute-done | bytes 262176 | tf_op jit(solution)/shard_map/ppermute | solution.py:27
  102.4 3.8 %collective-permute-start.22 = (bf16[1024,128]{1,0:T(8,128)(2,1)S(1)}, bf16[1024,128]{1,0:T(8,128)(2,1)S(1)}, u32[]{:S(2)}, u32[]{:S(2)}) collective-permute-start(bf16[1024,128]{1,0:T(8,128)(2,1)S(1)} %collective-permute-done.21.rest_4_), channel_id=1, source_target_pairs={{0,16},{16,0},{32,48},{48,32},{64,80},{80,64},{96,112},{112,96},{1... | collective-permute-start | bytes 786440 | tf_op jit(solution)/shard_map/ppermute | solution.py:27
  106.2 3.2 %collective-permute-start.20 = (bf16[1024,128]{1,0:T(8,128)(2,1)S(1)}, bf16[1024,128]{1,0:T(8,128)(2,1)S(1)}, u32[]{:S(2)}, u32[]{:S(2)}) collective-permute-start(bf16[1024,128]{1,0:T(8,128)(2,1)S(1)} %collective-permute-done.18.rest_1_), channel_id=1, source_target_pairs={{0,32},{16,48},{32,64},{48,80},{64,96},{80,112},{96,0},{112,16},{1... | collective-permute-start | bytes 786440 | tf_op jit(solution)/shard_map/ppermute | solution.py:27
  109.5 5.9 %collective-permute-done.22.rest_5_ = bf16[1024,128]{1,0:T(8,128)(2,1)S(1)} collective-permute-done((bf16[1024,128]{1,0:T(8,128)(2,1)S(1)}, bf16[1024,128]{1,0:T(8,128)(2,1)S(1)}, u32[]{:S(2)}, u32[]{:S(2)}) %collective-permute-start.22) | collective-permute-done | bytes 262176 | tf_op jit(solution)/shard_map/ppermute | solution.py:27
  116.3 7.7 %direct_sums.3 = (bf16[1024,128]{1,0:T(8,128)(2,1)S(1)}, bf16[1024,128]{1,0:T(8,128)(2,1)S(1)}, bf16[2048,128]{1,0:T(8,128)(2,1)S(1)}, bf16[1024,128]{1,0:T(8,12...) custom-call(s32[160]{0:T(256)S(1)} %get-tuple-element.67.out_slot, ...), custom_call_target="tpu_custom_call" | custom-call | flops 2684354560 | bytes 20971520 | tf_op jit(solution)/shard_map/direct_sums/pallas_call | solution.py:99
  124.1 4.4 %collective-permute-done.25 = bf16[8192,128]{1,0:T(8,128)(2,1)S(1)} collective-permute-done((bf16[8192,128]{1,0:T(8,128)(2,1)}, bf16[8192,128]{1,0:T(8,128)(2,1)S(1)}, u32[]{:S(2)}, u32[]{:S(2)}) %collective-permute-start.25) | collective-permute-done | bytes 2097184 | tf_op jit(solution)/shard_map/ppermute | solution.py:38
  133.7 7.9 %collective-permute-start.28 = (bf16[1024,128]{1,0:T(8,128)(2,1)}, bf16[1024,128]{1,0:T(8,128)(2,1)S(1)}, u32[]{:S(2)}, u32[]{:S(2)}) collective-permute-start(bf16[1024,128]{1,0:T(8,128)(2,1)} %add_convert_fusion.8), channel_id=1, source_target_pairs={{0,2},{1,3},{2,0},{3,1},{4,6},{5,7},{6,4},{7,5},{8,10},{9,11},{10,... | collective-permute-start | bytes 786440 | tf_op jit(solution)/shard_map/ppermute | solution.py:38
  141.6 9.3 %mirror_sums.3 = (bf16[1024,128]{1,0:T(8,128)(2,1)}, bf16[1024,128]{1,0:T(8,128)(2,1)}, bf16[2048,128]{1,0:T(8,128)(2,1)}, bf16[1024,128]{1,0:T(8,128)(2,1)}, bf...) custom-call(s32[160]{0:T(256)} %get-tuple-element.69.out_slot, s32[160]{0:T(256)} %get-tuple-element.68.in_slot, ...), custom_call_target="tpu_custom_call" | custom-call | flops 2684354560 | bytes 20971520 | tf_op jit(solution)/shard_map/mirror_sums/pallas_call | solution.py:99
  152.1 2.6 %collective-permute-start.32 = (bf16[2048,128]{1,0:T(8,128)(2,1)}, bf16[2048,128]{1,0:T(8,128)(2,1)S(1)}, u32[]{:S(2)}, u32[]{:S(2)}) collective-permute-start(bf16[2048,128]{1,0:T(8,128)(2,1)} %get-tuple-element.53), channel_id=1, source_target_pairs={{0,96},{16,112},{32,0},{48,16},{64,32},{80,48},{96,64},{112,80},{1... | collective-permute-start | bytes 1572872 | tf_op jit(solution)/shard_map/ppermute | solution.py:27
  154.8 5.5 %collective-permute-start.33 = (bf16[1024,128]{1,0:T(8,128)(2,1)}, bf16[1024,128]{1,0:T(8,128)(2,1)S(1)}, u32[]{:S(2)}, u32[]{:S(2)}) collective-permute-start(bf16[1024,128]{1,0:T(8,128)(2,1)} %get-tuple-element.55), channel_id=1, source_target_pairs={{0,16},{16,0},{32,48},{48,32},{64,80},{80,64},{96,112},{112,96},{1... | collective-permute-start | bytes 786440 | tf_op jit(solution)/shard_map/ppermute | solution.py:27
  161.8 5.9 %collective-permute-done.33 = bf16[1024,128]{1,0:T(8,128)(2,1)S(1)} collective-permute-done((bf16[1024,128]{1,0:T(8,128)(2,1)}, bf16[1024,128]{1,0:T(8,128)(2,1)S(1)}, u32[]{:S(2)}, u32[]{:S(2)}) %collective-permute-start.33) | collective-permute-done | bytes 262176 | tf_op jit(solution)/shard_map/ppermute | solution.py:27
  169.7 6.2 %collective-permute-start.35 = (bf16[1024,128]{1,0:T(8,128)(2,1)S(1)}, bf16[1024,128]{1,0:T(8,128)(2,1)S(1)}, u32[]{:S(2)}, u32[]{:S(2)}) collective-permute-start(bf16[1024,128]{1,0:T(8,128)(2,1)S(1)} %add_convert_fusion.4), channel_id=1, source_target_pairs={{0,16},{16,0},{32,48},{48,32},{64,80},{80,64},{96,112},{112,96},{1... | collective-permute-start | bytes 786440 | tf_op jit(solution)/shard_map/ppermute | solution.py:27
  175.9 4.3 %collective-permute-done.35 = bf16[1024,128]{1,0:T(8,128)(2,1)S(1)} collective-permute-done((bf16[1024,128]{1,0:T(8,128)(2,1)S(1)}, bf16[1024,128]{1,0:T(8,128)(2,1)S(1)}, u32[]{:S(2)}, u32[]{:S(2)}) %collective-permute-start.35) | collective-permute-done | bytes 262176 | tf_op jit(solution)/shard_map/ppermute | solution.py:27
  180.2 2.3 %convert_subtract_fusion = f32[1024,128]{1,0:T(8,128)} fusion(bf16[1024,128]{1,0:T(8,128)(2,1)S(1)} %copy-done.1, bf16[1024,128]{1,0:T(8,128)(2,1)S(1)} %copy-done.3, bf16[1024,128]{1,0:T(8,128)(2,1)S(1)} %collective-permute-done.35, bf16[1024,128]{1,0:T(8,128)(2,1)S(1)} %collective-permute-done.34, bf16[1024,128]{1,0:T(8,128)(2,1)S(1)} %copy-done.10, ...), kind=kLoop, calls=%fused_computation.4 | loop fusion | flops 3538944 | bytes 3932160 | tf_op jit(solution)/shard_map/sub | solution.py:189
  (85 shorter events, 26.4 us)
Async XLA Ops:
  6.5 48.0 %all-gather.3.cloned.1.call-start = ((), (), s32[]{:S(2)}) async-start(), calls=%async_computation | async-start | bytes 4456448 | tf_op jit(solution)/shard_map/all_gather | solution.py:131
  7.3 134.4 %all-gather.5.cloned.1.call-start = ((), (), s32[]{:S(2)}) async-start(), calls=%async_computation.1 | async-start | bytes 4456448 | tf_op jit(solution)/shard_map/all_gather | solution.py:131
  7.3 11.0 %collective-permute-start.3 = (bf16[1024,128]{1,0:T(8,128)(2,1)}, bf16[1024,128]{1,0:T(8,128)(2,1)S(1)}, u32[]{:S(2)}, u32[]{:S(2)}) collective-permute-start(bf16[1024,128]{1,0:T(8,128)(2,1)} %rest_0_.1), channel_id=1, source_target_pairs={{0,64},{16,80},{32,96},{48,112},{64,0},{80,16},{96,32},{112,48},{1... | collective-permute-start | bytes 786440 | tf_op jit(solution)/shard_map/ppermute | solution.py:27
  8.8 11.8 %collective-permute-start = (bf16[1024,128]{1,0:T(8,128)(2,1)}, bf16[1024,128]{1,0:T(8,128)(2,1)S(1)}, u32[]{:S(2)}, u32[]{:S(2)}) collective-permute-start(bf16[1024,128]{1,0:T(8,128)(2,1)} %rest_0_.1), channel_id=1, source_target_pairs={{0,16},{16,0},{32,48},{48,32},{64,80},{80,64},{96,112},{112,96},{1... | collective-permute-start | bytes 786440 | tf_op jit(solution)/shard_map/ppermute | solution.py:27
  11.1 14.8 %collective-permute-start.5 = (bf16[1024,128]{1,0:T(8,128)(2,1)}, bf16[1024,128]{1,0:T(8,128)(2,1)S(1)}, u32[]{:S(2)}, u32[]{:S(2)}) collective-permute-start(bf16[1024,128]{1,0:T(8,128)(2,1)} %rest_0_.1), channel_id=1, source_target_pairs={{0,96},{16,112},{32,0},{48,16},{64,32},{80,48},{96,64},{112,80},{1... | collective-permute-start | bytes 786440 | tf_op jit(solution)/shard_map/ppermute | solution.py:27
  11.1 14.8 %collective-permute-start.1 = (bf16[1024,128]{1,0:T(8,128)(2,1)}, bf16[1024,128]{1,0:T(8,128)(2,1)S(1)}, u32[]{:S(2)}, u32[]{:S(2)}) collective-permute-start(bf16[1024,128]{1,0:T(8,128)(2,1)} %rest_0_.1), channel_id=1, source_target_pairs={{0,32},{16,48},{32,64},{48,80},{64,96},{80,112},{96,0},{112,16},{1... | collective-permute-start | bytes 786440 | tf_op jit(solution)/shard_map/ppermute | solution.py:27
  18.3 13.3 %collective-permute-start.4 = (bf16[1024,128]{1,0:T(8,128)(2,1)S(1)}, bf16[1024,128]{1,0:T(8,128)(2,1)S(1)}, u32[]{:S(2)}, u32[]{:S(2)}) collective-permute-start(bf16[1024,128]{1,0:T(8,128)(2,1)S(1)} %collective-permute-done.3.rest_4_), channel_id=1, source_target_pairs={{0,16},{16,0},{32,48},{48,32},{64,80},{80,64},{96,112},{112,96},{1... | collective-permute-start | bytes 786440 | tf_op jit(solution)/shard_map/ppermute | solution.py:27
  20.6 11.0 %collective-permute-start.6 = (bf16[1024,128]{1,0:T(8,128)(2,1)S(1)}, bf16[1024,128]{1,0:T(8,128)(2,1)S(1)}, u32[]{:S(2)}, u32[]{:S(2)}) collective-permute-start(bf16[1024,128]{1,0:T(8,128)(2,1)S(1)} %collective-permute-done.rest_1_), channel_id=1, source_target_pairs={{0,96},{16,112},{32,0},{48,16},{64,32},{80,48},{96,64},{112,80},{1... | collective-permute-start | bytes 786440 | tf_op jit(solution)/shard_map/ppermute | solution.py:27
  21.5 10.1 %collective-permute-start.2 = (bf16[1024,128]{1,0:T(8,128)(2,1)S(1)}, bf16[1024,128]{1,0:T(8,128)(2,1)S(1)}, u32[]{:S(2)}, u32[]{:S(2)}) collective-permute-start(bf16[1024,128]{1,0:T(8,128)(2,1)S(1)} %collective-permute-done.rest_1_), channel_id=1, source_target_pairs={{0,32},{16,48},{32,64},{48,80},{64,96},{80,112},{96,0},{112,16},{1... | collective-permute-start | bytes 786440 | tf_op jit(solution)/shard_map/ppermute | solution.py:27
  46.1 23.7 %collective-permute-start.8 = (bf16[2048,128]{1,0:T(8,128)(2,1)}, bf16[2048,128]{1,0:T(8,128)(2,1)S(1)}, u32[]{:S(2)}, u32[]{:S(2)}) collective-permute-start(bf16[2048,128]{1,0:T(8,128)(2,1)} %get-tuple-element.63), channel_id=1, source_target_pairs={{0,4},{1,5},{2,6},{3,7},{4,8},{5,9},{6,10},{7,11},{8,12},{9,13},{1... | collective-permute-start | bytes 1572872 | tf_op jit(solution)/shard_map/ppermute | solution.py:38
  46.1 23.7 %collective-permute-start.9 = (bf16[2048,128]{1,0:T(8,128)(2,1)S(1)}, bf16[2048,128]{1,0:T(8,128)(2,1)S(1)}, u32[]{:S(2)}, u32[]{:S(2)}) collective-permute-start(bf16[2048,128]{1,0:T(8,128)(2,1)S(1)} %get-tuple-element.64), channel_id=1, source_target_pairs={{0,12},{1,13},{2,14},{3,15},{4,0},{5,1},{6,2},{7,3},{8,4},{9,5},{1... | collective-permute-start | bytes 1572872 | tf_op jit(solution)/shard_map/ppermute | solution.py:38
  54.4 11.6 %collective-permute-start.10 = (bf16[1024,128]{1,0:T(8,128)(2,1)S(1)}, bf16[1024,128]{1,0:T(8,128)(2,1)S(1)}, u32[]{:S(2)}, u32[]{:S(2)}) collective-permute-start(bf16[1024,128]{1,0:T(8,128)(2,1)S(1)} %add_convert_fusion.13), channel_id=1, source_target_pairs={{0,2},{1,3},{2,0},{3,1},{4,6},{5,7},{6,4},{7,5},{8,10},{9,11},{10,... | collective-permute-start | bytes 786440 | tf_op jit(solution)/shard_map/ppermute | solution.py:38
  63.9 14.7 %collective-permute-start.13 = (bf16[2048,128]{1,0:T(8,128)(2,1)}, bf16[2048,128]{1,0:T(8,128)(2,1)S(1)}, u32[]{:S(2)}, u32[]{:S(2)}) collective-permute-start(bf16[2048,128]{1,0:T(8,128)(2,1)} %get-tuple-element.39), channel_id=1, source_target_pairs={{0,32},{16,48},{32,64},{48,80},{64,96},{80,112},{96,0},{112,16},{1... | collective-permute-start | bytes 1572872 | tf_op jit(solution)/shard_map/ppermute | solution.py:27
  64.0 15.9 %collective-permute-start.14 = (bf16[2048,128]{1,0:T(8,128)(2,1)}, bf16[2048,128]{1,0:T(8,128)(2,1)S(1)}, u32[]{:S(2)}, u32[]{:S(2)}) collective-permute-start(bf16[2048,128]{1,0:T(8,128)(2,1)} %get-tuple-element.40), channel_id=1, source_target_pairs={{0,96},{16,112},{32,0},{48,16},{64,32},{80,48},{96,64},{112,80},{1... | collective-permute-start | bytes 1572872 | tf_op jit(solution)/shard_map/ppermute | solution.py:27
  66.0 11.1 %collective-permute-start.15 = (bf16[1024,128]{1,0:T(8,128)(2,1)}, bf16[1024,128]{1,0:T(8,128)(2,1)S(1)}, u32[]{:S(2)}, u32[]{:S(2)}) collective-permute-start(bf16[1024,128]{1,0:T(8,128)(2,1)} %get-tuple-element.42), channel_id=1, source_target_pairs={{0,16},{16,0},{32,48},{48,32},{64,80},{80,64},{96,112},{112,96},{1... | collective-permute-start | bytes 786440 | tf_op jit(solution)/shard_map/ppermute | solution.py:27
  71.2 14.5 %collective-permute-start.11 = (bf16[1024,128]{1,0:T(8,128)(2,1)S(1)}, bf16[1024,128]{1,0:T(8,128)(2,1)S(1)}, u32[]{:S(2)}, u32[]{:S(2)}) collective-permute-start(bf16[1024,128]{1,0:T(8,128)(2,1)S(1)} %get-tuple-element.61), channel_id=1, source_target_pairs={{0,8},{1,9},{2,10},{3,11},{4,12},{5,13},{6,14},{7,15},{8,0},{9,1},... | collective-permute-start | bytes 786440 | tf_op jit(solution)/shard_map/ppermute | solution.py:38
  71.2 14.4 %collective-permute-start.12 = (bf16[1024,128]{1,0:T(8,128)(2,1)S(1)}, bf16[1024,128]{1,0:T(8,128)(2,1)S(1)}, u32[]{:S(2)}, u32[]{:S(2)}) collective-permute-start(bf16[1024,128]{1,0:T(8,128)(2,1)S(1)} %get-tuple-element.62), channel_id=1, source_target_pairs={{0,2},{1,3},{2,0},{3,1},{4,6},{5,7},{6,4},{7,5},{8,10},{9,11},{10,... | collective-permute-start | bytes 786440 | tf_op jit(solution)/shard_map/ppermute | solution.py:38
  80.0 10.1 %collective-permute-start.17 = (bf16[1024,128]{1,0:T(8,128)(2,1)S(1)}, bf16[1024,128]{1,0:T(8,128)(2,1)S(1)}, u32[]{:S(2)}, u32[]{:S(2)}) collective-permute-start(bf16[1024,128]{1,0:T(8,128)(2,1)S(1)} %add_convert_fusion.9), channel_id=1, source_target_pairs={{0,16},{16,0},{32,48},{48,32},{64,80},{80,64},{96,112},{112,96},{1... | collective-permute-start | bytes 786440 | tf_op jit(solution)/shard_map/ppermute | solution.py:27
  92.2 10.2 %collective-permute-start.21 = (bf16[1024,128]{1,0:T(8,128)(2,1)}, bf16[1024,128]{1,0:T(8,128)(2,1)S(1)}, u32[]{:S(2)}, u32[]{:S(2)}) collective-permute-start(bf16[1024,128]{1,0:T(8,128)(2,1)} %fusion.2.rest_0_), channel_id=1, source_target_pairs={{0,64},{16,80},{32,96},{48,112},{64,0},{80,16},{96,32},{112,48},{1... | collective-permute-start | bytes 786440 | tf_op jit(solution)/shard_map/ppermute | solution.py:27
  93.1 13.1 %collective-permute-start.18 = (bf16[1024,128]{1,0:T(8,128)(2,1)}, bf16[1024,128]{1,0:T(8,128)(2,1)S(1)}, u32[]{:S(2)}, u32[]{:S(2)}) collective-permute-start(bf16[1024,128]{1,0:T(8,128)(2,1)} %fusion.2.rest_0_), channel_id=1, source_target_pairs={{0,16},{16,0},{32,48},{48,32},{64,80},{80,64},{96,112},{112,96},{1... | collective-permute-start | bytes 786440 | tf_op jit(solution)/shard_map/ppermute | solution.py:27
  95.9 13.6 %collective-permute-start.23 = (bf16[1024,128]{1,0:T(8,128)(2,1)}, bf16[1024,128]{1,0:T(8,128)(2,1)S(1)}, u32[]{:S(2)}, u32[]{:S(2)}) collective-permute-start(bf16[1024,128]{1,0:T(8,128)(2,1)} %fusion.2.rest_0_), channel_id=1, source_target_pairs={{0,96},{16,112},{32,0},{48,16},{64,32},{80,48},{96,64},{112,80},{1... | collective-permute-start | bytes 786440 | tf_op jit(solution)/shard_map/ppermute | solution.py:27
  96.3 13.2 %collective-permute-start.19 = (bf16[1024,128]{1,0:T(8,128)(2,1)}, bf16[1024,128]{1,0:T(8,128)(2,1)S(1)}, u32[]{:S(2)}, u32[]{:S(2)}) collective-permute-start(bf16[1024,128]{1,0:T(8,128)(2,1)} %fusion.2.rest_0_), channel_id=1, source_target_pairs={{0,32},{16,48},{32,64},{48,80},{64,96},{80,112},{96,0},{112,16},{1... | collective-permute-start | bytes 786440 | tf_op jit(solution)/shard_map/ppermute | solution.py:27
  102.4 12.9 %collective-permute-start.22 = (bf16[1024,128]{1,0:T(8,128)(2,1)S(1)}, bf16[1024,128]{1,0:T(8,128)(2,1)S(1)}, u32[]{:S(2)}, u32[]{:S(2)}) collective-permute-start(bf16[1024,128]{1,0:T(8,128)(2,1)S(1)} %collective-permute-done.21.rest_4_), channel_id=1, source_target_pairs={{0,16},{16,0},{32,48},{48,32},{64,80},{80,64},{96,112},{112,96},{1... | collective-permute-start | bytes 786440 | tf_op jit(solution)/shard_map/ppermute | solution.py:27
  129.7 30.6 %collective-permute-start.26 = (bf16[2048,128]{1,0:T(8,128)(2,1)}, bf16[2048,128]{1,0:T(8,128)(2,1)}, u32[]{:S(2)}, u32[]{:S(2)}) collective-permute-start(bf16[2048,128]{1,0:T(8,128)(2,1)} %get-tuple-element.59), channel_id=1, source_target_pairs={{0,4},{1,5},{2,6},{3,7},{4,8},{5,9},{6,10},{7,11},{8,12},{9,13},{1... | collective-permute-start | bytes 1572872 | tf_op jit(solution)/shard_map/ppermute | solution.py:38
  131.4 28.9 %collective-permute-start.27 = (bf16[2048,128]{1,0:T(8,128)(2,1)}, bf16[2048,128]{1,0:T(8,128)(2,1)}, u32[]{:S(2)}, u32[]{:S(2)}) collective-permute-start(bf16[2048,128]{1,0:T(8,128)(2,1)} %get-tuple-element.60), channel_id=1, source_target_pairs={{0,12},{1,13},{2,14},{3,15},{4,0},{5,1},{6,2},{7,3},{8,4},{9,5},{1... | collective-permute-start | bytes 1572872 | tf_op jit(solution)/shard_map/ppermute | solution.py:38
  133.7 21.0 %collective-permute-start.28 = (bf16[1024,128]{1,0:T(8,128)(2,1)}, bf16[1024,128]{1,0:T(8,128)(2,1)S(1)}, u32[]{:S(2)}, u32[]{:S(2)}) collective-permute-start(bf16[1024,128]{1,0:T(8,128)(2,1)} %add_convert_fusion.8), channel_id=1, source_target_pairs={{0,2},{1,3},{2,0},{3,1},{4,6},{5,7},{6,4},{7,5},{8,10},{9,11},{10,... | collective-permute-start | bytes 786440 | tf_op jit(solution)/shard_map/ppermute | solution.py:38
  151.0 18.6 %collective-permute-start.31 = (bf16[2048,128]{1,0:T(8,128)(2,1)}, bf16[2048,128]{1,0:T(8,128)(2,1)S(1)}, u32[]{:S(2)}, u32[]{:S(2)}) collective-permute-start(bf16[2048,128]{1,0:T(8,128)(2,1)} %get-tuple-element.52), channel_id=1, source_target_pairs={{0,32},{16,48},{32,64},{48,80},{64,96},{80,112},{96,0},{112,16},{1... | collective-permute-start | bytes 1572872 | tf_op jit(solution)/shard_map/ppermute | solution.py:27
  152.1 17.4 %collective-permute-start.32 = (bf16[2048,128]{1,0:T(8,128)(2,1)}, bf16[2048,128]{1,0:T(8,128)(2,1)S(1)}, u32[]{:S(2)}, u32[]{:S(2)}) collective-permute-start(bf16[2048,128]{1,0:T(8,128)(2,1)} %get-tuple-element.53), channel_id=1, source_target_pairs={{0,96},{16,112},{32,0},{48,16},{64,32},{80,48},{96,64},{112,80},{1... | collective-permute-start | bytes 1572872 | tf_op jit(solution)/shard_map/ppermute | solution.py:27
  154.8 12.9 %collective-permute-start.33 = (bf16[1024,128]{1,0:T(8,128)(2,1)}, bf16[1024,128]{1,0:T(8,128)(2,1)S(1)}, u32[]{:S(2)}, u32[]{:S(2)}) collective-permute-start(bf16[1024,128]{1,0:T(8,128)(2,1)} %get-tuple-element.55), channel_id=1, source_target_pairs={{0,16},{16,0},{32,48},{48,32},{64,80},{80,64},{96,112},{112,96},{1... | collective-permute-start | bytes 786440 | tf_op jit(solution)/shard_map/ppermute | solution.py:27
  161.6 14.2 %collective-permute-start.29 = (bf16[1024,128]{1,0:T(8,128)(2,1)S(1)}, bf16[1024,128]{1,0:T(8,128)(2,1)S(1)}, u32[]{:S(2)}, u32[]{:S(2)}) collective-permute-start(bf16[1024,128]{1,0:T(8,128)(2,1)S(1)} %get-tuple-element.57), channel_id=1, source_target_pairs={{0,8},{1,9},{2,10},{3,11},{4,12},{5,13},{6,14},{7,15},{8,0},{9,1},... | collective-permute-start | bytes 786440 | tf_op jit(solution)/shard_map/ppermute | solution.py:38
  161.7 14.2 %collective-permute-start.30 = (bf16[1024,128]{1,0:T(8,128)(2,1)S(1)}, bf16[1024,128]{1,0:T(8,128)(2,1)S(1)}, u32[]{:S(2)}, u32[]{:S(2)}) collective-permute-start(bf16[1024,128]{1,0:T(8,128)(2,1)S(1)} %get-tuple-element.58), channel_id=1, source_target_pairs={{0,2},{1,3},{2,0},{3,1},{4,6},{5,7},{6,4},{7,5},{8,10},{9,11},{10,... | collective-permute-start | bytes 786440 | tf_op jit(solution)/shard_map/ppermute | solution.py:38
  169.7 10.6 %collective-permute-start.35 = (bf16[1024,128]{1,0:T(8,128)(2,1)S(1)}, bf16[1024,128]{1,0:T(8,128)(2,1)S(1)}, u32[]{:S(2)}, u32[]{:S(2)}) collective-permute-start(bf16[1024,128]{1,0:T(8,128)(2,1)S(1)} %add_convert_fusion.4), channel_id=1, source_target_pairs={{0,16},{16,0},{32,48},{48,32},{64,80},{80,64},{96,112},{112,96},{1... | collective-permute-start | bytes 786440 | tf_op jit(solution)/shard_map/ppermute | solution.py:27
  (17 other events, 201.0 us)
Sparse Core Ops, SparseCore 0:
  9.1 44.0 all-gather.2
  92.3 44.2 all-gather.4
